TPU v7x, 128 devices: a whole 4x4x4 slice. The times are simulated.
128 devices in a mesh: slab: 8 (over x_lo, y), rel: 16 (over z, x_hi, core).
Axes of the slice: x: 4 (x_hi: 2, x_lo: 2; x = x_hi * 2 + x_lo), y: 4, z: 4, core: 2. Of those that a mesh axis runs over, the one named last changes fastest.
Arguments:
- concentration: float32 [64, 4, 512, 1024], P('rel', None, 'slab'), may hold values from 0 to 2
- wind_store: bfloat16 [32, 4, 4, 512, 1024], P('rel', None, None, 'slab'), may hold values from -0.45 to 0.45, as said below
- sources: int32 [64], P('rel'), may hold values from 0 to 2097151
- emission: float32 [64], P('rel'), may hold values from 1 to 4
- snapshot_ids: int32 [2], replicated, may hold values from 0 to 31
Outputs:
- advanced: float32 [64, 4, 512, 1024], P('rel', None, 'slab')
Inputs may be any that keep to these rules, and one draw needn't show every extreme that they name: `wind_store`: channels 0 to 2 are Courant numbers of magnitude at most 0.45, channel 3 a diffusion number between 0.01 and 0.12.
All inputs are finite; a program needn't handle non-finite values.
Results may differ from a plain program's by a relative error of at most 0.0003.
Values may be sent and summed in bfloat16 or wider, within the bound.
No kernel may reach another device: no remote copies, remote signals or barrier semaphores. Data moves between devices by JAX's collectives and lax.ppermute only.
A program may use at most 192 MiB of HBM per device.

v0:
```python
import jax
import jax.numpy as jnp
from jax import lax
from jax.sharding import PartitionSpec as P


def from_root(value, axis, source):
    kept = jnp.where(lax.axis_index(axis) == source, value, 0).astype(value.dtype)
    return lax.psum(kept, axis)


def padded_2(array, sides, width):
    for axis, dim in sides:
        count, length = (lax.axis_size(axis), array.shape[dim])
        up = [(i, (i + 1) % count) for i in range(count - 1)]
        down = [(j, i) for i, j in up]
        last = lax.slice_in_dim(array, length - width, length, axis=dim)
        first = lax.slice_in_dim(array, 0, width, axis=dim)
        before = lax.ppermute(last, axis, up)
        after = lax.ppermute(first, axis, down)
        array = jnp.concatenate([before, array, after], axis=dim)
    return array


def central(first, second, fourth, fifth):
    return (first - 8.0 * second + 8.0 * fourth - fifth) / 12.0


def quartic(first, second, middle, fourth, fifth):
    return (first - 4.0 * second + 6.0 * middle - 4.0 * fourth + fifth) / 12.0


def advance(field, padded, diffus_pad, courant):
    west_two = padded[..., 0:-4, :]
    west_one = padded[..., 1:-3, :]
    east_one = padded[..., 3:-1, :]
    east_two = padded[..., 4:, :]
    south_two = jnp.roll(field, 2, -1)
    south_one = jnp.roll(field, 1, -1)
    north_one = jnp.roll(field, -1, -1)
    north_two = jnp.roll(field, -2, -1)
    widths = [(0, 0)] * (field.ndim - 3) + [(2, 2), (0, 0), (0, 0)]
    levels_pad = jnp.pad(field, widths, mode="edge")
    below_two = levels_pad[..., 0:-4, :, :]
    below_one = levels_pad[..., 1:-3, :, :]
    above_one = levels_pad[..., 3:-1, :, :]
    above_two = levels_pad[..., 4:, :, :]
    advected = courant[0] * central(west_two, west_one, east_one, east_two)
    advected = advected + jnp.abs(courant[0]) * quartic(
        west_two, west_one, field, east_one, east_two
    )
    advected = advected + courant[1] * central(south_two, south_one, north_one, north_two)
    advected = advected + jnp.abs(courant[1]) * quartic(
        south_two, south_one, field, north_one, north_two
    )
    advected = advected + courant[2] * central(below_two, below_one, above_one, above_two)
    advected = advected + jnp.abs(courant[2]) * quartic(
        below_two, below_one, field, above_one, above_two
    )
    diffus = diffus_pad[:, 1:-1, :]
    face_east = 0.5 * (diffus + diffus_pad[:, 2:, :])
    face_west = 0.5 * (diffus + diffus_pad[:, :-2, :])
    face_north = 0.5 * (diffus + jnp.roll(diffus, -1, -1))
    face_south = 0.5 * (diffus + jnp.roll(diffus, 1, -1))
    diffus_levels = jnp.pad(diffus, ((1, 1), (0, 0), (0, 0)), mode="edge")
    face_above = 0.5 * (diffus + diffus_levels[2:])
    face_below = 0.5 * (diffus + diffus_levels[:-2])
    spread = face_east * (east_one - field) - face_west * (field - west_one)
    spread = spread + face_north * (north_one - field) - face_south * (field - south_one)
    spread = spread + face_above * (above_one - field) - face_below * (field - below_one)
    return field - advected + spread


def body(concentration, wind_store, sources, emission, snapshot_ids):
    releases_here = concentration.shape[0]
    slab_cells = concentration.shape[2]
    width_y = concentration.shape[3]
    per_device = wind_store.shape[0]
    steps_count = snapshot_ids.shape[0]
    full_x = slab_cells * lax.axis_size("slab")
    offset = lax.axis_index("slab") * slab_cells
    source_level = sources // (full_x * width_y)
    source_x = sources // width_y % full_x
    source_y = sources % width_y
    local_x = source_x - offset
    owned = jnp.logical_and(local_x >= 0, local_x < slab_cells)
    local_x = jnp.clip(local_x, 0, slab_cells - 1)
    amounts = jnp.where(owned, emission, jnp.zeros_like(emission))
    release_ids = jnp.arange(releases_here, dtype=jnp.int32)
    field = concentration
    for number in range(steps_count):
        chosen = snapshot_ids[number]
        local_tile = lax.dynamic_index_in_dim(wind_store, chosen % per_device, 0, keepdims=False)
        snapshot = from_root(local_tile, "rel", chosen // per_device)
        padded = padded_2(field, (("slab", 2),), 2)
        diffus_pad = padded_2(snapshot[3], (("slab", 1),), 1)
        padded, diffus_pad = (padded, diffus_pad.astype(jnp.float32))
        courant = snapshot[0:3].astype(jnp.float32)
        field = advance(field, padded, diffus_pad, courant)
        field = field.at[release_ids, source_level, local_x, source_y].add(amounts)
    return field


def solution(mesh):
    placed = (
        P("rel", None, "slab", None),
        P("rel", None, None, "slab", None),
        P("rel"),
        P("rel"),
        P(),
    )
    return jax.shard_map(
        body, mesh=mesh, in_specs=placed, out_specs=P("rel", None, "slab", None), check_vma=False
    )
```

profile of v0, /device:TPU:25, one launch (start us, length us, event | category | flops | bytes accessed | tf_op | source)
XLA Modules:
  0.0 309.4 jit_solution(56626120776109618)
XLA Ops:
  13.0 4.5 %select_bitcast_fusion = (bf16[4,4,64,1024]{3,2,1,0:T(8,128)(2,1)}, bf16[4,4,64,1024]{3,2,1,0:T(8,128)(2,1)}) fusion(bf16[2,4,4,64,1024]{4,3,2,1,0:T(8,128)(2,1)} %param.6, s32[]{:T(128)S(6)} %select_n.98, pred[]{:T(512)S(6)} %eq.13, s32[]{:T(128)S(6)} %select_n.84, pred[]{:T(512)S(6)} %eq.12), kind=kLoop, calls=%fused_computation.118 | loop fusion | flops 2097152 | bytes 8388618 | tf_op jit(solution)/shard_map/jit(_where)/select_n | solution.py:8
  18.8 2.8 collective-permute-start
  21.6 2.5 collective-permute-start.1
  24.2 2.5 fusion.122
  26.7 2.4 fusion.120
  30.6 4.8 %fusion.123 = (f32[4,4,64,1022]{3,2,1,0:T(8,128)}, f32[4,4,64,1022]{3,2,1,0:T(8,128)}) fusion(f32[4,4,64,1024]{3,2,1,0:T(8,128)S(1)} %copy-done.1), kind=kLoop, calls=%fused_computation.212 | loop fusion | bytes 16744448 | tf_op jit(solution)/shard_map/jit(_roll_static)/slice | solution.py:38
  35.4 4.8 %fusion.121 = (f32[4,4,64,1023]{3,2,1,0:T(8,128)}, f32[4,4,64,1023]{3,2,1,0:T(8,128)}) fusion(f32[4,4,64,1024]{3,2,1,0:T(8,128)S(1)} %copy-done.1), kind=kLoop, calls=%fused_computation.210 | loop fusion | bytes 16760832 | tf_op jit(solution)/shard_map/jit(_roll_static)/slice | solution.py:39
  40.1 2.3 constant_dynamic-update-slice_fusion.1
  43.1 132.3 %all-reduce.3.cloned.1.call-done = (bf16[4,4,64,1024]{3,2,1,0:T(8,128)(2,1)}, bf16[4,4,64,1024]{3,2,1,0:T(8,128)(2,1)}) async-done(((bf16[4,4,64,1024]{3,2,1,0:T(8,128)(2,1)}, bf16[4,4,64,1024]{3,2,1,0:T(8,128)(2,1)}), (bf16[4,4,64,1024]{3,2,1,0:T(8,128)(2,1)}, bf16[4,4,64,1024]{3,2,1,0:T(8,128)(2,1)})) %all-reduce.3.cloned.1.call-update) | async-done | bytes 4194320 | tf_op jit(solution)/shard_map/psum | solution.py:9
  176.8 2.8 slice_convert_fusion
  179.6 2.5 collective-permute-start.3
  182.1 4.9 %collective-permute-start.2 = (bf16[4,1,1024]{2,1,0:T(2,128)(2,1)S(1)}, bf16[4,1,1024]{2,1,0:T(2,128)(2,1)S(1)}, u32[]{:S(2)}, u32[]{:S(2)}) collective-permute-start(bf16[4,1,1024]{2,1,0:T(2,128)(2,1)S(1)} %get-tuple-element.75), channel_id=1, source_target_pairs={{0,16},{16,32},{32,48},{48,64},{64,80},{80,96},{96,112},{1,17},{17... | collective-permute-start | bytes 24584 | tf_op jit(solution)/shard_map/ppermute | solution.py:19
  187.0 3.3 %multiply_bitcast_fusion.11 = (f32[4,64,1024]{2,1,0:T(8,128)}, f32[4,64,1024]{2,1,0:T(8,128)}, f32[4,64,1024]{2,1,0:T(8,128)}, f32[4,64,1024]{2,1,0:T(8,128)}, f...) fusion(f32[3,4,64,1024]{3,2,1,0:T(8,128)S(1)} %get-tuple-element.80), kind=kLoop, calls=%fused_computation.165 | loop fusion | flops 2359296 | bytes 9437184 | tf_op jit(solution)/shard_map/mul | solution.py:48
  190.4 1.9 collective-permute-start.7
  192.3 5.7 %collective-permute-start.6 = (bf16[4,1,1024]{2,1,0:T(2,128)(2,1)S(1)}, bf16[4,1,1024]{2,1,0:T(2,128)(2,1)S(1)}, u32[]{:S(2)}, u32[]{:S(2)}) collective-permute-start(bf16[4,1,1024]{2,1,0:T(2,128)(2,1)S(1)} %get-tuple-element.73), channel_id=1, source_target_pairs={{0,16},{16,32},{32,48},{48,64},{64,80},{80,96},{96,112},{1,17},{17... | collective-permute-start | bytes 24584 | tf_op jit(solution)/shard_map/ppermute | solution.py:19
  198.0 2.8 multiply_bitcast_fusion.5
  201.7 2.6 fusion.99
  204.3 1.6 fusion.97
  206.6 1.7 reshape.61
  208.3 30.7 %fusion.52 = f32[4,4,64,1024]{3,2,1,0:T(8,128)} fusion(f32[4,4,64,1024]{3,2,1,0:T(8,128)} %param.5, f32[4,2,64,1024]{3,2,1,0:T(8,128)S(1)} %reshape.60, f32[4,2,64,1024]{3,2,1,0:T(8,128)} %reshape.61, f32[4,4,2,1024]{3,2,1,0:T(2,128)S(1)} %collective-permute-done, f32[4,4,66,1024]{3,2,1,0:T(8,128)} %constant_dynamic-update-slice_fusion, ...), kind=kLoop, calls=%fused_computation.72 | loop fusion | flops 77594624 | bytes 50462720 | tf_op jit(solution)/shard_map/add | solution.py:71
  238.9 2.0 scatter_fusion
  240.9 1.8 slice_bitcast_fusion
  244.9 4.8 %fusion.118 = (f32[4,4,64,1022]{3,2,1,0:T(8,128)}, f32[4,4,64,1022]{3,2,1,0:T(8,128)}) fusion(f32[4,4,64,1024]{3,2,1,0:T(8,128)S(1)} %copy-done), kind=kLoop, calls=%fused_computation.207 | loop fusion | bytes 16744448 | tf_op jit(solution)/shard_map/jit(_roll_static)/slice | solution.py:38
  250.8 4.8 %fusion.116 = (f32[4,4,64,1023]{3,2,1,0:T(8,128)}, f32[4,4,64,1023]{3,2,1,0:T(8,128)}) fusion(f32[4,4,64,1024]{3,2,1,0:T(8,128)S(1)} %copy-done), kind=kLoop, calls=%fused_computation.205 | loop fusion | bytes 16760832 | tf_op jit(solution)/shard_map/jit(_roll_static)/slice | solution.py:39
  256.7 1.9 collective-permute-start.4
  258.6 3.6 %collective-permute-start.5 = (f32[4,4,2,1024]{3,2,1,0:T(2,128)S(1)}, f32[4,4,2,1024]{3,2,1,0:T(2,128)S(1)}, u32[]{:S(2)}, u32[]{:S(2)}) collective-permute-start(f32[4,4,2,1024]{3,2,1,0:T(2,128)S(1)} %get-tuple-element.17), channel_id=1, source_target_pairs={{16,0},{32,16},{48,32},{64,48},{80,64},{96,80},{112,96},{17,1},{33... | collective-permute-start | bytes 393224 | tf_op jit(solution)/shard_map/ppermute | solution.py:20
  262.2 2.7 fusion.93
  264.9 1.6 fusion.91
  266.5 2.3 constant_dynamic-update-slice_fusion.3
  269.7 1.6 reshape.63
  271.4 29.2 %fusion.11 = f32[4,4,64,1024]{3,2,1,0:T(8,128)} fusion(f32[4,4,64,1024]{3,2,1,0:T(8,128)} %scatter_fusion, f32[4,2,64,1024]{3,2,1,0:T(8,128)S(1)} %reshape.62, f32[4,2,64,1024]{3,2,1,0:T(8,128)} %reshape.63, f32[4,4,2,1024]{3,2,1,0:T(2,128)S(1)} %collective-permute-done.4, f32[4,4,66,1024]{3,2,1,0:T(8,128)} %constant_dynamic-update-slice_fusion.2, ...), kind=kLoop, calls=%fused_computation.27 | loop fusion | flops 77594624 | bytes 50462720 | tf_op jit(solution)/shard_map/add | solution.py:71
  300.6 2.0 scatter_fusion.1
  (49 shorter events, 13.0 us)
Async XLA Ops:
  6.5 168.9 %all-reduce.3.cloned.1.call-start = ((), (), s32[]{:S(2)}) async-start(), calls=%async_computation | async-start | bytes 8388608 | tf_op jit(solution)/shard_map/psum | solution.py:9
  17.5 6.6 %copy-start.6 = (f32[4]{0:T(128)S(1)}, f32[4]{0:T(128)}, u32[]{:S(2)}) copy-start(f32[4]{0:T(128)} %param.8) | copy-start | bytes 52
  17.5 6.6 %copy-start.7 = (s32[4]{0:T(128)S(1)}, s32[4]{0:T(128)}, u32[]{:S(2)}) copy-start(s32[4]{0:T(128)} %param.7) | copy-start | bytes 52
  18.8 187.0 %collective-permute-start = (f32[4,4,2,1024]{3,2,1,0:T(2,128)S(1)}, f32[4,4,2,1024]{3,2,1,0:T(2,128)S(1)}, u32[]{:S(2)}, u32[]{:S(2)}) collective-permute-start(f32[4,4,2,1024]{3,2,1,0:T(2,128)S(1)} %get-tuple-element.32), channel_id=1, source_target_pairs={{0,16},{16,32},{32,48},{48,64},{64,80},{80,96},{96,112},{1,17},{17... | collective-permute-start | bytes 393224 | tf_op jit(solution)/shard_map/ppermute | solution.py:19
  21.6 20.8 %collective-permute-start.1 = (f32[4,4,2,1024]{3,2,1,0:T(2,128)S(1)}, f32[4,4,2,1024]{3,2,1,0:T(2,128)S(1)}, u32[]{:S(2)}, u32[]{:S(2)}) collective-permute-start(f32[4,4,2,1024]{3,2,1,0:T(2,128)S(1)} %get-tuple-element.31), channel_id=1, source_target_pairs={{16,0},{32,16},{48,32},{64,48},{80,64},{96,80},{112,96},{17,1},{33... | collective-permute-start | bytes 393224 | tf_op jit(solution)/shard_map/ppermute | solution.py:20
  24.1 4.9 %copy-start.1 = (f32[4,4,64,1024]{3,2,1,0:T(8,128)S(1)}, f32[4,4,64,1024]{3,2,1,0:T(8,128)}, u32[]{:S(2)}) copy-start(f32[4,4,64,1024]{3,2,1,0:T(8,128)} %param.5) | copy-start | bytes 12582916
  176.7 13.6 %copy-start.4 = (bf16[4,64,1024]{2,1,0:T(8,128)(2,1)}, bf16[4,64,1024]{2,1,0:T(8,128)(2,1)S(1)}, u32[]{:S(2)}) copy-start(bf16[4,64,1024]{2,1,0:T(8,128)(2,1)S(1)} %get-tuple-element.81) | copy-start | bytes 1572868
  179.6 21.2 %collective-permute-start.3 = (bf16[4,1,1024]{2,1,0:T(2,128)(2,1)S(1)}, bf16[4,1,1024]{2,1,0:T(2,128)(2,1)S(1)}, u32[]{:S(2)}, u32[]{:S(2)}) collective-permute-start(bf16[4,1,1024]{2,1,0:T(2,128)(2,1)S(1)} %get-tuple-element.76), channel_id=1, source_target_pairs={{16,0},{32,16},{48,32},{64,48},{80,64},{96,80},{112,96},{17,1},{33... | collective-permute-start | bytes 24584 | tf_op jit(solution)/shard_map/ppermute | solution.py:20
  182.1 18.7 %collective-permute-start.2 = (bf16[4,1,1024]{2,1,0:T(2,128)(2,1)S(1)}, bf16[4,1,1024]{2,1,0:T(2,128)(2,1)S(1)}, u32[]{:S(2)}, u32[]{:S(2)}) collective-permute-start(bf16[4,1,1024]{2,1,0:T(2,128)(2,1)S(1)} %get-tuple-element.75), channel_id=1, source_target_pairs={{0,16},{16,32},{32,48},{48,64},{64,80},{80,96},{96,112},{1,17},{17... | collective-permute-start | bytes 24584 | tf_op jit(solution)/shard_map/ppermute | solution.py:19
  190.4 65.4 %collective-permute-start.7 = (bf16[4,1,1024]{2,1,0:T(2,128)(2,1)S(1)}, bf16[4,1,1024]{2,1,0:T(2,128)(2,1)S(1)}, u32[]{:S(2)}, u32[]{:S(2)}) collective-permute-start(bf16[4,1,1024]{2,1,0:T(2,128)(2,1)S(1)} %get-tuple-element.74), channel_id=1, source_target_pairs={{16,0},{32,16},{48,32},{64,48},{80,64},{96,80},{112,96},{17,1},{33... | collective-permute-start | bytes 24584 | tf_op jit(solution)/shard_map/ppermute | solution.py:20
  192.3 63.5 %collective-permute-start.6 = (bf16[4,1,1024]{2,1,0:T(2,128)(2,1)S(1)}, bf16[4,1,1024]{2,1,0:T(2,128)(2,1)S(1)}, u32[]{:S(2)}, u32[]{:S(2)}) collective-permute-start(bf16[4,1,1024]{2,1,0:T(2,128)(2,1)S(1)} %get-tuple-element.73), channel_id=1, source_target_pairs={{0,16},{16,32},{32,48},{48,64},{64,80},{80,96},{96,112},{1,17},{17... | collective-permute-start | bytes 24584 | tf_op jit(solution)/shard_map/ppermute | solution.py:19
  204.3 1.6 copy-start.3
  204.3 2.3 copy-start.2
  240.9 2.8 copy-start
  250.8 5.0 %copy-start.5 = (bf16[4,64,1024]{2,1,0:T(8,128)(2,1)S(1)}, bf16[4,64,1024]{2,1,0:T(8,128)(2,1)}, u32[]{:S(2)}) copy-start(bf16[4,64,1024]{2,1,0:T(8,128)(2,1)} %copy-done.4) | copy-start | bytes 1572868
  256.7 12.8 %collective-permute-start.4 = (f32[4,4,2,1024]{3,2,1,0:T(2,128)S(1)}, f32[4,4,2,1024]{3,2,1,0:T(2,128)S(1)}, u32[]{:S(2)}, u32[]{:S(2)}) collective-permute-start(f32[4,4,2,1024]{3,2,1,0:T(2,128)S(1)} %get-tuple-element.18), channel_id=1, source_target_pairs={{0,16},{16,32},{32,48},{48,64},{64,80},{80,96},{96,112},{1,17},{17... | collective-permute-start | bytes 393224 | tf_op jit(solution)/shard_map/ppermute | solution.py:19
  258.6 10.1 %collective-permute-start.5 = (f32[4,4,2,1024]{3,2,1,0:T(2,128)S(1)}, f32[4,4,2,1024]{3,2,1,0:T(2,128)S(1)}, u32[]{:S(2)}, u32[]{:S(2)}) collective-permute-start(f32[4,4,2,1024]{3,2,1,0:T(2,128)S(1)} %get-tuple-element.17), channel_id=1, source_target_pairs={{16,0},{32,16},{48,32},{64,48},{80,64},{96,80},{112,96},{17,1},{33... | collective-permute-start | bytes 393224 | tf_op jit(solution)/shard_map/ppermute | solution.py:20
Sparse Core Ops, SparseCore 0:
  17.6 157.7 all-reduce.2
where the time goes:
time: 315 us; the launch traced here: 309 us
  waiting for transfers between devices  132 us (42%)
  other arithmetic  86.1 us (27%)
  local copies, waits for them, and re-layouts  46.4 us (15%)
  starting transfers between devices  25.8 us (8%)
  between operations  18.8 us (6%)
    psum x1, waiting for transfers between devices, from_root(): return lax.psum(kept, axis)  132 us
    add x2, other arithmetic, advance(): return field - advected + spread  59.9 us
    ppermute x4, starting transfers between devices, padded_2(): before = lax.ppermute(last, axis, up)  15.3 us
    slice x4, local copies, waits for them, and re-layouts, advance(): south_two = jnp.roll(field, 2, -1)  13.3 us
    slice x4, local copies, waits for them, and re-layouts, advance(): south_one = jnp.roll(field, 1, -1)  13.2 us
    ppermute x4, starting transfers between devices, padded_2(): after = lax.ppermute(first, axis, down)  10.5 us
  transfers between devices with their start and end apart: 9, of which 1 were waited for; matrix products, arithmetic and copies ran while one was open for 29% of the time, Pallas kernels for 0%

commit v1 on v0

v1 whole, which is shorter than its diff:
```python
import functools
import math
import jax
import jax.numpy as jnp
from jax import lax
from jax.experimental import pallas as pl
from jax.experimental.pallas import tpu as pltpu
from jax.sharding import PartitionSpec as P

LANES = 128
PAD = 16


PIECES = 4
PIECE = (4, 2, 16, 1024)
LINKS = 3
PHASES = 4

SCHEDULES = (
    (
        (2, 4, 5, -1, -1, -1, -1, -1, -1, -1, -1, -1, -1, -1, -1, -1, -1, -1, -1, -1, -1, -1, -1, -1),
        (3, 7, 6, 5, 5, -1, 2, -1, 2, -1, -1, -1, -1, -1, -1, -1, -1, -1, -1, -1, 4, -1, -1, -1),
        (7, 1, 0, 6, 6, -1, 3, -1, 3, 5, -1, 5, 2, -1, 2, -1, -1, -1, 7, 4, 7, -1, 4, 5),
        (1, 0, 1, 0, 0, 0, 7, 2, 7, -1, 3, 6, 3, -1, 3, 2, -1, 5, -1, 1, -1, 4, 6, -1),
        (7, 7, 7, 4, 1, 5, 3, 6, 1, 0, 0, 0, 1, 4, 1, 3, 6, 6, 4, 0, 5, 2, 7, 6),
    ),
    (
        (-1, -1, -1, -1, -1, -1, -1, -1, -1, -1, -1, -1, -1, -1, -1, -1, -1, -1, -1, -1, -1, -1, -1, -1),
        (0, 3, 1, 5, 7, 6, -1, -1, -1, -1, -1, -1, -1, -1, -1, -1, -1, -1, -1, -1, -1, -1, -1, -1),
        (1, 2, 2, 4, 6, 4, 0, -1, 0, 5, -1, 5, -1, -1, -1, -1, -1, -1, -1, 3, 3, -1, 7, 7),
        (6, 4, 3, 2, 1, -1, 1, -1, -1, 4, 5, 4, 3, 3, 0, 5, 7, 7, 7, 2, 2, 6, 6, 6),
        (7, 0, 1, 1, 7, 5, 5, 6, 3, 2, 0, 2, 1, 1, 1, 0, 6, 6, 4, 4, 4, 2, 3, 5),
    ),
    (
        (-1, -1, -1, -1, -1, -1, -1, -1, -1, -1, -1, -1, -1, -1, -1, -1, -1, -1, -1, -1, -1, -1, -1, -1),
        (0, 3, 0, -1, -1, -1, 6, 5, 7, -1, -1, -1, -1, -1, -1, -1, -1, -1, -1, -1, -1, -1, -1, -1),
        (1, 2, 1, -1, 0, -1, 4, 7, 5, 7, 7, -1, 6, -1, 6, -1, -1, -1, -1, 3, 3, -1, -1, -1),
        (2, 5, 2, 0, 7, 1, 1, 4, 1, 5, 5, -1, 4, 3, 4, 6, 6, 7, -1, 6, 2, 3, 0, 0),
        (7, 7, 4, 2, 1, 5, 2, 6, 3, 1, 0, 0, 1, 4, 3, 5, 4, 5, 4, 0, 4, 6, 2, -1),
    ),
    (
        (-1, -1, -1, -1, -1, -1, -1, -1, -1, -1, -1, -1, -1, -1, -1, -1, -1, -1, -1, -1, -1, -1, -1, -1),
        (0, 2, 1, -1, -1, -1, -1, -1, -1, 6, 4, 5, -1, -1, -1, -1, -1, -1, -1, -1, -1, -1, -1, -1),
        (3, 3, 0, 1, 1, 4, 0, 5, 0, 4, 5, 7, -1, -1, -1, -1, -1, 6, -1, 2, 2, -1, -1, -1),
        (1, 5, 3, -1, 0, -1, 7, 7, 3, 5, 7, 6, 6, 2, 2, 4, 4, 4, -1, -1, 3, -1, 1, 1),
        (7, 7, 1, 7, 7, 5, 1, 6, 3, 3, 6, 0, 0, 4, 7, 5, 2, 5, -1, 3, 6, 2, 0, 4),
    ),
    (
        (-1, -1, -1, -1, -1, -1, -1, -1, -1, -1, -1, -1, -1, -1, -1, -1, -1, -1, -1, -1, -1, -1, -1, -1),
        (0, 2, 3, -1, -1, -1, -1, -1, -1, -1, -1, -1, 6, 7, 5, -1, -1, -1, -1, -1, -1, -1, -1, -1),
        (1, 1, 1, 3, 3, -1, 0, 7, 0, -1, -1, -1, 4, 6, 4, -1, 5, -1, -1, 2, 6, -1, -1, -1),
        (3, 3, 7, 1, 1, 1, 1, 0, 6, 0, 5, -1, 5, 2, 2, 4, 4, -1, 2, 4, 2, 6, 3, 6),
        (7, 7, 0, 7, 7, 5, 6, 6, 3, 6, 4, 5, 0, 4, 7, 0, 2, 5, 4, 3, 5, 2, 1, 2),
    ),
    (
        (-1, -1, -1, -1, -1, -1, -1, -1, -1, -1, -1, -1, -1, -1, -1, -1, -1, -1, -1, -1, -1, -1, -1, -1),
        (1, 3, 0, -1, -1, -1, -1, -1, -1, -1, -1, -1, -1, -1, -1, 7, 5, 4, -1, -1, -1, -1, -1, -1),
        (0, 2, 1, -1, 0, -1, 1, -1, -1, -1, -1, 5, 4, -1, -1, 5, 6, 6, -1, 3, -1, 7, 7, 7),
        (2, 3, 3, 1, 1, 7, 0, 5, 0, 6, 6, 6, 6, 3, 3, 4, 4, 7, 4, 2, 2, 5, 0, 0),
        (7, 5, 4, 7, 3, 5, 6, 6, 2, 1, 0, 4, 1, 1, 7, 5, 3, 5, 4, 3, 6, 2, 2, 2),
    ),
    (
        (-1, -1, -1, -1, -1, -1, -1, -1, -1, -1, -1, -1, -1, -1, -1, -1, -1, -1, -1, -1, -1, -1, -1, -1),
        (0, 1, 1, -1, -1, -1, -1, -1, -1, -1, -1, -1, -1, -1, -1, -1, -1, -1, 6, 5, 7, -1, -1, -1),
        (2, 3, 6, 1, -1, -1, 0, -1, 0, -1, -1, -1, -1, -1, 5, -1, -1, -1, 7, 4, 4, 7, 7, -1),
        (3, 7, 2, 6, 6, -1, 2, 0, 2, 1, -1, 1, 0, 4, 0, 5, 5, 7, -1, 1, 3, 4, 4, -1),
        (6, 3, 3, 7, 2, 4, 3, -1, 3, 6, 0, 5, 2, 7, 2, 1, 4, -1, 5, 6, 0, 5, 3, 4),
    ),
    (
        (-1, -1, -1, -1, -1, -1, -1, -1, -1, -1, -1, -1, -1, -1, -1, -1, -1, -1, -1, -1, -1, -1, -1, -1),
        (3, 1, 2, -1, -1, -1, -1, -1, -1, -1, -1, -1, -1, -1, -1, -1, -1, -1, -1, -1, -1, 5, 6, 7),
        (0, 3, 0, 2, 2, 5, 3, -1, 3, -1, -1, -1, -1, -1, -1, -1, 6, 6, 7, 1, -1, 4, 4, 4),
        (2, 5, 1, 5, 0, 0, -1, 3, 0, 2, 6, 6, 1, 1, 1, -1, -1, 4, 4, 7, 3, 7, 5, 2),
        (7, 0, 3, 7, 7, 5, 0, 6, 1, 3, 0, 5, -1, 4, 7, 1, 4, 5, 4, 2, 5, 2, 0, 6),
    ),
)


def piece_of(tile, piece, half):
    at = pl.multiple_of(half * 32 + 16 * (piece // 2), 16)
    return tile.at[:, pl.ds(2 * (piece % 2), 2), pl.ds(at, 16), :]


def plan(ids_ref, table_ref):
    chip = lax.axis_index("rel") >> 1
    first = ids_ref[0] >> 2
    second = ids_ref[1] >> 2

    def place(of):
        return 2 * (((of >> 1) - (first >> 1)) & 3) + ((of ^ first) & 1)

    here = place(chip)
    row = place(second) * 5
    z, h = here >> 1, here & 1
    sources = (2 * ((z - 1) & 3) + h, 2 * ((z + 1) & 3) + h, 2 * z + 1 - h)

    def sent(phase, link):
        return table_ref[(row + phase) * 24 + here * LINKS + link]

    def got(phase, link):
        return table_ref[(row + phase) * 24 + sources[link] * LINKS + link]

    return sent, got


def run_copies(copies, stages=(True, False)):
    for begin in stages:
        for condition, source, target, sem in copies:
            def act(source=source, target=target, sem=sem):
                copy = pltpu.make_async_copy(source, target, sem)
                if begin:
                    copy.start()
                else:
                    copy.wait()
            if condition is None:
                act()
            else:
                pl.when(condition)(act)


def run_staged(loads, stores):
    run_copies(loads)
    run_copies(stores)


def share_kernel(ids_ref, store_ref, out_ref, stage, sems):
    core = lax.axis_index("rel") & 1
    slots = range(2 * PIECES)
    run_staged(
        [
            (None, piece_of(store_ref.at[ids_ref[slot // PIECES] & 1], slot % PIECES, 1 - core), stage.at[slot], sems.at[slot])
            for slot in slots
        ],
        [(None, stage.at[slot], out_ref.at[slot], sems.at[slot]) for slot in slots],
    )


def first_kernel(phase, brought, keeps, ids_ref, table_ref, store_ref, shared_ref, *rest):
    arrived, outs, held_ref = rest[:brought], rest[brought : brought + LINKS], rest[brought + LINKS]
    stage, sems = rest[-2:]
    me = lax.axis_index("rel")
    core = me & 1
    sent, got = plan(ids_ref, table_ref)
    loads, stores = [], []
    for slot in range(2 * PIECES):
        root = ids_ref[slot // PIECES] >> 1
        stored = piece_of(store_ref.at[ids_ref[slot // PIECES] & 1], slot % PIECES, core)
        loads.append((root == me, stored, stage.at[slot], sems.at[slot]))
        loads.append((root == (me ^ 1), shared_ref.at[slot], stage.at[slot], sems.at[slot]))
        held = (root >> 1) == (me >> 1)
        for link in range(LINKS):
            chosen = jnp.logical_and(held, sent(phase, link) == slot)
            stores.append((chosen, stage.at[slot], outs[link], sems.at[link]))
        if keeps:
            stores.append((held, stage.at[slot], held_ref.at[slot], sems.at[2 * LINKS + slot]))
    for way in range(brought):
        slot = got(0, way)
        at = 2 * PIECES + way
        loads.append((None, arrived[way], stage.at[at], sems.at[at]))
        for link in range(LINKS):
            chosen = jnp.logical_and(slot >= 0, sent(phase, link) == slot)
            stores.append((chosen, stage.at[at], outs[link], sems.at[link]))
        stores.append((slot >= 0, stage.at[at], held_ref.at[jnp.maximum(slot, 0)], sems.at[LINKS + way]))
    run_staged(loads, stores)


def forward_kernel(phase, ids_ref, table_ref, *rest):
    arrived, held_ref, outs, stage, sems = rest[:LINKS], rest[LINKS], rest[LINKS + 1 : -2], rest[-2], rest[-1]
    sent, got = plan(ids_ref, table_ref)
    loads, stores = [], []
    for link in range(LINKS):
        slot = sent(phase + 1, link)
        loads.extend(
            (condition, source, stage.at[link], sems.at[link])
            for condition, source in wherever(slot, phase, got, arrived, held_ref)
        )
        stores.append((slot >= 0, stage.at[link], outs[link], sems.at[link]))
    run_staged(loads, stores)


def keep_kernel(phase, ids_ref, table_ref, *rest):
    arrived, held_ref, stage, sems = rest[:LINKS], *rest[LINKS + 1 :]
    _, got = plan(ids_ref, table_ref)
    ways = range(LINKS)
    run_staged(
        [(got(phase, way) >= 0, arrived[way], stage.at[way], sems.at[way]) for way in ways],
        [(got(phase, way) >= 0, stage.at[way], held_ref.at[jnp.maximum(got(phase, way), 0)], sems.at[way]) for way in ways],
    )


def wherever(slot, phase, got, arrived, held_ref, inner=()):
    older = slot >= 0
    places = []
    for way in range(LINKS):
        places.append((jnp.logical_and(slot >= 0, got(phase, way) == slot), arrived[way].at[inner] if inner else arrived[way]))
        older = jnp.logical_and(older, got(phase, way) != slot)
    return [*places, (older, held_ref.at[(jnp.maximum(slot, 0), *inner)])]


def edge_kernel(ids_ref, table_ref, *rest):
    arrived, held_ref, out_ref, last_ref, stage, stage_kd, rows, last, sems = rest[:LINKS], *rest[LINKS:]
    core = lax.axis_index("rel") & 1
    _, got = plan(ids_ref, table_ref)
    copies = []
    for pair in range(2):
        slot = 2 * core + pair
        for condition, source in wherever(slot, PHASES, got, arrived, held_ref):
            copies.append((condition, source, stage.at[pair], sems.at[pair]))
        for condition, source in wherever(PIECES + slot, PHASES, got, arrived, held_ref, (3,)):
            copies.append((condition, source, stage_kd.at[pair], sems.at[2 + pair]))
    for way in range(LINKS):
        copies.append((None, arrived[way], last.at[way], sems.at[4 + way]))
    run_copies(copies)
    out_copies = [(None, last, last_ref, sems.at[4])]
    run_copies(out_copies, (True,))
    rows[:, 10:, :] = jnp.zeros_like(rows[:, 10:, :])
    for level in range(4):
        def ends(block, count):
            block = block.astype(jnp.float32)
            return jnp.where(core == 0, block[:count], block[16 - count :])

        for channel in range(3):
            rows[level, 2 * channel : 2 * channel + 2, :] = ends(stage[level // 2, channel, level % 2], 2)
        rows[level, 6:9, :] = ends(stage[level // 2, 3, level % 2], 3)
        rows[level, 9:10, :] = ends(stage_kd[level // 2, level % 2], 1)
    out_ref[...] = rows[...].astype(jnp.bfloat16)
    run_copies(out_copies, (False,))


def moved(kernel, scalars, inputs, outs, scratch, aliases=None, vmem_outs=0):
    smem = pl.BlockSpec(memory_space=pltpu.SMEM)
    anywhere = pl.BlockSpec(memory_space=pl.ANY)
    return pl.pallas_call(
        kernel,
        out_shape=tuple(jax.ShapeDtypeStruct(shape, jnp.bfloat16) for shape in outs),
        in_specs=[smem] * len(scalars) + [anywhere] * len(inputs),
        out_specs=(pl.BlockSpec(memory_space=pltpu.VMEM),) * vmem_outs + (anywhere,) * (len(outs) - vmem_outs),
        scratch_shapes=scratch,
        input_output_aliases=aliases or {},
        compiler_params=pltpu.CompilerParams(vmem_limit_bytes=12 * 2**20),
        cost_estimate=pl.CostEstimate(flops=0, bytes_accessed=2**21, transcendentals=0),
    )(*scalars, *inputs)


def exchange(sends):
    shifts = ((1, 0), (3, 0), (0, 1))
    arrived = []
    for send, (dz, dh) in zip(sends, shifts):
        pairs = []
        for z in range(4):
            for h in range(2):
                for core in range(2):
                    pairs.append((z * 4 + h * 2 + core, (z + dz) % 4 * 4 + (h ^ dh) * 2 + core))
        arrived.append(lax.ppermute(send, "rel", pairs))
    return arrived


def other_core(value):
    return lax.ppermute(value, "rel", [(i, i ^ 1) for i in range(16)])


def broadcast(wind_store, ids, field):
    table = jnp.asarray(SCHEDULES, jnp.int32).reshape(-1)
    every = (2 * PIECES,) + PIECE
    dma = pltpu.SemaphoreType.DMA
    sent = [PIECE] * LINKS

    def stage(slots):
        return pltpu.VMEM((slots,) + PIECE, jnp.bfloat16)

    (shared,) = moved(share_kernel, (ids,), [wind_store], [every], [stage(2 * PIECES), dma((2 * PIECES,))])
    shared = other_core(shared)

    def begin(phase, keeps, wind_store, shared, arrived):
        return moved(
            functools.partial(first_kernel, phase, len(arrived), keeps), (ids, table), [wind_store, shared, *arrived],
            sent + [every] * keeps, [stage(2 * PIECES + LINKS), dma((2 * LINKS + 2 * PIECES,))],
        )

    def one_chip(wind_store, shared):
        return begin(1, True, wind_store, shared, exchange(begin(0, False, wind_store, shared, [])))

    *sends, held = lax.cond(
        ids[0] >> 2 == ids[1] >> 2, one_chip, lambda store, shared: begin(1, True, store, shared, []), wind_store, shared
    )
    ends = (field[:, :, :4], field[:, :, -4:])
    for phase in range(1, PHASES + 1):
        if phase == 2:
            *ends, sends[0] = lax.optimization_barrier((*ends, sends[0]))
            west, east = halos(*ends)
        arrived = exchange(sends)
        if phase == 3:
            west, east, arrived[0] = lax.optimization_barrier((west, east, arrived[0]))
        if phase < PHASES:
            sends = moved(
                functools.partial(forward_kernel, phase), (ids, table), [*arrived, held], sent, [stage(LINKS), dma((LINKS,))]
            )
            *sends, held = lax.optimization_barrier((*sends, held))
            (held,) = moved(
                functools.partial(keep_kernel, phase), (ids, table), [*arrived, held], [every], [stage(LINKS), dma((LINKS,))],
                {2 + LINKS: 0},
            )
    other = other_core(held)
    other, arrived[0] = lax.optimization_barrier((other, arrived[0]))
    edges, last = moved(
        edge_kernel, (ids, table), [*arrived, held], [(4, 16, 1024), (LINKS,) + PIECE],
        [
            stage(2), pltpu.VMEM((2,) + PIECE[1:], jnp.bfloat16), pltpu.VMEM((4, 16, 1024), jnp.float32), stage(LINKS),
            dma((4 + LINKS,)),
        ], vmem_outs=1,
    )
    ends = []
    for flip in range(2):
        pairs = []
        for slab in range(8):
            for rel in range(16):
                to = slab - 1 + 2 * (rel & 1)
                if 0 <= to < 8:
                    pairs.append((slab * 16 + rel, to * 16 + (rel ^ flip)))
        ends.append(lax.ppermute(edges, ("slab", "rel"), pairs))
    after, west, east, edges = lax.optimization_barrier((field, west, east, edges))
    start = lay_out(after, west, east)
    return (ids, table), start, held, other, last, other_core(last), *ends


def shifted_y(here, left, right, lane):
    south_one = pltpu.roll(jnp.where(lane == LANES - 1, left, here), 1, 1)
    south_two = pltpu.roll(jnp.where(lane >= LANES - 2, left, here), 2, 1)
    north_one = pltpu.roll(jnp.where(lane == 0, right, here), LANES - 1, 1)
    north_two = pltpu.roll(jnp.where(lane <= 1, right, here), LANES - 2, 1)
    return south_two, south_one, north_one, north_two


def upwind(courant):
    sixth = courant * (1.0 / 6.0)
    far = jnp.abs(sixth)
    near = far + far
    tilt = 4.0 * sixth
    return near + tilt, near - tilt, far


def roll_one(here, left, right, lane):
    south = pltpu.roll(jnp.where(lane == LANES - 1, left, here), 1, 1)
    north = pltpu.roll(jnp.where(lane == 0, right, here), LANES - 1, 1)
    return south, north


def weights(level, levels, cx, cy, cz, kd_here, kd_west, kd_east, kd_left, kd_right, lane):
    middle = kd_here[level]
    kd_south, kd_north = roll_one(middle, kd_left, kd_right, lane)
    west, east = middle + kd_west, middle + kd_east
    south, north = middle + kd_south, middle + kd_north
    below = middle + kd_here[max(level - 1, 0)]
    above = middle + kd_here[min(level + 1, levels - 1)]
    w1, e1, far_x = upwind(cx)
    s1, n1, far_y = upwind(cy)
    b1, a1, far_z = upwind(cz)
    loss = 3.0 * (far_x + far_y + far_z) + ((west + east) + (south + north) + (below + above))
    positive = jnp.maximum(cz * (1.0 / 6.0), 0.0)
    by_level = [None] * levels
    by_level[level] = 1.0 - loss
    for offset, weight in ((-2, -positive), (-1, b1 + below), (1, a1 + above), (2, positive - far_z)):
        at = min(max(level + offset, 0), levels - 1)
        by_level[at] = weight if by_level[at] is None else by_level[at] + weight
    return (cx > 0.0, far_x, w1 + west, e1 + east), (cy > 0.0, far_y, s1 + south, n1 + north), by_level


def weighted(along_x, along_y, by_level, level, x_cells, columns, left, right, lane):
    center = columns[level]
    y_cells = shifted_y(center, left, right, lane)
    total = by_level[level] * center
    for (forward, far, behind, ahead), cells in ((along_y, y_cells), (along_x, x_cells)):
        total = total + (behind * cells[1] + ahead * cells[2])
        total = total - far * jnp.where(forward, cells[0], cells[3])
    for other, weight in enumerate(by_level):
        if other != level and weight is not None:
            total = total + weight * columns[other]
    return total


def lay_out_kernel(field_hbm, west_ref, east_ref, out_ref, sems):
    chunks = out_ref.shape[2]
    rows = out_ref.shape[3] - 2 * PAD
    copies = []
    for j in range(chunks):
        span = pl.ds(j * LANES, LANES)
        copies.append((None, field_hbm.at[:, :, :, span], out_ref.at[:, :, j, pl.ds(PAD, rows), :], sems.at[j]))
        out_ref[:, :, j, PAD - 4 : PAD, :] = west_ref[:, :, :, span]
        out_ref[:, :, j, PAD + rows : PAD + rows + 4, :] = east_ref[:, :, :, span]
    run_copies(copies)


def lay_out(field, west, east):
    releases, levels, rows, width = field.shape
    chunks = width // LANES
    vmem = pl.BlockSpec(memory_space=pltpu.VMEM)
    return pl.pallas_call(
        lay_out_kernel,
        out_shape=jax.ShapeDtypeStruct((releases, levels, chunks, rows + 2 * PAD, LANES), jnp.float32),
        in_specs=[pl.BlockSpec(memory_space=pltpu.HBM), vmem, vmem],
        out_specs=vmem,
        scratch_shapes=[pltpu.SemaphoreType.DMA((chunks,))],
        compiler_params=pltpu.CompilerParams(vmem_limit_bytes=16 * 2**20),
        cost_estimate=pl.CostEstimate(flops=0, bytes_accessed=2**23, transcendentals=0),
    )(field, west, east)


def steps_kernel(ids_ref, table_ref, cells_ref, amount_ref, first, mine_ref, other_ref, mine_last, other_last, *rest):
    near_ref, far_ref, out_hbm, second, result, winds, half_kds, halo_wind, wind_sems, out_sems = rest
    releases, levels, chunks, padded_rows, _ = first.shape
    rows = padded_rows - 2 * PAD
    core = lax.rem(lax.axis_index("rel"), 2)
    slab = lax.axis_index("slab")

    def store(j):
        return pltpu.make_async_copy(
            result.at[:, :, j],
            out_hbm.at[:, :, :, pl.ds(pl.multiple_of(j * LANES, LANES), LANES)],
            out_sems.at[j],
        )

    _, got = plan(ids_ref, table_ref)
    wind_copies = []
    for slot in range(2 * PIECES):
        for number, (held_ref, last, half) in enumerate(((mine_ref, mine_last, core), (other_ref, other_last, 1 - core))):
            target = piece_of(winds.at[slot // PIECES], slot % PIECES, half)
            for condition, source in wherever(jnp.int32(slot), PHASES, got, [last.at[way] for way in range(LINKS)], held_ref):
                wind_copies.append((condition, source, target, wind_sems.at[2 * slot + number]))
    run_copies(wind_copies, (True,))

    lane = lax.broadcasted_iota(jnp.int32, (8, LANES), 1)
    sublane = lax.broadcasted_iota(jnp.int32, (8, LANES), 0)
    lane_row = lax.broadcasted_iota(jnp.int32, (1, LANES), 1)

    def span_of(j):
        return pl.ds(pl.multiple_of(j * LANES, LANES), LANES)

    def halo_rows(j, carry):
        span = span_of(j)
        near = near_ref[:, :, span].astype(jnp.float32)
        far = far_ref[:, :, span].astype(jnp.float32)
        east = jnp.where(core == 0, near, far)
        west = jnp.where(core == 0, far, near)
        for channel in range(3):
            halo_wind[channel, :, j, 0:2, :] = east[:, 2 * channel : 2 * channel + 2]
            halo_wind[channel, :, j, 6:8, :] = west[:, 2 * channel : 2 * channel + 2]
        half_kds[0, :, j, PAD + rows : PAD + rows + 3, :] = 0.5 * east[:, 6:9]
        half_kds[0, :, j, PAD - 3 : PAD, :] = 0.5 * west[:, 6:9]
        half_kds[1, :, j, PAD + rows : PAD + rows + 1, :] = 0.5 * east[:, 9:10]
        half_kds[1, :, j, PAD - 1 : PAD, :] = 0.5 * west[:, 9:10]
        return carry

    lax.fori_loop(0, chunks, halo_rows, 0)
    run_copies(wind_copies, (False,))

    def spread_kd(j, carry):
        for snap in range(2):
            for level in range(levels):
                half_kds[snap, level, j, PAD : PAD + rows, :] = 0.5 * winds[snap, 3, level, :, span_of(j)].astype(jnp.float32)
        return carry

    lax.fori_loop(0, chunks, spread_kd, 0)

    def chunk(snap, source, target, pad, j):
        before = lax.rem(j + chunks - 1, chunks)
        after = lax.rem(j + 1, chunks)
        span = span_of(j)
        half_kd = half_kds.at[snap]

        for start in range(0, rows, 16):
            for level in range(levels):
                courant = [
                    winds[snap, channel, level, pl.ds(start, 16), span].astype(jnp.float32) for channel in range(3)
                ]
                for half in range(2):
                    at = PAD + start + 8 * half
                    here = pl.ds(at, 8)
                    cx, cy, cz = (value[8 * half : 8 * half + 8] for value in courant)
                    along_x, along_y, by_level = weights(
                        level, levels, cx, cy, cz,
                        [half_kd[other, j, here, :] for other in range(levels)],
                        half_kd[level, j, pl.ds(at - 1, 8), :], half_kd[level, j, pl.ds(at + 1, 8), :],
                        half_kd[level, before, here, :], half_kd[level, after, here, :], lane,
                    )
                    for release in range(releases):
                        target[release, level, j, pl.ds(at - PAD + pad, 8), :] = weighted(
                            along_x, along_y, by_level, level,
                            [source[release, level, j, pl.ds(at + shift, 8), :] for shift in (-2, -1, 1, 2)],
                            [source[release, other, j, here, :] for other in range(levels)],
                            source[release, level, before, here, :], source[release, level, after, here, :], lane,
                        )

    def halo_chunk(j):
        before = lax.rem(j + chunks - 1, chunks)
        after = lax.rem(j + 1, chunks)
        kept = jnp.logical_or(
            jnp.logical_and(sublane < 4, slab < lax.axis_size("slab") - 1), jnp.logical_and(sublane >= 4, slab > 0)
        )

        def around(ref, index, shift=0):
            east = ref[(*index, pl.ds(PAD + rows + shift, 8), slice(None))]
            west = ref[(*index, pl.ds(PAD - 8 + shift, 8), slice(None))]
            return jnp.where(sublane < 4, east, west)

        half_kd = half_kds.at[0]
        for level in range(levels):
            along_x, along_y, by_level = weights(
                level, levels, *(halo_wind[channel, level, j] for channel in range(3)),
                [around(half_kd, (other, j)) for other in range(levels)],
                around(half_kd, (level, j), -1), around(half_kd, (level, j), 1),
                around(half_kd, (level, before)), around(half_kd, (level, after)), lane,
            )
            for release in range(releases):
                value = weighted(
                    along_x, along_y, by_level, level,
                    [around(first, (release, level, j), shift) for shift in (-2, -1, 1, 2)],
                    [around(first, (release, other, j)) for other in range(levels)],
                    around(first, (release, level, before)), around(first, (release, level, after)), lane,
                )
                value = jnp.where(kept, value, 0.0)
                second[release, level, j, PAD + rows : PAD + rows + 4, :] = value[0:4]
                second[release, level, j, PAD - 4 : PAD, :] = value[4:8]

    def emit(ref, j, pad, reach):
        for release in range(releases):
            at_row = cells_ref[1, release]
            inside = jnp.logical_and(at_row >= -reach, at_row < rows + reach)
            amount = jnp.where(inside, amount_ref[release], 0.0)
            row = pad + jnp.clip(at_row, -reach, rows + reach - 1)
            spot = (release, cells_ref[0, release], j, pl.ds(row, 1), slice(None))
            ref[spot] = ref[spot] + jnp.where(j * LANES + lane_row == cells_ref[2, release], amount, 0.0)

    def first_step(j, carry):
        chunk(0, first, second, PAD, j)
        halo_chunk(j)
        emit(second, j, PAD, 2)
        return carry

    def second_step(j, carry):
        chunk(1, second, result, 0, j)
        emit(result, j, 0, 0)
        store(j).start()
        return carry

    lax.fori_loop(0, chunks, first_step, 0)
    lax.fori_loop(0, chunks, second_step, 0)
    for j in range(chunks):
        store(j).wait()


def steps(shape, scalars, start, mine, other, mine_last, other_last, near, far, cells, amounts):
    releases, levels, rows, width = shape
    chunks = width // LANES
    vmem = pl.BlockSpec(memory_space=pltpu.VMEM)
    smem = pl.BlockSpec(memory_space=pltpu.SMEM)
    anywhere = pl.BlockSpec(memory_space=pl.ANY)
    return pl.pallas_call(
        steps_kernel,
        out_shape=jax.ShapeDtypeStruct(shape, jnp.float32),
        in_specs=[smem] * 4 + [vmem] + [anywhere] * 4 + [vmem, vmem],
        out_specs=pl.BlockSpec(memory_space=pltpu.HBM),
        scratch_shapes=[
            pltpu.VMEM(start.shape, jnp.float32),
            pltpu.VMEM((releases, levels, chunks, rows, LANES), jnp.float32),
            pltpu.VMEM((2, 4, levels, rows, width), jnp.bfloat16),
            pltpu.VMEM((2,) + start.shape[1:], jnp.float32),
            pltpu.VMEM((3, levels, chunks, 8, LANES), jnp.float32),
            pltpu.SemaphoreType.DMA((4 * PIECES,)),
            pltpu.SemaphoreType.DMA((chunks,)),
        ],
        compiler_params=pltpu.CompilerParams(vmem_limit_bytes=36 * 2**20),
        cost_estimate=pl.CostEstimate(flops=120 * math.prod(shape), bytes_accessed=12 * math.prod(shape), transcendentals=0),
    )(*scalars, cells, amounts, start, mine, other, mine_last, other_last, near, far)


def halos(first, last):
    count = lax.axis_size("slab")
    up = [(i, (i + 1) % count) for i in range(count - 1)]
    down = [(j, i) for i, j in up]
    return lax.ppermute(last, "slab", up), lax.ppermute(first, "slab", down)


def body(concentration, wind_store, sources, emission, snapshot_ids):
    rows, width = concentration.shape[2:]
    full = rows * lax.axis_size("slab")
    cells = jnp.stack([
        sources // (full * width),
        sources // width % full - lax.axis_index("slab") * rows,
        sources % width,
    ])
    return steps(concentration.shape, *broadcast(wind_store, snapshot_ids, concentration), cells, emission)


def solution(mesh):
    placed = (
        P("rel", None, "slab", None),
        P("rel", None, None, "slab", None),
        P("rel"),
        P("rel"),
        P(),
    )
    return jax.shard_map(
        body, mesh=mesh, in_specs=placed, out_specs=P("rel", None, "slab", None), check_vma=False
    )
```

time: 315 us -> 111 us (0.35); the launches traced: 309 us -> 110 us
  waiting for transfers between devices: 132 us -> 21.8 us
  other arithmetic: 86.1 us -> 0.03 us
  local copies, waits for them, and re-layouts: 46.4 us -> 4.09 us
  Pallas kernels: 0 us -> 33.5 us
  starting transfers between devices: 25.8 us -> 48.4 us
  between operations: 18.8 us -> 1.68 us
    psum x1 -> x0, waiting for transfers between devices: 132 us -> none  [from_root(): return lax.psum(kept, axis)]
    add x2 -> x0, other arithmetic: 59.9 us -> none  [advance(): return field - advected + spread]
    pallas_call x0 -> x12, Pallas kernels: none -> 33.5 us  [the longest x1 17.1 us: steps(): pl.pallas_call(steps_kernel, out_shape=jax.ShapeDtypeStruct(shape, jnp.fl...]
    slice x21 -> x2, local copies, waits for them, and re-layouts: 33.8 us -> 1.88 us  [the longest x1 1.3 us: broadcast(): ends = (field[:, :, :4], field[:, :, -4:])]
    ppermute x8 -> x22, starting transfers between devices: 25.8 us -> 48.4 us  [the longest x15 28.9 us: exchange(): arrived.append(lax.ppermute(send, 'rel', pairs))]
    ppermute x8 -> x22, waiting for transfers between devices: 0.02 us -> 21.8 us  [the longest x15 19.3 us: exchange(): arrived.append(lax.ppermute(send, 'rel', pairs))]
    mul x6 -> x0, other arithmetic: 14.6 us -> none  [the longest x2 6.16 us: advance(): advected = courant[0] * central(west_two, west_one, east_one, east_two)]
    select_n x2 -> x0, other arithmetic: 4.49 us -> none  [the longest x1 4.47 us: from_root(): jnp.where(lax.axis_index(axis) == source, value, 0).astype(value.dtype)]
  transfers between devices with their start and end apart: 9 -> 22, of which waited for: 1 -> 10; matrix products, arithmetic and copies ran while one was open for 29% -> 2% of each run, Pallas kernels for 0% -> 4%
where the time goes in v1:
time: 111 us; the launch traced here: 110 us
  starting transfers between devices  48.4 us (44%)
  Pallas kernels  33.5 us (30%)
  waiting for transfers between devices  21.8 us (20%)
  local copies, waits for them, and re-layouts  4.09 us (4%)
  between operations  1.68 us (2%)
    ppermute x15, starting transfers between devices, exchange(): arrived.append(lax.ppermute(send, 'rel', pairs))  28.9 us
    ppermute x15, waiting for transfers between devices, exchange(): arrived.append(lax.ppermute(send, 'rel', pairs))  19.3 us
    pallas_call x1, Pallas kernels, steps(): pl.pallas_call(steps_kernel, out_shape=jax.ShapeDtypeStruct(shape, jnp.fl...  17.1 us
    pallas_call x10, Pallas kernels, moved(): pl.pallas_call(kernel, out_shape=tuple((jax.ShapeDtypeStruct(shape, jnp.b...  15.6 us
    ppermute x3, starting transfers between devices, other_core(): return lax.ppermute(value, 'rel', [(i, i ^ 1) for i in range(16)])  8.21 us
    ppermute x2, starting transfers between devices, broadcast(): ends.append(lax.ppermute(edges, ('slab', 'rel'), pairs))  6.05 us
    ppermute x2, starting transfers between devices, halos(): return (lax.ppermute(last, 'slab', up), lax.ppermute(first, 'slab', down))  5.27 us
  transfers between devices with their start and end apart: 22, of which 10 were waited for; matrix products, arithmetic and copies ran while one was open for 2% of the time, Pallas kernels for 4%

profile of v1, /device:TPU:25, one launch (start us, length us, event | category | flops | bytes accessed | tf_op | source)
XLA Modules:
  0.0 109.6 jit_solution(14806793043118899590)
XLA Ops:
  0.0 2.9 %shard_map.64 = bf16[8,4,2,16,1024]{4,3,2,1,0:T(8,128)(2,1)S(1)} custom-call(s32[2]{0:T(128)} %ids_ref.17, bf16[2,4,4,64,1024]{4,3,2,1,0:T(8,128)(2,1)} %store_ref.1), custom_call_target="tpu_custom_call" | custom-call | bytes 2097152 | tf_op jit(solution)/shard_map/pallas_call | solution.py:233
  5.6 1.9 %collective-permute-done.3 = bf16[8,4,2,16,1024]{4,3,2,1,0:T(8,128)(2,1)S(1)} collective-permute-done((bf16[8,4,2,16,1024]{4,3,2,1,0:T(8,128)(2,1)S(1)}, bf16[8,4,2,16,1024]{4,3,2,1,0:T(8,128)(2,1)S(1)}, u32[]{:S(2)}, u32[]{:S(2)}) %collective-permute-start.3) | collective-permute-done | bytes 2097184 | tf_op jit(solution)/shard_map/ppermute | solution.py:259
  7.5 15.6 %conditional.1 = ((bf16[4,2,16,1024]{3,2,1,0:T(8,128)(2,1)S(1)}, bf16[4,2,16,1024]{3,2,1,0:T(8,128)(2,1)S(1)}, bf16[4,2,16,1024]{3,2,1,0:T(8,128)(2,1)S(1)}, bf16[8,4,2,16,1024]{4,3,2,1,0:T(8,128)(2,1)})) conditional(s32[]{:T(128)} %bitcast.3, (s32[2]{0:T(128)S(1)}, s32[960]{0:T(1024)S(1)}, bf16[2,4,4,64,1024]{4,3,2,1,0:T(8,128)(2,1)S(1)}, ...), branch_computations={%region_0.1_spmd, %region_1.2_spmd} | conditional | bytes 7340160 | solution.py:283
  8.6 1.7 %collective-permute-start = (bf16[4,2,16,1024]{3,2,1,0:T(8,128)(2,1)S(1)}, bf16[4,2,16,1024]{3,2,1,0:T(8,128)(2,1)S(1)}, u32[]{:S(2)}, u32[]{:S(2)}) collective-permute-start(bf16[4,2,16,1024]{3,2,1,0:T(8,128)(2,1)S(1)} %get-tuple-element.29), channel_id=1, source_target_pairs={{0,4},{1,5},{2,6},{3,7},{4,8},{5,9},{6,10},{7,11},{8,12},{9,13},{1... | collective-permute-start | bytes 786440 | tf_op jit(solution)/shard_map/cond/branch_1_fun/ppermute | solution.py:254
  10.3 2.2 %collective-permute-start.1 = (bf16[4,2,16,1024]{3,2,1,0:T(8,128)(2,1)S(1)}, bf16[4,2,16,1024]{3,2,1,0:T(8,128)(2,1)S(1)}, u32[]{:S(2)}, u32[]{:S(2)}) collective-permute-start(bf16[4,2,16,1024]{3,2,1,0:T(8,128)(2,1)S(1)} %get-tuple-element.30), channel_id=1, source_target_pairs={{0,12},{1,13},{2,14},{3,15},{4,0},{5,1},{6,2},{7,3},{8,4},{9,5},{1... | collective-permute-start | bytes 786440 | tf_op jit(solution)/shard_map/cond/branch_1_fun/ppermute | solution.py:254
  12.5 2.7 %collective-permute-start.2 = (bf16[4,2,16,1024]{3,2,1,0:T(8,128)(2,1)S(1)}, bf16[4,2,16,1024]{3,2,1,0:T(8,128)(2,1)S(1)}, u32[]{:S(2)}, u32[]{:S(2)}) collective-permute-start(bf16[4,2,16,1024]{3,2,1,0:T(8,128)(2,1)S(1)} %get-tuple-element.31), channel_id=1, source_target_pairs={{0,2},{1,3},{2,0},{3,1},{4,6},{5,7},{6,4},{7,5},{8,10},{9,11},{10,... | collective-permute-start | bytes 786440 | tf_op jit(solution)/shard_map/cond/branch_1_fun/ppermute | solution.py:254
  15.2 3.6 %collective-permute-done.rest_0_ = bf16[4,2,16,1024]{3,2,1,0:T(8,128)(2,1)S(1)} collective-permute-done((bf16[4,2,16,1024]{3,2,1,0:T(8,128)(2,1)S(1)}, bf16[4,2,16,1024]{3,2,1,0:T(8,128)(2,1)S(1)}, u32[]{:S(2)}, u32[]{:S(2)}) %collective-permute-start) | collective-permute-done | bytes 262176 | tf_op jit(solution)/shard_map/cond/branch_1_fun/ppermute | solution.py:254
  18.8 2.4 %collective-permute-done.2.rest_2_ = bf16[4,2,16,1024]{3,2,1,0:T(8,128)(2,1)S(1)} collective-permute-done((bf16[4,2,16,1024]{3,2,1,0:T(8,128)(2,1)S(1)}, bf16[4,2,16,1024]{3,2,1,0:T(8,128)(2,1)S(1)}, u32[]{:S(2)}, u32[]{:S(2)}) %collective-permute-start.2) | collective-permute-done | bytes 262176 | tf_op jit(solution)/shard_map/cond/branch_1_fun/ppermute | solution.py:254
  21.2 1.9 %branch_1_fun.3 = (bf16[4,2,16,1024]{3,2,1,0:T(8,128)(2,1)S(1)}, bf16[4,2,16,1024]{3,2,1,0:T(8,128)(2,1)S(1)}, bf16[4,2,16,1024]{3,2,1,0:T(8,128)(2,1)S(1)}, bf16[8,4,2,16,1024]{4,3,2,1,0:T(8,128)(2,1)}) custom-call(s32[2]{0:T(128)S(1)} %get-tuple-element.25.ids_ref, s32[960]{0:T(1024)S(1)} %get-tuple-element.26.table_ref, ...), custom_call_target="tpu_custom_call" | custom-call | bytes 2097152 | tf_op jit(solution)/shard_map/cond/branch_1_fun/pallas_call | solution.py:233
  23.2 2.7 %collective-permute-start.5 = (bf16[4,2,16,1024]{3,2,1,0:T(8,128)(2,1)S(1)}, bf16[4,2,16,1024]{3,2,1,0:T(8,128)(2,1)S(1)}, u32[]{:S(2)}, u32[]{:S(2)}) collective-permute-start(bf16[4,2,16,1024]{3,2,1,0:T(8,128)(2,1)S(1)} %get-tuple-element.71), channel_id=1, source_target_pairs={{0,12},{1,13},{2,14},{3,15},{4,0},{5,1},{6,2},{7,3},{8,4},{9,5},{1... | collective-permute-start | bytes 786440 | tf_op jit(solution)/shard_map/ppermute | solution.py:254
  25.8 3.3 %collective-permute-start.6 = (bf16[4,2,16,1024]{3,2,1,0:T(8,128)(2,1)S(1)}, bf16[4,2,16,1024]{3,2,1,0:T(8,128)(2,1)S(1)}, u32[]{:S(2)}, u32[]{:S(2)}) collective-permute-start(bf16[4,2,16,1024]{3,2,1,0:T(8,128)(2,1)S(1)} %get-tuple-element.72), channel_id=1, source_target_pairs={{0,2},{1,3},{2,0},{3,1},{4,6},{5,7},{6,4},{7,5},{8,10},{9,11},{10,... | collective-permute-start | bytes 786440 | tf_op jit(solution)/shard_map/ppermute | solution.py:254
  30.6 3.0 %collective-permute-done.6.rest_2_ = bf16[4,2,16,1024]{3,2,1,0:T(8,128)(2,1)S(1)} collective-permute-done((bf16[4,2,16,1024]{3,2,1,0:T(8,128)(2,1)S(1)}, bf16[4,2,16,1024]{3,2,1,0:T(8,128)(2,1)S(1)}, u32[]{:S(2)}, u32[]{:S(2)}) %collective-permute-start.6) | collective-permute-done | bytes 262176 | tf_op jit(solution)/shard_map/ppermute | solution.py:254
  34.5 2.7 %collective-permute-start.10 = (bf16[4,2,16,1024]{3,2,1,0:T(8,128)(2,1)S(1)}, bf16[4,2,16,1024]{3,2,1,0:T(8,128)(2,1)S(1)}, u32[]{:S(2)}, u32[]{:S(2)}) collective-permute-start(bf16[4,2,16,1024]{3,2,1,0:T(8,128)(2,1)S(1)} %get-tuple-element.81), channel_id=1, source_target_pairs={{0,12},{1,13},{2,14},{3,15},{4,0},{5,1},{6,2},{7,3},{8,4},{9,5},{1... | collective-permute-start | bytes 786440 | tf_op jit(solution)/shard_map/ppermute | solution.py:254
  37.2 3.7 %collective-permute-start.11 = (bf16[4,2,16,1024]{3,2,1,0:T(8,128)(2,1)S(1)}, bf16[4,2,16,1024]{3,2,1,0:T(8,128)(2,1)S(1)}, u32[]{:S(2)}, u32[]{:S(2)}) collective-permute-start(bf16[4,2,16,1024]{3,2,1,0:T(8,128)(2,1)S(1)} %get-tuple-element.82), channel_id=1, source_target_pairs={{0,2},{1,3},{2,0},{3,1},{4,6},{5,7},{6,4},{7,5},{8,10},{9,11},{10,... | collective-permute-start | bytes 786440 | tf_op jit(solution)/shard_map/ppermute | solution.py:254
  40.9 1.9 %collective-permute-start.7 = (f32[4,4,4,1024]{3,2,1,0:T(4,128)S(1)}, f32[4,4,4,1024]{3,2,1,0:T(4,128)S(1)}, u32[]{:S(2)}, u32[]{:S(2)}) collective-permute-start(f32[4,4,4,1024]{3,2,1,0:T(4,128)S(1)} %get-tuple-element.78), channel_id=1, source_target_pairs={{0,16},{16,32},{32,48},{48,64},{64,80},{80,96},{96,112},{1,17},{17... | collective-permute-start | bytes 786440 | tf_op jit(solution)/shard_map/ppermute | solution.py:580
  42.9 3.4 %collective-permute-start.8 = (f32[4,4,4,1024]{3,2,1,0:T(4,128)S(1)}, f32[4,4,4,1024]{3,2,1,0:T(4,128)S(1)}, u32[]{:S(2)}, u32[]{:S(2)}) collective-permute-start(f32[4,4,4,1024]{3,2,1,0:T(4,128)S(1)} %get-tuple-element.79), channel_id=1, source_target_pairs={{16,0},{32,16},{48,32},{64,48},{80,64},{96,80},{112,96},{17,1},{33... | collective-permute-start | bytes 786440 | tf_op jit(solution)/shard_map/ppermute | solution.py:580
  46.2 1.4 %shard_map.66.rest_3_ = bf16[8,4,2,16,1024]{4,3,2,1,0:T(8,128)(2,1)} custom-call(s32[2]{0:T(128)S(1)} %copy-done.4, s32[960]{0:T(1024)S(1)} %copy-done.3, bf16[4,2,16,1024]{3,2,1,0:T(8,128)(2,1)S(1)} %collective-permute-done.4.rest_0_, bf16[4,2,16,1024]{3,2,1,0:T(8,128)(2,1)S(1)} %collective-permute-done.5.rest_1_, ...), custom_call_target="tpu_custom_call", output_to_operand_aliasing={{}: (5, {})} | custom-call | bytes 2097152 | tf_op jit(solution)/shard_map/pallas_call | solution.py:233
  48.6 2.7 %collective-permute-start.13 = (bf16[4,2,16,1024]{3,2,1,0:T(8,128)(2,1)S(1)}, bf16[4,2,16,1024]{3,2,1,0:T(8,128)(2,1)S(1)}, u32[]{:S(2)}, u32[]{:S(2)}) collective-permute-start(bf16[4,2,16,1024]{3,2,1,0:T(8,128)(2,1)S(1)} %get-tuple-element.91), channel_id=1, source_target_pairs={{0,12},{1,13},{2,14},{3,15},{4,0},{5,1},{6,2},{7,3},{8,4},{9,5},{1... | collective-permute-start | bytes 786440 | tf_op jit(solution)/shard_map/ppermute | solution.py:254
  55.3 3.0 %collective-permute-done.14.rest_2_ = bf16[4,2,16,1024]{3,2,1,0:T(8,128)(2,1)S(1)} collective-permute-done((bf16[4,2,16,1024]{3,2,1,0:T(8,128)(2,1)S(1)}, bf16[4,2,16,1024]{3,2,1,0:T(8,128)(2,1)S(1)}, u32[]{:S(2)}, u32[]{:S(2)}) %collective-permute-start.14) | collective-permute-done | bytes 262176 | tf_op jit(solution)/shard_map/ppermute | solution.py:254
  58.3 1.8 %shard_map.69 = (bf16[4,2,16,1024]{3,2,1,0:T(8,128)(2,1)S(1)}, bf16[4,2,16,1024]{3,2,1,0:T(8,128)(2,1)S(1)}, bf16[4,2,16,1024]{3,2,1,0:T(8,128)(2,1)S(1)}) custom-call(s32[2]{0:T(128)S(1)} %copy-done.4, s32[960]{0:T(1024)S(1)} %copy-done.3, bf16[4,2,16,1024]{3,2,1,0:T(8,128)(2,1)S(1)} %collective-permute-done.12.rest_0_, ...), custom_call_target="tpu_custom_call" | custom-call | bytes 2097152 | tf_op jit(solution)/shard_map/pallas_call | solution.py:233
  60.1 1.6 %shard_map.70.rest_3_.mine_ref = bf16[8,4,2,16,1024]{4,3,2,1,0:T(8,128)(2,1)} custom-call(s32[2]{0:T(128)S(1)} %copy-done.4, s32[960]{0:T(1024)S(1)} %copy-done.3, bf16[4,2,16,1024]{3,2,1,0:T(8,128)(2,1)S(1)} %collective-permute-done.12.rest_0_, bf16[4,2,16,1024]{3,2,1,0:T(8,128)(2,1)S(1)} %collective-permute-done.13.rest_1_, ...), custom_call_target="tpu_custom_call", output_to_operand_aliasing={{}: (5, {})} | custom-call | bytes 2097152 | tf_op jit(solution)/shard_map/pallas_call | solution.py:233
  61.7 5.9 %collective-permute-start.15 = (bf16[8,4,2,16,1024]{4,3,2,1,0:T(8,128)(2,1)}, bf16[8,4,2,16,1024]{4,3,2,1,0:T(8,128)(2,1)S(1)}, u32[]{:S(2)}, u32[]{:S(2)}) collective-permute-start(bf16[8,4,2,16,1024]{4,3,2,1,0:T(8,128)(2,1)} %shard_map.70.rest_3_.mine_ref), channel_id=1, source_target_pairs={{0,1},{1,0},{2,3},{3,2},{4,5},{5,4},{6,7},{7,6},{8,9},{9,8},{10,11... | collective-permute-start | bytes 6291464 | tf_op jit(solution)/shard_map/ppermute | solution.py:259
  67.6 2.7 %collective-permute-start.17 = (bf16[4,2,16,1024]{3,2,1,0:T(8,128)(2,1)S(1)}, bf16[4,2,16,1024]{3,2,1,0:T(8,128)(2,1)S(1)}, u32[]{:S(2)}, u32[]{:S(2)}) collective-permute-start(bf16[4,2,16,1024]{3,2,1,0:T(8,128)(2,1)S(1)} %get-tuple-element.100), channel_id=1, source_target_pairs={{0,12},{1,13},{2,14},{3,15},{4,0},{5,1},{6,2},{7,3},{8,4},{9,5},{1... | collective-permute-start | bytes 786440 | tf_op jit(solution)/shard_map/ppermute | solution.py:254
  70.3 3.0 %collective-permute-start.18 = (bf16[4,2,16,1024]{3,2,1,0:T(8,128)(2,1)S(1)}, bf16[4,2,16,1024]{3,2,1,0:T(8,128)(2,1)S(1)}, u32[]{:S(2)}, u32[]{:S(2)}) collective-permute-start(bf16[4,2,16,1024]{3,2,1,0:T(8,128)(2,1)S(1)} %get-tuple-element.101), channel_id=1, source_target_pairs={{0,2},{1,3},{2,0},{3,1},{4,6},{5,7},{6,4},{7,5},{8,10},{9,11},{10,... | collective-permute-start | bytes 786440 | tf_op jit(solution)/shard_map/ppermute | solution.py:254
  73.3 3.4 %collective-permute-done.16.rest_0_ = bf16[4,2,16,1024]{3,2,1,0:T(8,128)(2,1)S(1)} collective-permute-done((bf16[4,2,16,1024]{3,2,1,0:T(8,128)(2,1)S(1)}, bf16[4,2,16,1024]{3,2,1,0:T(8,128)(2,1)S(1)}, u32[]{:S(2)}, u32[]{:S(2)}) %collective-permute-start.16) | collective-permute-done | bytes 262176 | tf_op jit(solution)/shard_map/ppermute | solution.py:254
  76.7 2.4 %collective-permute-done.18.rest_2_ = bf16[4,2,16,1024]{3,2,1,0:T(8,128)(2,1)S(1)} collective-permute-done((bf16[4,2,16,1024]{3,2,1,0:T(8,128)(2,1)S(1)}, bf16[4,2,16,1024]{3,2,1,0:T(8,128)(2,1)S(1)}, u32[]{:S(2)}, u32[]{:S(2)}) %collective-permute-start.18) | collective-permute-done | bytes 262176 | tf_op jit(solution)/shard_map/ppermute | solution.py:254
  79.1 1.9 %shard_map.71 = (bf16[4,16,1024]{2,1,0:T(8,128)(2,1)S(1)}, bf16[3,4,2,16,1024]{4,3,2,1,0:T(8,128)(2,1)S(1)}) custom-call(s32[2]{0:T(128)S(1)} %copy-done.4, s32[960]{0:T(1024)S(1)} %copy-done.3, bf16[4,2,16,1024]{3,2,1,0:T(8,128)(2,1)S(1)} %collective-permute-done.16.rest_0_, bf16[4,2,16,1024]{3,2,1,0:T(8,128)(2,1)S(1)} %collective-permute-done.17.rest_1_, ...), custom_call_target="tpu_custom_call" | custom-call | bytes 2097152 | tf_op jit(solution)/shard_map/pallas_call | solution.py:233
  81.0 1.5 %collective-permute-start.19 = (bf16[3,4,2,16,1024]{4,3,2,1,0:T(8,128)(2,1)S(1)}, bf16[3,4,2,16,1024]{4,3,2,1,0:T(8,128)(2,1)}, u32[]{:S(2)}, u32[]{:S(2)}) collective-permute-start(bf16[3,4,2,16,1024]{4,3,2,1,0:T(8,128)(2,1)S(1)} %get-tuple-element.107.mine_last), channel_id=1, source_target_pairs={{0,1},{1,0},{2,3},{3,2},{4,5},{5,4},{6,7},{7,6},{8,9},{9,8},{10,11... | collective-permute-start | bytes 2359304 | tf_op jit(solution)/shard_map/ppermute | solution.py:259
  82.5 4.0 %collective-permute-start.21 = (bf16[4,16,1024]{2,1,0:T(8,128)(2,1)S(1)}, bf16[4,16,1024]{2,1,0:T(8,128)(2,1)S(1)}, u32[]{:S(2)}, u32[]{:S(2)}) collective-permute-start(bf16[4,16,1024]{2,1,0:T(8,128)(2,1)S(1)} %get-tuple-element.102), channel_id=1, source_target_pairs={{1,16},{3,18},{5,20},{7,22},{9,24},{11,26},{13,28},{15,30},{16,1},... | collective-permute-start | bytes 393224 | tf_op jit(solution)/shard_map/ppermute | solution.py:320
  86.6 2.0 %collective-permute-start.20 = (bf16[4,16,1024]{2,1,0:T(8,128)(2,1)S(1)}, bf16[4,16,1024]{2,1,0:T(8,128)(2,1)S(1)}, u32[]{:S(2)}, u32[]{:S(2)}) collective-permute-start(bf16[4,16,1024]{2,1,0:T(8,128)(2,1)S(1)} %get-tuple-element.102), channel_id=1, source_target_pairs={{1,17},{3,19},{5,21},{7,23},{9,25},{11,27},{13,29},{15,31},{16,0},... | collective-permute-start | bytes 393224 | tf_op jit(solution)/shard_map/ppermute | solution.py:320
  88.7 2.2 %copy-done = f32[4,4,64,1024]{3,2,1,0:T(8,128)S(1)} copy-done((f32[4,4,64,1024]{3,2,1,0:T(8,128)S(1)}, f32[4,4,64,1024]{3,2,1,0:T(8,128)}, u32[]{:S(2)}) %copy-start) | copy-done | bytes 4194328
  92.3 17.1 %shard_map.73 = f32[4,4,64,1024]{3,2,1,0:T(8,128)} custom-call(s32[2]{0:T(128)S(1)} %copy-done.4, s32[960]{0:T(1024)S(1)} %copy-done.3, s32[3,4]{1,0:T(4,128)S(1)} %pad_add_fusion.cells_ref, f32[4]{0:T(128)S(1)} %copy-done.1, f32[4,4,8,96,128]{4,3,2,1,0:T(8,128)S(1)} %shard_map.72.first, bf16[8,4,2,16,1024]{4,3,2,1,0:T(8,128)(2,1)} %shard_map.70.rest_3_.mine_ref, ...), custom_call_target="tpu_custom_call" | custom-call | flops 125829120 | bytes 12582912 | tf_op jit(solution)/shard_map/pallas_call | solution.py:557
  (41 shorter events, 11.4 us)
Async XLA Ops:
  0.0 7.5 %copy-start.3 = (s32[960]{0:T(1024)S(1)}, s32[960]{0:T(1024)}, u32[]{:S(2)}) copy-start(s32[960]{0:T(1024)} %constant.69.table_ref) | copy-start | bytes 11524
  0.0 3.7 %copy-start.4 = (s32[2]{0:T(128)S(1)}, s32[2]{0:T(128)}, u32[]{:S(2)}) copy-start(s32[2]{0:T(128)} %ids_ref.17) | copy-start | bytes 28
  0.0 7.5 %copy-start.2 = (bf16[2,4,4,64,1024]{4,3,2,1,0:T(8,128)(2,1)S(1)}, bf16[2,4,4,64,1024]{4,3,2,1,0:T(8,128)(2,1)}, u32[]{:S(2)}) copy-start(bf16[2,4,4,64,1024]{4,3,2,1,0:T(8,128)(2,1)} %store_ref.1) | copy-start | bytes 12582916
  2.9 4.5 %collective-permute-start.3 = (bf16[8,4,2,16,1024]{4,3,2,1,0:T(8,128)(2,1)S(1)}, bf16[8,4,2,16,1024]{4,3,2,1,0:T(8,128)(2,1)S(1)}, u32[]{:S(2)}, u32[]{:S(2)}) collective-permute-start(bf16[8,4,2,16,1024]{4,3,2,1,0:T(8,128)(2,1)S(1)} %shard_map.64), channel_id=1, source_target_pairs={{0,1},{1,0},{2,3},{3,2},{4,5},{5,4},{6,7},{7,6},{8,9},{9,8},{10,11... | collective-permute-start | bytes 6291464 | tf_op jit(solution)/shard_map/ppermute | solution.py:259
  8.6 10.2 %collective-permute-start = (bf16[4,2,16,1024]{3,2,1,0:T(8,128)(2,1)S(1)}, bf16[4,2,16,1024]{3,2,1,0:T(8,128)(2,1)S(1)}, u32[]{:S(2)}, u32[]{:S(2)}) collective-permute-start(bf16[4,2,16,1024]{3,2,1,0:T(8,128)(2,1)S(1)} %get-tuple-element.29), channel_id=1, source_target_pairs={{0,4},{1,5},{2,6},{3,7},{4,8},{5,9},{6,10},{7,11},{8,12},{9,13},{1... | collective-permute-start | bytes 786440 | tf_op jit(solution)/shard_map/cond/branch_1_fun/ppermute | solution.py:254
  10.3 8.5 %collective-permute-start.1 = (bf16[4,2,16,1024]{3,2,1,0:T(8,128)(2,1)S(1)}, bf16[4,2,16,1024]{3,2,1,0:T(8,128)(2,1)S(1)}, u32[]{:S(2)}, u32[]{:S(2)}) collective-permute-start(bf16[4,2,16,1024]{3,2,1,0:T(8,128)(2,1)S(1)} %get-tuple-element.30), channel_id=1, source_target_pairs={{0,12},{1,13},{2,14},{3,15},{4,0},{5,1},{6,2},{7,3},{8,4},{9,5},{1... | collective-permute-start | bytes 786440 | tf_op jit(solution)/shard_map/cond/branch_1_fun/ppermute | solution.py:254
  12.5 8.7 %collective-permute-start.2 = (bf16[4,2,16,1024]{3,2,1,0:T(8,128)(2,1)S(1)}, bf16[4,2,16,1024]{3,2,1,0:T(8,128)(2,1)S(1)}, u32[]{:S(2)}, u32[]{:S(2)}) collective-permute-start(bf16[4,2,16,1024]{3,2,1,0:T(8,128)(2,1)S(1)} %get-tuple-element.31), channel_id=1, source_target_pairs={{0,2},{1,3},{2,0},{3,1},{4,6},{5,7},{6,4},{7,5},{8,10},{9,11},{10,... | collective-permute-start | bytes 786440 | tf_op jit(solution)/shard_map/cond/branch_1_fun/ppermute | solution.py:254
  23.1 7.6 %collective-permute-start.4 = (bf16[4,2,16,1024]{3,2,1,0:T(8,128)(2,1)S(1)}, bf16[4,2,16,1024]{3,2,1,0:T(8,128)(2,1)S(1)}, u32[]{:S(2)}, u32[]{:S(2)}) collective-permute-start(bf16[4,2,16,1024]{3,2,1,0:T(8,128)(2,1)S(1)} %get-tuple-element.70), channel_id=1, source_target_pairs={{0,4},{1,5},{2,6},{3,7},{4,8},{5,9},{6,10},{7,11},{8,12},{9,13},{1... | collective-permute-start | bytes 786440 | tf_op jit(solution)/shard_map/ppermute | solution.py:254
  23.2 7.5 %collective-permute-start.5 = (bf16[4,2,16,1024]{3,2,1,0:T(8,128)(2,1)S(1)}, bf16[4,2,16,1024]{3,2,1,0:T(8,128)(2,1)S(1)}, u32[]{:S(2)}, u32[]{:S(2)}) collective-permute-start(bf16[4,2,16,1024]{3,2,1,0:T(8,128)(2,1)S(1)} %get-tuple-element.71), channel_id=1, source_target_pairs={{0,12},{1,13},{2,14},{3,15},{4,0},{5,1},{6,2},{7,3},{8,4},{9,5},{1... | collective-permute-start | bytes 786440 | tf_op jit(solution)/shard_map/ppermute | solution.py:254
  25.8 7.8 %collective-permute-start.6 = (bf16[4,2,16,1024]{3,2,1,0:T(8,128)(2,1)S(1)}, bf16[4,2,16,1024]{3,2,1,0:T(8,128)(2,1)S(1)}, u32[]{:S(2)}, u32[]{:S(2)}) collective-permute-start(bf16[4,2,16,1024]{3,2,1,0:T(8,128)(2,1)S(1)} %get-tuple-element.72), channel_id=1, source_target_pairs={{0,2},{1,3},{2,0},{3,1},{4,6},{5,7},{6,4},{7,5},{8,10},{9,11},{10,... | collective-permute-start | bytes 786440 | tf_op jit(solution)/shard_map/ppermute | solution.py:254
  34.5 13.2 %collective-permute-start.9 = (bf16[4,2,16,1024]{3,2,1,0:T(8,128)(2,1)S(1)}, bf16[4,2,16,1024]{3,2,1,0:T(8,128)(2,1)S(1)}, u32[]{:S(2)}, u32[]{:S(2)}) collective-permute-start(bf16[4,2,16,1024]{3,2,1,0:T(8,128)(2,1)S(1)} %get-tuple-element.80), channel_id=1, source_target_pairs={{0,4},{1,5},{2,6},{3,7},{4,8},{5,9},{6,10},{7,11},{8,12},{9,13},{1... | collective-permute-start | bytes 786440 | tf_op jit(solution)/shard_map/ppermute | solution.py:254
  34.5 13.1 %collective-permute-start.10 = (bf16[4,2,16,1024]{3,2,1,0:T(8,128)(2,1)S(1)}, bf16[4,2,16,1024]{3,2,1,0:T(8,128)(2,1)S(1)}, u32[]{:S(2)}, u32[]{:S(2)}) collective-permute-start(bf16[4,2,16,1024]{3,2,1,0:T(8,128)(2,1)S(1)} %get-tuple-element.81), channel_id=1, source_target_pairs={{0,12},{1,13},{2,14},{3,15},{4,0},{5,1},{6,2},{7,3},{8,4},{9,5},{1... | collective-permute-start | bytes 786440 | tf_op jit(solution)/shard_map/ppermute | solution.py:254
  37.2 10.4 %collective-permute-start.11 = (bf16[4,2,16,1024]{3,2,1,0:T(8,128)(2,1)S(1)}, bf16[4,2,16,1024]{3,2,1,0:T(8,128)(2,1)S(1)}, u32[]{:S(2)}, u32[]{:S(2)}) collective-permute-start(bf16[4,2,16,1024]{3,2,1,0:T(8,128)(2,1)S(1)} %get-tuple-element.82), channel_id=1, source_target_pairs={{0,2},{1,3},{2,0},{3,1},{4,6},{5,7},{6,4},{7,5},{8,10},{9,11},{10,... | collective-permute-start | bytes 786440 | tf_op jit(solution)/shard_map/ppermute | solution.py:254
  40.9 13.0 %collective-permute-start.7 = (f32[4,4,4,1024]{3,2,1,0:T(4,128)S(1)}, f32[4,4,4,1024]{3,2,1,0:T(4,128)S(1)}, u32[]{:S(2)}, u32[]{:S(2)}) collective-permute-start(f32[4,4,4,1024]{3,2,1,0:T(4,128)S(1)} %get-tuple-element.78), channel_id=1, source_target_pairs={{0,16},{16,32},{32,48},{48,64},{64,80},{80,96},{96,112},{1,17},{17... | collective-permute-start | bytes 786440 | tf_op jit(solution)/shard_map/ppermute | solution.py:580
  42.9 11.1 %collective-permute-start.8 = (f32[4,4,4,1024]{3,2,1,0:T(4,128)S(1)}, f32[4,4,4,1024]{3,2,1,0:T(4,128)S(1)}, u32[]{:S(2)}, u32[]{:S(2)}) collective-permute-start(f32[4,4,4,1024]{3,2,1,0:T(4,128)S(1)} %get-tuple-element.79), channel_id=1, source_target_pairs={{16,0},{32,16},{48,32},{64,48},{80,64},{96,80},{112,96},{17,1},{33... | collective-permute-start | bytes 786440 | tf_op jit(solution)/shard_map/ppermute | solution.py:580
  48.5 6.8 %collective-permute-start.12 = (bf16[4,2,16,1024]{3,2,1,0:T(8,128)(2,1)S(1)}, bf16[4,2,16,1024]{3,2,1,0:T(8,128)(2,1)S(1)}, u32[]{:S(2)}, u32[]{:S(2)}) collective-permute-start(bf16[4,2,16,1024]{3,2,1,0:T(8,128)(2,1)S(1)} %get-tuple-element.87), channel_id=1, source_target_pairs={{0,4},{1,5},{2,6},{3,7},{4,8},{5,9},{6,10},{7,11},{8,12},{9,13},{1... | collective-permute-start | bytes 786440 | tf_op jit(solution)/shard_map/ppermute | solution.py:254
  48.6 6.7 %collective-permute-start.13 = (bf16[4,2,16,1024]{3,2,1,0:T(8,128)(2,1)S(1)}, bf16[4,2,16,1024]{3,2,1,0:T(8,128)(2,1)S(1)}, u32[]{:S(2)}, u32[]{:S(2)}) collective-permute-start(bf16[4,2,16,1024]{3,2,1,0:T(8,128)(2,1)S(1)} %get-tuple-element.91), channel_id=1, source_target_pairs={{0,12},{1,13},{2,14},{3,15},{4,0},{5,1},{6,2},{7,3},{8,4},{9,5},{1... | collective-permute-start | bytes 786440 | tf_op jit(solution)/shard_map/ppermute | solution.py:254
  51.3 7.0 %collective-permute-start.14 = (bf16[4,2,16,1024]{3,2,1,0:T(8,128)(2,1)S(1)}, bf16[4,2,16,1024]{3,2,1,0:T(8,128)(2,1)S(1)}, u32[]{:S(2)}, u32[]{:S(2)}) collective-permute-start(bf16[4,2,16,1024]{3,2,1,0:T(8,128)(2,1)S(1)} %get-tuple-element.92), channel_id=1, source_target_pairs={{0,2},{1,3},{2,0},{3,1},{4,6},{5,7},{6,4},{7,5},{8,10},{9,11},{10,... | collective-permute-start | bytes 786440 | tf_op jit(solution)/shard_map/ppermute | solution.py:254
  61.7 26.9 %copy-start.5 = (s32[4]{0:T(128)S(1)}, s32[4]{0:T(128)}, u32[]{:S(2)}) copy-start(s32[4]{0:T(128)} %param.10) | copy-start | bytes 52
  61.7 15.0 %collective-permute-start.15 = (bf16[8,4,2,16,1024]{4,3,2,1,0:T(8,128)(2,1)}, bf16[8,4,2,16,1024]{4,3,2,1,0:T(8,128)(2,1)S(1)}, u32[]{:S(2)}, u32[]{:S(2)}) collective-permute-start(bf16[8,4,2,16,1024]{4,3,2,1,0:T(8,128)(2,1)} %shard_map.70.rest_3_.mine_ref), channel_id=1, source_target_pairs={{0,1},{1,0},{2,3},{3,2},{4,5},{5,4},{6,7},{7,6},{8,9},{9,8},{10,11... | collective-permute-start | bytes 6291464 | tf_op jit(solution)/shard_map/ppermute | solution.py:259
  67.6 9.1 %collective-permute-start.16 = (bf16[4,2,16,1024]{3,2,1,0:T(8,128)(2,1)S(1)}, bf16[4,2,16,1024]{3,2,1,0:T(8,128)(2,1)S(1)}, u32[]{:S(2)}, u32[]{:S(2)}) collective-permute-start(bf16[4,2,16,1024]{3,2,1,0:T(8,128)(2,1)S(1)} %get-tuple-element.98), channel_id=1, source_target_pairs={{0,4},{1,5},{2,6},{3,7},{4,8},{5,9},{6,10},{7,11},{8,12},{9,13},{1... | collective-permute-start | bytes 786440 | tf_op jit(solution)/shard_map/ppermute | solution.py:254
  67.6 9.1 %collective-permute-start.17 = (bf16[4,2,16,1024]{3,2,1,0:T(8,128)(2,1)S(1)}, bf16[4,2,16,1024]{3,2,1,0:T(8,128)(2,1)S(1)}, u32[]{:S(2)}, u32[]{:S(2)}) collective-permute-start(bf16[4,2,16,1024]{3,2,1,0:T(8,128)(2,1)S(1)} %get-tuple-element.100), channel_id=1, source_target_pairs={{0,12},{1,13},{2,14},{3,15},{4,0},{5,1},{6,2},{7,3},{8,4},{9,5},{1... | collective-permute-start | bytes 786440 | tf_op jit(solution)/shard_map/ppermute | solution.py:254
  70.3 8.8 %collective-permute-start.18 = (bf16[4,2,16,1024]{3,2,1,0:T(8,128)(2,1)S(1)}, bf16[4,2,16,1024]{3,2,1,0:T(8,128)(2,1)S(1)}, u32[]{:S(2)}, u32[]{:S(2)}) collective-permute-start(bf16[4,2,16,1024]{3,2,1,0:T(8,128)(2,1)S(1)} %get-tuple-element.101), channel_id=1, source_target_pairs={{0,2},{1,3},{2,0},{3,1},{4,6},{5,7},{6,4},{7,5},{8,10},{9,11},{10,... | collective-permute-start | bytes 786440 | tf_op jit(solution)/shard_map/ppermute | solution.py:254
  81.0 11.3 %collective-permute-start.19 = (bf16[3,4,2,16,1024]{4,3,2,1,0:T(8,128)(2,1)S(1)}, bf16[3,4,2,16,1024]{4,3,2,1,0:T(8,128)(2,1)}, u32[]{:S(2)}, u32[]{:S(2)}) collective-permute-start(bf16[3,4,2,16,1024]{4,3,2,1,0:T(8,128)(2,1)S(1)} %get-tuple-element.107.mine_last), channel_id=1, source_target_pairs={{0,1},{1,0},{2,3},{3,2},{4,5},{5,4},{6,7},{7,6},{8,9},{9,8},{10,11... | collective-permute-start | bytes 2359304 | tf_op jit(solution)/shard_map/ppermute | solution.py:259
  82.5 9.1 %collective-permute-start.21 = (bf16[4,16,1024]{2,1,0:T(8,128)(2,1)S(1)}, bf16[4,16,1024]{2,1,0:T(8,128)(2,1)S(1)}, u32[]{:S(2)}, u32[]{:S(2)}) collective-permute-start(bf16[4,16,1024]{2,1,0:T(8,128)(2,1)S(1)} %get-tuple-element.102), channel_id=1, source_target_pairs={{1,16},{3,18},{5,20},{7,22},{9,24},{11,26},{13,28},{15,30},{16,1},... | collective-permute-start | bytes 393224 | tf_op jit(solution)/shard_map/ppermute | solution.py:320
  86.6 5.7 %collective-permute-start.20 = (bf16[4,16,1024]{2,1,0:T(8,128)(2,1)S(1)}, bf16[4,16,1024]{2,1,0:T(8,128)(2,1)S(1)}, u32[]{:S(2)}, u32[]{:S(2)}) collective-permute-start(bf16[4,16,1024]{2,1,0:T(8,128)(2,1)S(1)} %get-tuple-element.102), channel_id=1, source_target_pairs={{1,17},{3,19},{5,21},{7,23},{9,25},{11,27},{13,29},{15,31},{16,0},... | collective-permute-start | bytes 393224 | tf_op jit(solution)/shard_map/ppermute | solution.py:320
  88.7 2.2 %copy-start = (f32[4,4,64,1024]{3,2,1,0:T(8,128)S(1)}, f32[4,4,64,1024]{3,2,1,0:T(8,128)}, u32[]{:S(2)}) copy-start(f32[4,4,64,1024]{3,2,1,0:T(8,128)} %field_hbm) | copy-start | bytes 12582916
  90.9 1.5 %copy-start.1 = (f32[4]{0:T(128)S(1)}, f32[4]{0:T(128)}, u32[]{:S(2)}) copy-start(f32[4]{0:T(128)} %amount_ref.1) | copy-start | bytes 52

commit v2 on v1

--- a/solution.py
+++ b/solution.py
@@ -18,67 +18,72 @@
 
 SCHEDULES = (
     (
-        (2, 4, 5, -1, -1, -1, -1, -1, -1, -1, -1, -1, -1, -1, -1, -1, -1, -1, -1, -1, -1, -1, -1, -1),
-        (3, 7, 6, 5, 5, -1, 2, -1, 2, -1, -1, -1, -1, -1, -1, -1, -1, -1, -1, -1, 4, -1, -1, -1),
-        (7, 1, 0, 6, 6, -1, 3, -1, 3, 5, -1, 5, 2, -1, 2, -1, -1, -1, 7, 4, 7, -1, 4, 5),
-        (1, 0, 1, 0, 0, 0, 7, 2, 7, -1, 3, 6, 3, -1, 3, 2, -1, 5, -1, 1, -1, 4, 6, -1),
-        (7, 7, 7, 4, 1, 5, 3, 6, 1, 0, 0, 0, 1, 4, 1, 3, 6, 6, 4, 0, 5, 2, 7, 6),
-    ),
-    (
-        (-1, -1, -1, -1, -1, -1, -1, -1, -1, -1, -1, -1, -1, -1, -1, -1, -1, -1, -1, -1, -1, -1, -1, -1),
-        (0, 3, 1, 5, 7, 6, -1, -1, -1, -1, -1, -1, -1, -1, -1, -1, -1, -1, -1, -1, -1, -1, -1, -1),
-        (1, 2, 2, 4, 6, 4, 0, -1, 0, 5, -1, 5, -1, -1, -1, -1, -1, -1, -1, 3, 3, -1, 7, 7),
-        (6, 4, 3, 2, 1, -1, 1, -1, -1, 4, 5, 4, 3, 3, 0, 5, 7, 7, 7, 2, 2, 6, 6, 6),
-        (7, 0, 1, 1, 7, 5, 5, 6, 3, 2, 0, 2, 1, 1, 1, 0, 6, 6, 4, 4, 4, 2, 3, 5),
-    ),
-    (
-        (-1, -1, -1, -1, -1, -1, -1, -1, -1, -1, -1, -1, -1, -1, -1, -1, -1, -1, -1, -1, -1, -1, -1, -1),
-        (0, 3, 0, -1, -1, -1, 6, 5, 7, -1, -1, -1, -1, -1, -1, -1, -1, -1, -1, -1, -1, -1, -1, -1),
-        (1, 2, 1, -1, 0, -1, 4, 7, 5, 7, 7, -1, 6, -1, 6, -1, -1, -1, -1, 3, 3, -1, -1, -1),
-        (2, 5, 2, 0, 7, 1, 1, 4, 1, 5, 5, -1, 4, 3, 4, 6, 6, 7, -1, 6, 2, 3, 0, 0),
-        (7, 7, 4, 2, 1, 5, 2, 6, 3, 1, 0, 0, 1, 4, 3, 5, 4, 5, 4, 0, 4, 6, 2, -1),
-    ),
-    (
-        (-1, -1, -1, -1, -1, -1, -1, -1, -1, -1, -1, -1, -1, -1, -1, -1, -1, -1, -1, -1, -1, -1, -1, -1),
-        (0, 2, 1, -1, -1, -1, -1, -1, -1, 6, 4, 5, -1, -1, -1, -1, -1, -1, -1, -1, -1, -1, -1, -1),
-        (3, 3, 0, 1, 1, 4, 0, 5, 0, 4, 5, 7, -1, -1, -1, -1, -1, 6, -1, 2, 2, -1, -1, -1),
-        (1, 5, 3, -1, 0, -1, 7, 7, 3, 5, 7, 6, 6, 2, 2, 4, 4, 4, -1, -1, 3, -1, 1, 1),
-        (7, 7, 1, 7, 7, 5, 1, 6, 3, 3, 6, 0, 0, 4, 7, 5, 2, 5, -1, 3, 6, 2, 0, 4),
-    ),
-    (
-        (-1, -1, -1, -1, -1, -1, -1, -1, -1, -1, -1, -1, -1, -1, -1, -1, -1, -1, -1, -1, -1, -1, -1, -1),
-        (0, 2, 3, -1, -1, -1, -1, -1, -1, -1, -1, -1, 6, 7, 5, -1, -1, -1, -1, -1, -1, -1, -1, -1),
-        (1, 1, 1, 3, 3, -1, 0, 7, 0, -1, -1, -1, 4, 6, 4, -1, 5, -1, -1, 2, 6, -1, -1, -1),
-        (3, 3, 7, 1, 1, 1, 1, 0, 6, 0, 5, -1, 5, 2, 2, 4, 4, -1, 2, 4, 2, 6, 3, 6),
-        (7, 7, 0, 7, 7, 5, 6, 6, 3, 6, 4, 5, 0, 4, 7, 0, 2, 5, 4, 3, 5, 2, 1, 2),
-    ),
-    (
-        (-1, -1, -1, -1, -1, -1, -1, -1, -1, -1, -1, -1, -1, -1, -1, -1, -1, -1, -1, -1, -1, -1, -1, -1),
-        (1, 3, 0, -1, -1, -1, -1, -1, -1, -1, -1, -1, -1, -1, -1, 7, 5, 4, -1, -1, -1, -1, -1, -1),
-        (0, 2, 1, -1, 0, -1, 1, -1, -1, -1, -1, 5, 4, -1, -1, 5, 6, 6, -1, 3, -1, 7, 7, 7),
-        (2, 3, 3, 1, 1, 7, 0, 5, 0, 6, 6, 6, 6, 3, 3, 4, 4, 7, 4, 2, 2, 5, 0, 0),
-        (7, 5, 4, 7, 3, 5, 6, 6, 2, 1, 0, 4, 1, 1, 7, 5, 3, 5, 4, 3, 6, 2, 2, 2),
-    ),
-    (
-        (-1, -1, -1, -1, -1, -1, -1, -1, -1, -1, -1, -1, -1, -1, -1, -1, -1, -1, -1, -1, -1, -1, -1, -1),
-        (0, 1, 1, -1, -1, -1, -1, -1, -1, -1, -1, -1, -1, -1, -1, -1, -1, -1, 6, 5, 7, -1, -1, -1),
-        (2, 3, 6, 1, -1, -1, 0, -1, 0, -1, -1, -1, -1, -1, 5, -1, -1, -1, 7, 4, 4, 7, 7, -1),
-        (3, 7, 2, 6, 6, -1, 2, 0, 2, 1, -1, 1, 0, 4, 0, 5, 5, 7, -1, 1, 3, 4, 4, -1),
-        (6, 3, 3, 7, 2, 4, 3, -1, 3, 6, 0, 5, 2, 7, 2, 1, 4, -1, 5, 6, 0, 5, 3, 4),
-    ),
-    (
-        (-1, -1, -1, -1, -1, -1, -1, -1, -1, -1, -1, -1, -1, -1, -1, -1, -1, -1, -1, -1, -1, -1, -1, -1),
-        (3, 1, 2, -1, -1, -1, -1, -1, -1, -1, -1, -1, -1, -1, -1, -1, -1, -1, -1, -1, -1, 5, 6, 7),
-        (0, 3, 0, 2, 2, 5, 3, -1, 3, -1, -1, -1, -1, -1, -1, -1, 6, 6, 7, 1, -1, 4, 4, 4),
-        (2, 5, 1, 5, 0, 0, -1, 3, 0, 2, 6, 6, 1, 1, 1, -1, -1, 4, 4, 7, 3, 7, 5, 2),
-        (7, 0, 3, 7, 7, 5, 0, 6, 1, 3, 0, 5, -1, 4, 7, 1, 4, 5, 4, 2, 5, 2, 0, 6),
+        (4, 5, 0, -1, -1, -1, -1, -1, -1, -1, -1, -1, -1, -1, -1, -1, -1, -1, -1, -1, -1, -1, -1, -1),
+        (3, 1, 7, -1, 0, -1, 4, -1, 4, -1, -1, -1, -1, -1, -1, -1, -1, -1, -1, 5, 5, -1, -1, -1),
+        (1, 2, 6, 7, -1, -1, -1, -1, 3, -1, -1, -1, -1, 5, 4, -1, -1, -1, -1, 1, 1, 5, 0, 0),
+        (0, 6, 2, 6, 7, -1, 3, -1, 1, 3, 4, 7, 4, 4, 1, 4, 0, 0, -1, 2, 2, 1, 5, -1),
+        (5, 7, 3, 2, -1, -1, 7, -1, 3, 6, 7, 6, 3, 2, 2, 3, 5, -1, -1, 6, 6, -1, 7, 2),
+    ),
+    (
+        (-1, -1, -1, -1, -1, -1, -1, -1, -1, -1, -1, -1, -1, -1, -1, -1, -1, -1, -1, -1, -1, -1, -1, -1),
+        (1, 3, 0, 6, 4, 4, -1, -1, -1, -1, -1, -1, -1, -1, -1, -1, -1, -1, -1, -1, -1, -1, -1, -1),
+        (0, 2, 1, 5, 0, 7, 1, -1, 1, 6, -1, -1, -1, -1, -1, -1, -1, -1, -1, 3, 3, -1, 4, 4),
+        (4, 7, 2, 7, 1, 5, 0, -1, 0, 5, -1, 5, 1, 3, 1, 6, 4, 4, -1, 2, 4, -1, 0, 0),
+        (7, 5, 3, 2, 7, 6, 5, -1, 3, 7, -1, 6, 3, 2, 2, 5, 5, 6, -1, 7, 2, -1, 3, 6),
+    ),
+    (
+        (-1, -1, -1, -1, -1, -1, -1, -1, -1, -1, -1, -1, -1, -1, -1, -1, -1, -1, -1, -1, -1, -1, -1, -1),
+        (1, 0, 1, -1, -1, -1, 6, 5, 4, -1, -1, -1, -1, -1, -1, -1, -1, -1, -1, -1, -1, -1, -1, -1),
+        (0, 3, 2, 1, 1, -1, 5, 4, 7, 4, 4, -1, 6, -1, 6, -1, -1, -1, -1, 0, 0, -1, -1, -1),
+        (2, 4, 3, 2, 2, -1, 1, 7, 0, 7, 7, -1, 5, -1, 0, 4, 6, 4, -1, 3, 3, 0, 1, 1),
+        (2, 7, 5, 3, 7, -1, 2, 7, 5, 2, 6, -1, 5, 3, 5, 6, -1, 7, 6, -1, 5, -1, 3, 2),
+    ),
+    (
+        (-1, -1, -1, -1, -1, -1, -1, -1, -1, -1, -1, -1, -1, -1, -1, -1, -1, -1, -1, -1, -1, -1, -1, -1),
+        (0, 1, 0, -1, -1, -1, -1, -1, -1, 4, 5, 6, -1, -1, -1, -1, -1, -1, -1, -1, -1, -1, -1, -1),
+        (1, 2, 3, -1, 0, 5, 0, -1, 0, 7, 6, 4, -1, -1, -1, 4, -1, 4, -1, 1, 1, -1, -1, -1),
+        (3, 5, 2, 3, 6, -1, 6, 4, 1, 5, 4, 7, 0, 1, 1, -1, -1, 7, 1, 2, 2, 1, 0, 4),
+        (5, 3, 5, 2, 3, 6, 3, 7, 6, 3, 7, 7, 7, 2, 2, 7, -1, 7, -1, 5, 5, 2, 6, 6),
+    ),
+    (
+        (-1, -1, -1, -1, -1, -1, -1, -1, -1, -1, -1, -1, -1, -1, -1, -1, -1, -1, -1, -1, -1, -1, -1, -1),
+        (0, 0, 1, -1, -1, -1, -1, -1, -1, -1, -1, -1, 4, 6, 4, -1, -1, -1, -1, -1, -1, -1, -1, -1),
+        (3, 1, 2, 1, 1, -1, -1, 6, 0, -1, -1, -1, 6, 7, 5, 4, 4, -1, -1, -1, 0, -1, -1, -1),
+        (3, 2, 3, 2, 2, -1, 0, 7, 3, 1, 4, 1, 5, 4, 7, 5, 5, 5, 4, 1, 6, 0, 0, -1),
+        (7, 3, 7, 3, 3, -1, 3, 6, 6, 3, 5, 2, 7, 5, 6, 7, 7, -1, 5, 2, 2, 6, 2, 6),
+    ),
+    (
+        (-1, -1, -1, -1, -1, -1, -1, -1, -1, -1, -1, -1, -1, -1, -1, -1, -1, -1, -1, -1, -1, -1, -1, -1),
+        (1, 2, 0, -1, -1, -1, -1, -1, -1, -1, -1, -1, -1, -1, -1, 6, 4, 7, -1, -1, -1, -1, -1, -1),
+        (0, 3, 1, 0, 0, -1, 1, -1, 1, -1, 4, -1, -1, 7, -1, 5, 6, 4, 2, -1, 2, 6, -1, 6),
+        (2, 1, 3, -1, 1, 4, 0, 7, -1, 1, 0, 6, 4, 4, 7, 4, 5, -1, -1, 3, 6, 5, 0, 0),
+        (7, 7, 7, 3, 3, 5, 2, 2, 2, -1, -1, 5, 3, 3, 3, 7, 7, 5, 6, 6, 2, 2, 2, 5),
+    ),
+    (
+        (-1, -1, -1, -1, -1, -1, -1, -1, -1, -1, -1, -1, -1, -1, -1, -1, -1, -1, -1, -1, -1, -1, -1, -1),
+        (0, 0, 1, -1, -1, -1, -1, -1, -1, -1, -1, -1, -1, -1, -1, -1, -1, -1, 6, 7, 4, -1, -1, -1),
+        (3, 1, 2, 1, 1, -1, 0, -1, 0, -1, -1, -1, -1, 7, 7, -1, -1, -1, 4, 5, 6, 4, 4, -1),
+        (4, 2, 3, 2, 2, -1, -1, 7, 3, 1, 0, 1, -1, 5, 0, 7, 4, 4, 5, 1, 0, 6, 6, -1),
+        (6, 3, 5, 6, 3, -1, 3, -1, 5, 3, -1, 2, -1, -1, 5, -1, 7, 6, -1, 2, 5, 7, 2, -1),
+    ),
+    (
+        (-1, -1, -1, -1, -1, -1, -1, -1, -1, -1, -1, -1, -1, -1, -1, -1, -1, -1, -1, -1, -1, -1, -1, -1),
+        (0, 1, 2, -1, -1, -1, -1, -1, -1, -1, -1, -1, -1, -1, -1, -1, -1, -1, -1, -1, -1, 4, 7, 4),
+        (1, 3, 0, 4, -1, -1, 0, -1, 0, -1, -1, -1, -1, -1, -1, -1, 7, -1, -1, 4, 1, 5, 6, 5),
+        (3, 2, 1, 2, 0, 5, 1, -1, 1, 4, 0, 7, 0, 4, 0, -1, 6, 7, 4, 5, 3, 5, 1, 6),
+        (2, 2, 3, 5, 2, -1, 3, 7, 3, 2, 6, 6, 7, 5, 5, 7, -1, 6, 6, 2, 6, 7, 3, 5),
     ),
 )
 
 
-def piece_of(tile, piece, half):
-    at = pl.multiple_of(half * 32 + 16 * (piece // 2), 16)
-    return tile.at[:, pl.ds(2 * (piece % 2), 2), pl.ds(at, 16), :]
+def parts_of(snap, piece, half, tile, held):
+    if snap == 0:
+        at = pl.multiple_of(half * 32 + 16 * ((piece // 2) ^ half), 16)
+        return [(tile.at[:, pl.ds(2 * (piece % 2), 2), pl.ds(at, 16), :], held)]
+    return [
+        (tile.at[(piece + 3) % 4, :, pl.ds(pl.multiple_of(half * 32 + 16 * part, 16), 16), :], held.at[:, part])
+        for part in range(2)
+    ]
 
 
 def plan(ids_ref, table_ref):
@@ -126,13 +131,12 @@
 def share_kernel(ids_ref, store_ref, out_ref, stage, sems):
     core = lax.axis_index("rel") & 1
     slots = range(2 * PIECES)
-    run_staged(
-        [
-            (None, piece_of(store_ref.at[ids_ref[slot // PIECES] & 1], slot % PIECES, 1 - core), stage.at[slot], sems.at[slot])
-            for slot in slots
-        ],
-        [(None, stage.at[slot], out_ref.at[slot], sems.at[slot]) for slot in slots],
-    )
+    loads = []
+    for slot in slots:
+        store = store_ref.at[ids_ref[slot // PIECES] & 1]
+        for part, (source, target) in enumerate(parts_of(slot // PIECES, slot % PIECES, 1 - core, store, stage.at[slot])):
+            loads.append((None, source, target, sems.at[2 * slot + part]))
+    run_staged(loads, [(None, stage.at[slot], out_ref.at[slot], sems.at[slot]) for slot in slots])
 
 
 def first_kernel(phase, brought, keeps, ids_ref, table_ref, store_ref, shared_ref, *rest):
@@ -144,9 +148,10 @@
     loads, stores = [], []
     for slot in range(2 * PIECES):
         root = ids_ref[slot // PIECES] >> 1
-        stored = piece_of(store_ref.at[ids_ref[slot // PIECES] & 1], slot % PIECES, core)
-        loads.append((root == me, stored, stage.at[slot], sems.at[slot]))
-        loads.append((root == (me ^ 1), shared_ref.at[slot], stage.at[slot], sems.at[slot]))
+        store = store_ref.at[ids_ref[slot // PIECES] & 1]
+        for part, (source, target) in enumerate(parts_of(slot // PIECES, slot % PIECES, core, store, stage.at[slot])):
+            loads.append((root == me, source, target, sems.at[2 * slot + part]))
+        loads.append((root == (me ^ 1), shared_ref.at[slot], stage.at[slot], sems.at[2 * slot]))
         held = (root >> 1) == (me >> 1)
         for link in range(LINKS):
             chosen = jnp.logical_and(held, sent(phase, link) == slot)
@@ -156,7 +161,7 @@
     for way in range(brought):
         slot = got(0, way)
         at = 2 * PIECES + way
-        loads.append((None, arrived[way], stage.at[at], sems.at[at]))
+        loads.append((None, arrived[way], stage.at[at], sems.at[4 * PIECES + way]))
         for link in range(LINKS):
             chosen = jnp.logical_and(slot >= 0, sent(phase, link) == slot)
             stores.append((chosen, stage.at[at], outs[link], sems.at[link]))
@@ -188,31 +193,22 @@
     )
 
 
-def wherever(slot, phase, got, arrived, held_ref, inner=()):
+def wherever(slot, phase, got, arrived, held_ref):
     older = slot >= 0
     places = []
     for way in range(LINKS):
-        places.append((jnp.logical_and(slot >= 0, got(phase, way) == slot), arrived[way].at[inner] if inner else arrived[way]))
+        places.append((jnp.logical_and(slot >= 0, got(phase, way) == slot), arrived[way]))
         older = jnp.logical_and(older, got(phase, way) != slot)
-    return [*places, (older, held_ref.at[(jnp.maximum(slot, 0), *inner)])]
-
-
-def edge_kernel(ids_ref, table_ref, *rest):
-    arrived, held_ref, out_ref, last_ref, stage, stage_kd, rows, last, sems = rest[:LINKS], *rest[LINKS:]
+    return [*places, (older, held_ref.at[jnp.maximum(slot, 0)])]
+
+
+def edge_kernel(held_ref, out_ref, stage, stage_kd, rows, sems):
     core = lax.axis_index("rel") & 1
-    _, got = plan(ids_ref, table_ref)
-    copies = []
-    for pair in range(2):
-        slot = 2 * core + pair
-        for condition, source in wherever(slot, PHASES, got, arrived, held_ref):
-            copies.append((condition, source, stage.at[pair], sems.at[pair]))
-        for condition, source in wherever(PIECES + slot, PHASES, got, arrived, held_ref, (3,)):
-            copies.append((condition, source, stage_kd.at[pair], sems.at[2 + pair]))
-    for way in range(LINKS):
-        copies.append((None, arrived[way], last.at[way], sems.at[4 + way]))
-    run_copies(copies)
-    out_copies = [(None, last, last_ref, sems.at[4])]
-    run_copies(out_copies, (True,))
+    run_copies([
+        (None, held_ref.at[0], stage.at[0], sems.at[0]),
+        (None, held_ref.at[1], stage.at[1], sems.at[1]),
+        (None, held_ref.at[PIECES, :, core], stage_kd, sems.at[2]),
+    ])
     rows[:, 10:, :] = jnp.zeros_like(rows[:, 10:, :])
     for level in range(4):
         def ends(block, count):
@@ -222,9 +218,8 @@
         for channel in range(3):
             rows[level, 2 * channel : 2 * channel + 2, :] = ends(stage[level // 2, channel, level % 2], 2)
         rows[level, 6:9, :] = ends(stage[level // 2, 3, level % 2], 3)
-        rows[level, 9:10, :] = ends(stage_kd[level // 2, level % 2], 1)
+        rows[level, 9:10, :] = ends(stage_kd[level], 1)
     out_ref[...] = rows[...].astype(jnp.bfloat16)
-    run_copies(out_copies, (False,))
 
 
 def moved(kernel, scalars, inputs, outs, scratch, aliases=None, vmem_outs=0):
@@ -268,13 +263,13 @@
     def stage(slots):
         return pltpu.VMEM((slots,) + PIECE, jnp.bfloat16)
 
-    (shared,) = moved(share_kernel, (ids,), [wind_store], [every], [stage(2 * PIECES), dma((2 * PIECES,))])
+    (shared,) = moved(share_kernel, (ids,), [wind_store], [every], [stage(2 * PIECES), dma((4 * PIECES,))])
     shared = other_core(shared)
 
     def begin(phase, keeps, wind_store, shared, arrived):
         return moved(
             functools.partial(first_kernel, phase, len(arrived), keeps), (ids, table), [wind_store, shared, *arrived],
-            sent + [every] * keeps, [stage(2 * PIECES + LINKS), dma((2 * LINKS + 2 * PIECES,))],
+            sent + [every] * keeps, [stage(2 * PIECES + LINKS), dma((4 * PIECES + LINKS,))],
         )
 
     def one_chip(wind_store, shared):
@@ -291,24 +286,23 @@
         arrived = exchange(sends)
         if phase == 3:
             west, east, arrived[0] = lax.optimization_barrier((west, east, arrived[0]))
-        if phase < PHASES:
+        if phase == PHASES:
+            held, arrived[0] = lax.optimization_barrier((held, arrived[0]))
+            (edges,) = moved(
+                edge_kernel, (), [held], [(4, 16, 1024)],
+                [stage(2), pltpu.VMEM((4, 16, 1024), jnp.bfloat16), pltpu.VMEM((4, 16, 1024), jnp.float32), dma((3,))],
+                vmem_outs=1,
+            )
+        else:
             sends = moved(
                 functools.partial(forward_kernel, phase), (ids, table), [*arrived, held], sent, [stage(LINKS), dma((LINKS,))]
             )
             *sends, held = lax.optimization_barrier((*sends, held))
-            (held,) = moved(
-                functools.partial(keep_kernel, phase), (ids, table), [*arrived, held], [every], [stage(LINKS), dma((LINKS,))],
-                {2 + LINKS: 0},
-            )
+        (held,) = moved(
+            functools.partial(keep_kernel, phase), (ids, table), [*arrived, held], [every], [stage(LINKS), dma((LINKS,))],
+            {2 + LINKS: 0},
+        )
     other = other_core(held)
-    other, arrived[0] = lax.optimization_barrier((other, arrived[0]))
-    edges, last = moved(
-        edge_kernel, (ids, table), [*arrived, held], [(4, 16, 1024), (LINKS,) + PIECE],
-        [
-            stage(2), pltpu.VMEM((2,) + PIECE[1:], jnp.bfloat16), pltpu.VMEM((4, 16, 1024), jnp.float32), stage(LINKS),
-            dma((4 + LINKS,)),
-        ], vmem_outs=1,
-    )
     ends = []
     for flip in range(2):
         pairs = []
@@ -318,9 +312,8 @@
                 if 0 <= to < 8:
                     pairs.append((slab * 16 + rel, to * 16 + (rel ^ flip)))
         ends.append(lax.ppermute(edges, ("slab", "rel"), pairs))
-    after, west, east, edges = lax.optimization_barrier((field, west, east, edges))
-    start = lay_out(after, west, east)
-    return (ids, table), start, held, other, last, other_core(last), *ends
+    after, west, east, held = lax.optimization_barrier((field, west, east, held))
+    return lay_out(after, west, east), held, other, *ends
 
 
 def shifted_y(here, left, right, lane):
@@ -405,7 +398,7 @@
     )(field, west, east)
 
 
-def steps_kernel(ids_ref, table_ref, cells_ref, amount_ref, first, mine_ref, other_ref, mine_last, other_last, *rest):
+def steps_kernel(cells_ref, amount_ref, first, mine_ref, other_ref, *rest):
     near_ref, far_ref, out_hbm, second, result, winds, half_kds, halo_wind, wind_sems, out_sems = rest
     releases, levels, chunks, padded_rows, _ = first.shape
     rows = padded_rows - 2 * PAD
@@ -419,13 +412,12 @@
             out_sems.at[j],
         )
 
-    _, got = plan(ids_ref, table_ref)
     wind_copies = []
     for slot in range(2 * PIECES):
-        for number, (held_ref, last, half) in enumerate(((mine_ref, mine_last, core), (other_ref, other_last, 1 - core))):
-            target = piece_of(winds.at[slot // PIECES], slot % PIECES, half)
-            for condition, source in wherever(jnp.int32(slot), PHASES, got, [last.at[way] for way in range(LINKS)], held_ref):
-                wind_copies.append((condition, source, target, wind_sems.at[2 * slot + number]))
+        snap = slot // PIECES
+        for number, (held, half) in enumerate(((mine_ref, core), (other_ref, 1 - core))):
+            for part, (target, source) in enumerate(parts_of(snap, slot % PIECES, half, winds.at[snap], held.at[slot])):
+                wind_copies.append((None, source, target, wind_sems.at[4 * slot + 2 * number + part]))
     run_copies(wind_copies, (True,))
 
     lane = lax.broadcasted_iota(jnp.int32, (8, LANES), 1)
@@ -548,7 +540,7 @@
         store(j).wait()
 
 
-def steps(shape, scalars, start, mine, other, mine_last, other_last, near, far, cells, amounts):
+def steps(shape, start, mine, other, near, far, cells, amounts):
     releases, levels, rows, width = shape
     chunks = width // LANES
     vmem = pl.BlockSpec(memory_space=pltpu.VMEM)
@@ -557,7 +549,7 @@
     return pl.pallas_call(
         steps_kernel,
         out_shape=jax.ShapeDtypeStruct(shape, jnp.float32),
-        in_specs=[smem] * 4 + [vmem] + [anywhere] * 4 + [vmem, vmem],
+        in_specs=[smem, smem, vmem, anywhere, anywhere, vmem, vmem],
         out_specs=pl.BlockSpec(memory_space=pltpu.HBM),
         scratch_shapes=[
             pltpu.VMEM(start.shape, jnp.float32),
@@ -565,12 +557,12 @@
             pltpu.VMEM((2, 4, levels, rows, width), jnp.bfloat16),
             pltpu.VMEM((2,) + start.shape[1:], jnp.float32),
             pltpu.VMEM((3, levels, chunks, 8, LANES), jnp.float32),
-            pltpu.SemaphoreType.DMA((4 * PIECES,)),
+            pltpu.SemaphoreType.DMA((8 * PIECES,)),
             pltpu.SemaphoreType.DMA((chunks,)),
         ],
         compiler_params=pltpu.CompilerParams(vmem_limit_bytes=36 * 2**20),
         cost_estimate=pl.CostEstimate(flops=120 * math.prod(shape), bytes_accessed=12 * math.prod(shape), transcendentals=0),
-    )(*scalars, cells, amounts, start, mine, other, mine_last, other_last, near, far)
+    )(cells, amounts, start, mine, other, near, far)
 
 
 def halos(first, last):

time: 111 us -> 93.9 us (0.85)
  the two profiles are of different devices: /device:TPU:25 before, /device:TPU:6 now
where the time goes in v2:
time: 93.9 us; the launch traced here: 94 us
  starting transfers between devices  36.5 us (39%)
  Pallas kernels  32.7 us (35%)
  waiting for transfers between devices  18.8 us (20%)
  local copies, waits for them, and re-layouts  4.09 us (4%)
  between operations  1.78 us (2%)
    ppermute x12, starting transfers between devices, exchange(): arrived.append(lax.ppermute(send, 'rel', pairs))  21.1 us
    pallas_call x1, Pallas kernels, steps(): pl.pallas_call(steps_kernel, out_shape=jax.ShapeDtypeStruct(shape, jnp.fl...  17.1 us
    ppermute x12, waiting for transfers between devices, exchange(): arrived.append(lax.ppermute(send, 'rel', pairs))  14.9 us
    pallas_call x10, Pallas kernels, moved(): pl.pallas_call(kernel, out_shape=tuple((jax.ShapeDtypeStruct(shape, jnp.b...  14.8 us
    ppermute x2, starting transfers between devices, halos(): return (lax.ppermute(last, 'slab', up), lax.ppermute(first, 'slab', down))  7.94 us
    ppermute x2, starting transfers between devices, broadcast(): ends.append(lax.ppermute(edges, ('slab', 'rel'), pairs))  7.3 us
    ppermute x2, waiting for transfers between devices, other_core(): return lax.ppermute(value, 'rel', [(i, i ^ 1) for i in range(16)])  2.22 us
    unnamed x12, local copies, waits for them, and re-layouts  2.2 us
  transfers between devices with their start and end apart: 18, of which 8 were waited for; matrix products, arithmetic and copies ran while one was open for 2% of the time, Pallas kernels for 8%

profile of v2, /device:TPU:6, one launch (start us, length us, event | category | flops | bytes accessed | tf_op | source)
XLA Modules:
  0.0 94.0 jit_solution(13000672730100543621)
XLA Ops:
  0.0 3.0 %shard_map.64 = bf16[8,4,2,16,1024]{4,3,2,1,0:T(8,128)(2,1)S(1)} custom-call(s32[2]{0:T(128)} %ids_ref.15, bf16[2,4,4,64,1024]{4,3,2,1,0:T(8,128)(2,1)} %store_ref.1), custom_call_target="tpu_custom_call" | custom-call | bytes 2097152 | tf_op jit(solution)/shard_map/pallas_call | solution.py:228
  5.0 2.2 %collective-permute-done.3 = bf16[8,4,2,16,1024]{4,3,2,1,0:T(8,128)(2,1)S(1)} collective-permute-done((bf16[8,4,2,16,1024]{4,3,2,1,0:T(8,128)(2,1)S(1)}, bf16[8,4,2,16,1024]{4,3,2,1,0:T(8,128)(2,1)S(1)}, u32[]{:S(2)}, u32[]{:S(2)}) %collective-permute-start.3) | collective-permute-done | bytes 2097184 | tf_op jit(solution)/shard_map/ppermute | solution.py:254
  7.2 1.2 %conditional.1 = ((bf16[4,2,16,1024]{3,2,1,0:T(8,128)(2,1)S(1)}, bf16[4,2,16,1024]{3,2,1,0:T(8,128)(2,1)S(1)}, bf16[4,2,16,1024]{3,2,1,0:T(8,128)(2,1)S(1)}, bf16[8,4,2,16,1024]{4,3,2,1,0:T(8,128)(2,1)})) conditional(s32[]{:T(128)} %bitcast.3, (s32[2]{0:T(128)S(1)}, s32[960]{0:T(1024)S(1)}, bf16[2,4,4,64,1024]{4,3,2,1,0:T(8,128)(2,1)S(1)}, ...), branch_computations={%region_0.1_spmd, %region_1.2_spmd} | conditional | bytes 7340160 | solution.py:278
  7.2 1.2 %branch_0_fun.1 = (bf16[4,2,16,1024]{3,2,1,0:T(8,128)(2,1)S(1)}, bf16[4,2,16,1024]{3,2,1,0:T(8,128)(2,1)S(1)}, bf16[4,2,16,1024]{3,2,1,0:T(8,128)(2,1)S(1)}, bf16[8,4,2,16,1024]{4,3,2,1,0:T(8,128)(2,1)}) custom-call(s32[2]{0:T(128)S(1)} %get-tuple-element.21.ids_ref, s32[960]{0:T(1024)S(1)} %get-tuple-element.22.table_ref, ...), custom_call_target="tpu_custom_call" | custom-call | bytes 2097152 | tf_op jit(solution)/shard_map/cond/branch_0_fun/pallas_call | solution.py:228
  8.4 2.0 %collective-permute-start.4 = (bf16[4,2,16,1024]{3,2,1,0:T(8,128)(2,1)S(1)}, bf16[4,2,16,1024]{3,2,1,0:T(8,128)(2,1)S(1)}, u32[]{:S(2)}, u32[]{:S(2)}) collective-permute-start(bf16[4,2,16,1024]{3,2,1,0:T(8,128)(2,1)S(1)} %get-tuple-element.69), channel_id=1, source_target_pairs={{0,4},{1,5},{2,6},{3,7},{4,8},{5,9},{6,10},{7,11},{8,12},{9,13},{1... | collective-permute-start | bytes 786440 | tf_op jit(solution)/shard_map/ppermute | solution.py:249
  10.4 3.4 %collective-permute-start.5 = (bf16[4,2,16,1024]{3,2,1,0:T(8,128)(2,1)S(1)}, bf16[4,2,16,1024]{3,2,1,0:T(8,128)(2,1)S(1)}, u32[]{:S(2)}, u32[]{:S(2)}) collective-permute-start(bf16[4,2,16,1024]{3,2,1,0:T(8,128)(2,1)S(1)} %get-tuple-element.70), channel_id=1, source_target_pairs={{0,12},{1,13},{2,14},{3,15},{4,0},{5,1},{6,2},{7,3},{8,4},{9,5},{1... | collective-permute-start | bytes 786440 | tf_op jit(solution)/shard_map/ppermute | solution.py:249
  13.8 1.0 %collective-permute-start.6 = (bf16[4,2,16,1024]{3,2,1,0:T(8,128)(2,1)S(1)}, bf16[4,2,16,1024]{3,2,1,0:T(8,128)(2,1)S(1)}, u32[]{:S(2)}, u32[]{:S(2)}) collective-permute-start(bf16[4,2,16,1024]{3,2,1,0:T(8,128)(2,1)S(1)} %get-tuple-element.71), channel_id=1, source_target_pairs={{0,2},{1,3},{2,0},{3,1},{4,6},{5,7},{6,4},{7,5},{8,10},{9,11},{10,... | collective-permute-start | bytes 786440 | tf_op jit(solution)/shard_map/ppermute | solution.py:249
  14.8 1.3 %fusion.5 = (f32[4,4,4,1024]{3,2,1,0:T(4,128)S(1)}, f32[4,4,4,1024]{3,2,1,0:T(4,128)S(1)}) fusion(f32[4,4,64,1024]{3,2,1,0:T(8,128)} %field_hbm), kind=kLoop, calls=%fused_computation.18 | loop fusion | bytes 1048576 | tf_op jit(solution)/shard_map/slice | solution.py:281
  16.1 3.9 %collective-permute-done.4.rest_0_ = bf16[4,2,16,1024]{3,2,1,0:T(8,128)(2,1)S(1)} collective-permute-done((bf16[4,2,16,1024]{3,2,1,0:T(8,128)(2,1)S(1)}, bf16[4,2,16,1024]{3,2,1,0:T(8,128)(2,1)S(1)}, u32[]{:S(2)}, u32[]{:S(2)}) %collective-permute-start.4) | collective-permute-done | bytes 262176 | tf_op jit(solution)/shard_map/ppermute | solution.py:249
  20.1 3.0 %collective-permute-done.6.rest_2_ = bf16[4,2,16,1024]{3,2,1,0:T(8,128)(2,1)S(1)} collective-permute-done((bf16[4,2,16,1024]{3,2,1,0:T(8,128)(2,1)S(1)}, bf16[4,2,16,1024]{3,2,1,0:T(8,128)(2,1)S(1)}, u32[]{:S(2)}, u32[]{:S(2)}) %collective-permute-start.6) | collective-permute-done | bytes 262176 | tf_op jit(solution)/shard_map/ppermute | solution.py:249
  24.0 3.2 %collective-permute-start.10 = (bf16[4,2,16,1024]{3,2,1,0:T(8,128)(2,1)S(1)}, bf16[4,2,16,1024]{3,2,1,0:T(8,128)(2,1)S(1)}, u32[]{:S(2)}, u32[]{:S(2)}) collective-permute-start(bf16[4,2,16,1024]{3,2,1,0:T(8,128)(2,1)S(1)} %get-tuple-element.80), channel_id=1, source_target_pairs={{0,12},{1,13},{2,14},{3,15},{4,0},{5,1},{6,2},{7,3},{8,4},{9,5},{1... | collective-permute-start | bytes 786440 | tf_op jit(solution)/shard_map/ppermute | solution.py:249
  27.2 1.3 %collective-permute-start.11 = (bf16[4,2,16,1024]{3,2,1,0:T(8,128)(2,1)S(1)}, bf16[4,2,16,1024]{3,2,1,0:T(8,128)(2,1)S(1)}, u32[]{:S(2)}, u32[]{:S(2)}) collective-permute-start(bf16[4,2,16,1024]{3,2,1,0:T(8,128)(2,1)S(1)} %get-tuple-element.81), channel_id=1, source_target_pairs={{0,2},{1,3},{2,0},{3,1},{4,6},{5,7},{6,4},{7,5},{8,10},{9,11},{10,... | collective-permute-start | bytes 786440 | tf_op jit(solution)/shard_map/ppermute | solution.py:249
  28.5 3.5 %collective-permute-start.7 = (f32[4,4,4,1024]{3,2,1,0:T(4,128)S(1)}, f32[4,4,4,1024]{3,2,1,0:T(4,128)S(1)}, u32[]{:S(2)}, u32[]{:S(2)}) collective-permute-start(f32[4,4,4,1024]{3,2,1,0:T(4,128)S(1)} %get-tuple-element.77), channel_id=1, source_target_pairs={{0,16},{16,32},{32,48},{48,64},{64,80},{80,96},{96,112},{1,17},{17... | collective-permute-start | bytes 786440 | tf_op jit(solution)/shard_map/ppermute | solution.py:572
  32.0 4.5 %collective-permute-start.8 = (f32[4,4,4,1024]{3,2,1,0:T(4,128)S(1)}, f32[4,4,4,1024]{3,2,1,0:T(4,128)S(1)}, u32[]{:S(2)}, u32[]{:S(2)}) collective-permute-start(f32[4,4,4,1024]{3,2,1,0:T(4,128)S(1)} %get-tuple-element.78), channel_id=1, source_target_pairs={{16,0},{32,16},{48,32},{64,48},{80,64},{96,80},{112,96},{17,1},{33... | collective-permute-start | bytes 786440 | tf_op jit(solution)/shard_map/ppermute | solution.py:572
  36.5 1.4 %shard_map.66.rest_3_ = bf16[8,4,2,16,1024]{4,3,2,1,0:T(8,128)(2,1)} custom-call(s32[2]{0:T(128)S(1)} %copy-done.4, s32[960]{0:T(1024)S(1)} %copy-done.3, bf16[4,2,16,1024]{3,2,1,0:T(8,128)(2,1)S(1)} %collective-permute-done.4.rest_0_, bf16[4,2,16,1024]{3,2,1,0:T(8,128)(2,1)S(1)} %collective-permute-done.5.rest_1_, ...), custom_call_target="tpu_custom_call", output_to_operand_aliasing={{}: (5, {})} | custom-call | bytes 2097152 | tf_op jit(solution)/shard_map/pallas_call | solution.py:228
  38.8 3.2 %collective-permute-start.13 = (bf16[4,2,16,1024]{3,2,1,0:T(8,128)(2,1)S(1)}, bf16[4,2,16,1024]{3,2,1,0:T(8,128)(2,1)S(1)}, u32[]{:S(2)}, u32[]{:S(2)}) collective-permute-start(bf16[4,2,16,1024]{3,2,1,0:T(8,128)(2,1)S(1)} %get-tuple-element.90), channel_id=1, source_target_pairs={{0,12},{1,13},{2,14},{3,15},{4,0},{5,1},{6,2},{7,3},{8,4},{9,5},{1... | collective-permute-start | bytes 786440 | tf_op jit(solution)/shard_map/ppermute | solution.py:249
  42.1 2.2 %collective-permute-start.14 = (bf16[4,2,16,1024]{3,2,1,0:T(8,128)(2,1)S(1)}, bf16[4,2,16,1024]{3,2,1,0:T(8,128)(2,1)S(1)}, u32[]{:S(2)}, u32[]{:S(2)}) collective-permute-start(bf16[4,2,16,1024]{3,2,1,0:T(8,128)(2,1)S(1)} %get-tuple-element.91), channel_id=1, source_target_pairs={{0,2},{1,3},{2,0},{3,1},{4,6},{5,7},{6,4},{7,5},{8,10},{9,11},{10,... | collective-permute-start | bytes 786440 | tf_op jit(solution)/shard_map/ppermute | solution.py:249
  44.3 1.5 %shard_map.68.rest_3_ = bf16[8,4,2,16,1024]{4,3,2,1,0:T(8,128)(2,1)} custom-call(s32[2]{0:T(128)S(1)} %copy-done.4, s32[960]{0:T(1024)S(1)} %copy-done.3, bf16[4,2,16,1024]{3,2,1,0:T(8,128)(2,1)S(1)} %collective-permute-done.9.rest_0_, bf16[4,2,16,1024]{3,2,1,0:T(8,128)(2,1)S(1)} %collective-permute-done.10.rest_1_, ...), custom_call_target="tpu_custom_call", output_to_operand_aliasing={{}: (5, {})} | custom-call | bytes 2097152 | tf_op jit(solution)/shard_map/pallas_call | solution.py:228
  46.4 3.5 %collective-permute-done.14.rest_2_ = bf16[4,2,16,1024]{3,2,1,0:T(8,128)(2,1)S(1)} collective-permute-done((bf16[4,2,16,1024]{3,2,1,0:T(8,128)(2,1)S(1)}, bf16[4,2,16,1024]{3,2,1,0:T(8,128)(2,1)S(1)}, u32[]{:S(2)}, u32[]{:S(2)}) %collective-permute-start.14) | collective-permute-done | bytes 262176 | tf_op jit(solution)/shard_map/ppermute | solution.py:249
  49.9 1.7 %shard_map.69 = (bf16[4,2,16,1024]{3,2,1,0:T(8,128)(2,1)S(1)}, bf16[4,2,16,1024]{3,2,1,0:T(8,128)(2,1)S(1)}, bf16[4,2,16,1024]{3,2,1,0:T(8,128)(2,1)S(1)}) custom-call(s32[2]{0:T(128)S(1)} %copy-done.4, s32[960]{0:T(1024)S(1)} %copy-done.3, bf16[4,2,16,1024]{3,2,1,0:T(8,128)(2,1)S(1)} %collective-permute-done.12.rest_0_, ...), custom_call_target="tpu_custom_call" | custom-call | bytes 2097152 | tf_op jit(solution)/shard_map/pallas_call | solution.py:228
  51.8 3.2 %collective-permute-start.16 = (bf16[4,2,16,1024]{3,2,1,0:T(8,128)(2,1)S(1)}, bf16[4,2,16,1024]{3,2,1,0:T(8,128)(2,1)S(1)}, u32[]{:S(2)}, u32[]{:S(2)}) collective-permute-start(bf16[4,2,16,1024]{3,2,1,0:T(8,128)(2,1)S(1)} %get-tuple-element.99), channel_id=1, source_target_pairs={{0,12},{1,13},{2,14},{3,15},{4,0},{5,1},{6,2},{7,3},{8,4},{9,5},{1... | collective-permute-start | bytes 786440 | tf_op jit(solution)/shard_map/ppermute | solution.py:249
  55.0 1.3 %collective-permute-start.17 = (bf16[4,2,16,1024]{3,2,1,0:T(8,128)(2,1)S(1)}, bf16[4,2,16,1024]{3,2,1,0:T(8,128)(2,1)S(1)}, u32[]{:S(2)}, u32[]{:S(2)}) collective-permute-start(bf16[4,2,16,1024]{3,2,1,0:T(8,128)(2,1)S(1)} %get-tuple-element.100), channel_id=1, source_target_pairs={{0,2},{1,3},{2,0},{3,1},{4,6},{5,7},{6,4},{7,5},{8,10},{9,11},{10,... | collective-permute-start | bytes 786440 | tf_op jit(solution)/shard_map/ppermute | solution.py:249
  56.3 1.6 %shard_map.70.rest_3_.held_ref = bf16[8,4,2,16,1024]{4,3,2,1,0:T(8,128)(2,1)} custom-call(s32[2]{0:T(128)S(1)} %copy-done.4, s32[960]{0:T(1024)S(1)} %copy-done.3, bf16[4,2,16,1024]{3,2,1,0:T(8,128)(2,1)S(1)} %collective-permute-done.12.rest_0_, bf16[4,2,16,1024]{3,2,1,0:T(8,128)(2,1)S(1)} %collective-permute-done.13.rest_1_, ...), custom_call_target="tpu_custom_call", output_to_operand_aliasing={{}: (5, {})} | custom-call | bytes 2097152 | tf_op jit(solution)/shard_map/pallas_call | solution.py:228
  57.9 1.5 %collective-permute-done.15.rest_0_ = bf16[4,2,16,1024]{3,2,1,0:T(8,128)(2,1)S(1)} collective-permute-done((bf16[4,2,16,1024]{3,2,1,0:T(8,128)(2,1)S(1)}, bf16[4,2,16,1024]{3,2,1,0:T(8,128)(2,1)S(1)}, u32[]{:S(2)}, u32[]{:S(2)}) %collective-permute-start.15) | collective-permute-done | bytes 262176 | tf_op jit(solution)/shard_map/ppermute | solution.py:249
  59.3 1.2 %shard_map.73 = bf16[4,16,1024]{2,1,0:T(8,128)(2,1)S(1)} custom-call(bf16[8,4,2,16,1024]{4,3,2,1,0:T(8,128)(2,1)} %shard_map.70.rest_3_.held_ref), custom_call_target="tpu_custom_call" | custom-call | bytes 2097152 | tf_op jit(solution)/shard_map/pallas_call | solution.py:228
  60.6 2.3 %collective-permute-done.17.rest_2_ = bf16[4,2,16,1024]{3,2,1,0:T(8,128)(2,1)S(1)} collective-permute-done((bf16[4,2,16,1024]{3,2,1,0:T(8,128)(2,1)S(1)}, bf16[4,2,16,1024]{3,2,1,0:T(8,128)(2,1)S(1)}, u32[]{:S(2)}, u32[]{:S(2)}) %collective-permute-start.17) | collective-permute-done | bytes 262176 | tf_op jit(solution)/shard_map/ppermute | solution.py:249
  62.9 1.6 %shard_map.71.mine_ref = bf16[8,4,2,16,1024]{4,3,2,1,0:T(8,128)(2,1)} custom-call(s32[2]{0:T(128)S(1)} %copy-done.4, s32[960]{0:T(1024)S(1)} %copy-done.3, bf16[4,2,16,1024]{3,2,1,0:T(8,128)(2,1)S(1)} %collective-permute-done.15.rest_0_, bf16[4,2,16,1024]{3,2,1,0:T(8,128)(2,1)S(1)} %collective-permute-done.16.rest_1_, ...), custom_call_target="tpu_custom_call", output_to_operand_aliasing={{}: (5, {})} | custom-call | bytes 2097152 | tf_op jit(solution)/shard_map/pallas_call | solution.py:228
  64.6 5.2 %collective-permute-start.20 = (bf16[4,16,1024]{2,1,0:T(8,128)(2,1)S(1)}, bf16[4,16,1024]{2,1,0:T(8,128)(2,1)S(1)}, u32[]{:S(2)}, u32[]{:S(2)}) collective-permute-start(bf16[4,16,1024]{2,1,0:T(8,128)(2,1)S(1)} %shard_map.73), channel_id=1, source_target_pairs={{1,16},{3,18},{5,20},{7,22},{9,24},{11,26},{13,28},{15,30},{16,1},... | collective-permute-start | bytes 393224 | tf_op jit(solution)/shard_map/ppermute | solution.py:314
  69.8 2.1 %collective-permute-start.19 = (bf16[4,16,1024]{2,1,0:T(8,128)(2,1)S(1)}, bf16[4,16,1024]{2,1,0:T(8,128)(2,1)S(1)}, u32[]{:S(2)}, u32[]{:S(2)}) collective-permute-start(bf16[4,16,1024]{2,1,0:T(8,128)(2,1)S(1)} %shard_map.73), channel_id=1, source_target_pairs={{1,17},{3,19},{5,21},{7,23},{9,25},{11,27},{13,29},{15,31},{16,0},... | collective-permute-start | bytes 393224 | tf_op jit(solution)/shard_map/ppermute | solution.py:314
  72.0 2.2 %copy-done = f32[4,4,64,1024]{3,2,1,0:T(8,128)S(1)} copy-done((f32[4,4,64,1024]{3,2,1,0:T(8,128)S(1)}, f32[4,4,64,1024]{3,2,1,0:T(8,128)}, u32[]{:S(2)}) %copy-start) | copy-done | bytes 4194328
  75.0 1.7 %collective-permute-done.19.rest_0_ = bf16[4,16,1024]{2,1,0:T(8,128)(2,1)S(1)} collective-permute-done((bf16[4,16,1024]{2,1,0:T(8,128)(2,1)S(1)}, bf16[4,16,1024]{2,1,0:T(8,128)(2,1)S(1)}, u32[]{:S(2)}, u32[]{:S(2)}) %collective-permute-start.19) | collective-permute-done | bytes 131104 | tf_op jit(solution)/shard_map/ppermute | solution.py:314
  76.7 17.1 %shard_map.74 = f32[4,4,64,1024]{3,2,1,0:T(8,128)} custom-call(s32[3,4]{1,0:T(4,128)S(1)} %pad_add_fusion.cells_ref, f32[4]{0:T(128)S(1)} %copy-done.1, f32[4,4,8,96,128]{4,3,2,1,0:T(8,128)S(1)} %shard_map.72.first, bf16[8,4,2,16,1024]{4,3,2,1,0:T(8,128)(2,1)} %shard_map.71.mine_ref, bf16[8,4,2,16,1024]{4,3,2,1,0:T(8,128)(2,1)S(1)} %collective-permute-done.18.other_ref, ...), custom_call_target="tpu_custom_call" | custom-call | flops 125829120 | bytes 12582912 | tf_op jit(solution)/shard_map/pallas_call | solution.py:549
  (33 shorter events, 4.1 us)
Async XLA Ops:
  0.0 7.2 %copy-start.3 = (s32[960]{0:T(1024)S(1)}, s32[960]{0:T(1024)}, u32[]{:S(2)}) copy-start(s32[960]{0:T(1024)} %constant.69.table_ref) | copy-start | bytes 11524
  0.0 3.1 %copy-start.4 = (s32[2]{0:T(128)S(1)}, s32[2]{0:T(128)}, u32[]{:S(2)}) copy-start(s32[2]{0:T(128)} %ids_ref.15) | copy-start | bytes 28
  0.0 7.2 %copy-start.2 = (bf16[2,4,4,64,1024]{4,3,2,1,0:T(8,128)(2,1)S(1)}, bf16[2,4,4,64,1024]{4,3,2,1,0:T(8,128)(2,1)}, u32[]{:S(2)}) copy-start(bf16[2,4,4,64,1024]{4,3,2,1,0:T(8,128)(2,1)} %store_ref.1) | copy-start | bytes 12582916
  3.0 4.2 %collective-permute-start.3 = (bf16[8,4,2,16,1024]{4,3,2,1,0:T(8,128)(2,1)S(1)}, bf16[8,4,2,16,1024]{4,3,2,1,0:T(8,128)(2,1)S(1)}, u32[]{:S(2)}, u32[]{:S(2)}) collective-permute-start(bf16[8,4,2,16,1024]{4,3,2,1,0:T(8,128)(2,1)S(1)} %shard_map.64), channel_id=1, source_target_pairs={{0,1},{1,0},{2,3},{3,2},{4,5},{5,4},{6,7},{7,6},{8,9},{9,8},{10,11... | collective-permute-start | bytes 6291464 | tf_op jit(solution)/shard_map/ppermute | solution.py:254
  8.4 11.6 %collective-permute-start.4 = (bf16[4,2,16,1024]{3,2,1,0:T(8,128)(2,1)S(1)}, bf16[4,2,16,1024]{3,2,1,0:T(8,128)(2,1)S(1)}, u32[]{:S(2)}, u32[]{:S(2)}) collective-permute-start(bf16[4,2,16,1024]{3,2,1,0:T(8,128)(2,1)S(1)} %get-tuple-element.69), channel_id=1, source_target_pairs={{0,4},{1,5},{2,6},{3,7},{4,8},{5,9},{6,10},{7,11},{8,12},{9,13},{1... | collective-permute-start | bytes 786440 | tf_op jit(solution)/shard_map/ppermute | solution.py:249
  10.4 9.7 %collective-permute-start.5 = (bf16[4,2,16,1024]{3,2,1,0:T(8,128)(2,1)S(1)}, bf16[4,2,16,1024]{3,2,1,0:T(8,128)(2,1)S(1)}, u32[]{:S(2)}, u32[]{:S(2)}) collective-permute-start(bf16[4,2,16,1024]{3,2,1,0:T(8,128)(2,1)S(1)} %get-tuple-element.70), channel_id=1, source_target_pairs={{0,12},{1,13},{2,14},{3,15},{4,0},{5,1},{6,2},{7,3},{8,4},{9,5},{1... | collective-permute-start | bytes 786440 | tf_op jit(solution)/shard_map/ppermute | solution.py:249
  13.8 9.3 %collective-permute-start.6 = (bf16[4,2,16,1024]{3,2,1,0:T(8,128)(2,1)S(1)}, bf16[4,2,16,1024]{3,2,1,0:T(8,128)(2,1)S(1)}, u32[]{:S(2)}, u32[]{:S(2)}) collective-permute-start(bf16[4,2,16,1024]{3,2,1,0:T(8,128)(2,1)S(1)} %get-tuple-element.71), channel_id=1, source_target_pairs={{0,2},{1,3},{2,0},{3,1},{4,6},{5,7},{6,4},{7,5},{8,10},{9,11},{10,... | collective-permute-start | bytes 786440 | tf_op jit(solution)/shard_map/ppermute | solution.py:249
  23.9 14.0 %collective-permute-start.9 = (bf16[4,2,16,1024]{3,2,1,0:T(8,128)(2,1)S(1)}, bf16[4,2,16,1024]{3,2,1,0:T(8,128)(2,1)S(1)}, u32[]{:S(2)}, u32[]{:S(2)}) collective-permute-start(bf16[4,2,16,1024]{3,2,1,0:T(8,128)(2,1)S(1)} %get-tuple-element.79), channel_id=1, source_target_pairs={{0,4},{1,5},{2,6},{3,7},{4,8},{5,9},{6,10},{7,11},{8,12},{9,13},{1... | collective-permute-start | bytes 786440 | tf_op jit(solution)/shard_map/ppermute | solution.py:249
  24.0 13.9 %collective-permute-start.10 = (bf16[4,2,16,1024]{3,2,1,0:T(8,128)(2,1)S(1)}, bf16[4,2,16,1024]{3,2,1,0:T(8,128)(2,1)S(1)}, u32[]{:S(2)}, u32[]{:S(2)}) collective-permute-start(bf16[4,2,16,1024]{3,2,1,0:T(8,128)(2,1)S(1)} %get-tuple-element.80), channel_id=1, source_target_pairs={{0,12},{1,13},{2,14},{3,15},{4,0},{5,1},{6,2},{7,3},{8,4},{9,5},{1... | collective-permute-start | bytes 786440 | tf_op jit(solution)/shard_map/ppermute | solution.py:249
  27.2 10.7 %collective-permute-start.11 = (bf16[4,2,16,1024]{3,2,1,0:T(8,128)(2,1)S(1)}, bf16[4,2,16,1024]{3,2,1,0:T(8,128)(2,1)S(1)}, u32[]{:S(2)}, u32[]{:S(2)}) collective-permute-start(bf16[4,2,16,1024]{3,2,1,0:T(8,128)(2,1)S(1)} %get-tuple-element.81), channel_id=1, source_target_pairs={{0,2},{1,3},{2,0},{3,1},{4,6},{5,7},{6,4},{7,5},{8,10},{9,11},{10,... | collective-permute-start | bytes 786440 | tf_op jit(solution)/shard_map/ppermute | solution.py:249
  28.5 17.2 %collective-permute-start.7 = (f32[4,4,4,1024]{3,2,1,0:T(4,128)S(1)}, f32[4,4,4,1024]{3,2,1,0:T(4,128)S(1)}, u32[]{:S(2)}, u32[]{:S(2)}) collective-permute-start(f32[4,4,4,1024]{3,2,1,0:T(4,128)S(1)} %get-tuple-element.77), channel_id=1, source_target_pairs={{0,16},{16,32},{32,48},{48,64},{64,80},{80,96},{96,112},{1,17},{17... | collective-permute-start | bytes 786440 | tf_op jit(solution)/shard_map/ppermute | solution.py:572
  32.0 13.8 %collective-permute-start.8 = (f32[4,4,4,1024]{3,2,1,0:T(4,128)S(1)}, f32[4,4,4,1024]{3,2,1,0:T(4,128)S(1)}, u32[]{:S(2)}, u32[]{:S(2)}) collective-permute-start(f32[4,4,4,1024]{3,2,1,0:T(4,128)S(1)} %get-tuple-element.78), channel_id=1, source_target_pairs={{16,0},{32,16},{48,32},{64,48},{80,64},{96,80},{112,96},{17,1},{33... | collective-permute-start | bytes 786440 | tf_op jit(solution)/shard_map/ppermute | solution.py:572
  38.8 7.7 %collective-permute-start.12 = (bf16[4,2,16,1024]{3,2,1,0:T(8,128)(2,1)S(1)}, bf16[4,2,16,1024]{3,2,1,0:T(8,128)(2,1)S(1)}, u32[]{:S(2)}, u32[]{:S(2)}) collective-permute-start(bf16[4,2,16,1024]{3,2,1,0:T(8,128)(2,1)S(1)} %get-tuple-element.86), channel_id=1, source_target_pairs={{0,4},{1,5},{2,6},{3,7},{4,8},{5,9},{6,10},{7,11},{8,12},{9,13},{1... | collective-permute-start | bytes 786440 | tf_op jit(solution)/shard_map/ppermute | solution.py:249
  38.8 7.6 %collective-permute-start.13 = (bf16[4,2,16,1024]{3,2,1,0:T(8,128)(2,1)S(1)}, bf16[4,2,16,1024]{3,2,1,0:T(8,128)(2,1)S(1)}, u32[]{:S(2)}, u32[]{:S(2)}) collective-permute-start(bf16[4,2,16,1024]{3,2,1,0:T(8,128)(2,1)S(1)} %get-tuple-element.90), channel_id=1, source_target_pairs={{0,12},{1,13},{2,14},{3,15},{4,0},{5,1},{6,2},{7,3},{8,4},{9,5},{1... | collective-permute-start | bytes 786440 | tf_op jit(solution)/shard_map/ppermute | solution.py:249
  42.1 7.9 %collective-permute-start.14 = (bf16[4,2,16,1024]{3,2,1,0:T(8,128)(2,1)S(1)}, bf16[4,2,16,1024]{3,2,1,0:T(8,128)(2,1)S(1)}, u32[]{:S(2)}, u32[]{:S(2)}) collective-permute-start(bf16[4,2,16,1024]{3,2,1,0:T(8,128)(2,1)S(1)} %get-tuple-element.91), channel_id=1, source_target_pairs={{0,2},{1,3},{2,0},{3,1},{4,6},{5,7},{6,4},{7,5},{8,10},{9,11},{10,... | collective-permute-start | bytes 786440 | tf_op jit(solution)/shard_map/ppermute | solution.py:249
  51.7 7.7 %collective-permute-start.15 = (bf16[4,2,16,1024]{3,2,1,0:T(8,128)(2,1)S(1)}, bf16[4,2,16,1024]{3,2,1,0:T(8,128)(2,1)S(1)}, u32[]{:S(2)}, u32[]{:S(2)}) collective-permute-start(bf16[4,2,16,1024]{3,2,1,0:T(8,128)(2,1)S(1)} %get-tuple-element.97), channel_id=1, source_target_pairs={{0,4},{1,5},{2,6},{3,7},{4,8},{5,9},{6,10},{7,11},{8,12},{9,13},{1... | collective-permute-start | bytes 786440 | tf_op jit(solution)/shard_map/ppermute | solution.py:249
  51.8 8.8 %collective-permute-start.16 = (bf16[4,2,16,1024]{3,2,1,0:T(8,128)(2,1)S(1)}, bf16[4,2,16,1024]{3,2,1,0:T(8,128)(2,1)S(1)}, u32[]{:S(2)}, u32[]{:S(2)}) collective-permute-start(bf16[4,2,16,1024]{3,2,1,0:T(8,128)(2,1)S(1)} %get-tuple-element.99), channel_id=1, source_target_pairs={{0,12},{1,13},{2,14},{3,15},{4,0},{5,1},{6,2},{7,3},{8,4},{9,5},{1... | collective-permute-start | bytes 786440 | tf_op jit(solution)/shard_map/ppermute | solution.py:249
  55.0 7.9 %collective-permute-start.17 = (bf16[4,2,16,1024]{3,2,1,0:T(8,128)(2,1)S(1)}, bf16[4,2,16,1024]{3,2,1,0:T(8,128)(2,1)S(1)}, u32[]{:S(2)}, u32[]{:S(2)}) collective-permute-start(bf16[4,2,16,1024]{3,2,1,0:T(8,128)(2,1)S(1)} %get-tuple-element.100), channel_id=1, source_target_pairs={{0,2},{1,3},{2,0},{3,1},{4,6},{5,7},{6,4},{7,5},{8,10},{9,11},{10,... | collective-permute-start | bytes 786440 | tf_op jit(solution)/shard_map/ppermute | solution.py:249
  60.6 11.4 %copy-start.5 = (s32[4]{0:T(128)S(1)}, s32[4]{0:T(128)}, u32[]{:S(2)}) copy-start(s32[4]{0:T(128)} %param.10) | copy-start | bytes 52
  64.5 12.2 %collective-permute-start.18 = (bf16[8,4,2,16,1024]{4,3,2,1,0:T(8,128)(2,1)}, bf16[8,4,2,16,1024]{4,3,2,1,0:T(8,128)(2,1)S(1)}, u32[]{:S(2)}, u32[]{:S(2)}) collective-permute-start(bf16[8,4,2,16,1024]{4,3,2,1,0:T(8,128)(2,1)} %shard_map.71.mine_ref), channel_id=1, source_target_pairs={{0,1},{1,0},{2,3},{3,2},{4,5},{5,4},{6,7},{7,6},{8,9},{9,8},{10,11... | collective-permute-start | bytes 6291464 | tf_op jit(solution)/shard_map/ppermute | solution.py:254
  64.6 10.4 %collective-permute-start.20 = (bf16[4,16,1024]{2,1,0:T(8,128)(2,1)S(1)}, bf16[4,16,1024]{2,1,0:T(8,128)(2,1)S(1)}, u32[]{:S(2)}, u32[]{:S(2)}) collective-permute-start(bf16[4,16,1024]{2,1,0:T(8,128)(2,1)S(1)} %shard_map.73), channel_id=1, source_target_pairs={{1,16},{3,18},{5,20},{7,22},{9,24},{11,26},{13,28},{15,30},{16,1},... | collective-permute-start | bytes 393224 | tf_op jit(solution)/shard_map/ppermute | solution.py:314
  69.8 6.9 %collective-permute-start.19 = (bf16[4,16,1024]{2,1,0:T(8,128)(2,1)S(1)}, bf16[4,16,1024]{2,1,0:T(8,128)(2,1)S(1)}, u32[]{:S(2)}, u32[]{:S(2)}) collective-permute-start(bf16[4,16,1024]{2,1,0:T(8,128)(2,1)S(1)} %shard_map.73), channel_id=1, source_target_pairs={{1,17},{3,19},{5,21},{7,23},{9,25},{11,27},{13,29},{15,31},{16,0},... | collective-permute-start | bytes 393224 | tf_op jit(solution)/shard_map/ppermute | solution.py:314
  72.0 2.2 %copy-start = (f32[4,4,64,1024]{3,2,1,0:T(8,128)S(1)}, f32[4,4,64,1024]{3,2,1,0:T(8,128)}, u32[]{:S(2)}) copy-start(f32[4,4,64,1024]{3,2,1,0:T(8,128)} %field_hbm) | copy-start | bytes 12582916
  74.2 2.5 %copy-start.1 = (f32[4]{0:T(128)S(1)}, f32[4]{0:T(128)}, u32[]{:S(2)}) copy-start(f32[4]{0:T(128)} %amount_ref.1) | copy-start | bytes 52

commit v3 on v2

--- a/solution.py
+++ b/solution.py
@@ -170,36 +170,51 @@
 
 
 def forward_kernel(phase, ids_ref, table_ref, *rest):
-    arrived, held_ref, outs, stage, sems = rest[:LINKS], rest[LINKS], rest[LINKS + 1 : -2], rest[-2], rest[-1]
+    arrived, older, outs, stage, sems = rest[:LINKS], rest[LINKS : 2 * LINKS], rest[2 * LINKS : -2], rest[-2], rest[-1]
     sent, got = plan(ids_ref, table_ref)
     loads, stores = [], []
     for link in range(LINKS):
         slot = sent(phase + 1, link)
         loads.extend(
             (condition, source, stage.at[link], sems.at[link])
-            for condition, source in wherever(slot, phase, got, arrived, held_ref)
+            for condition, source in wherever(slot, phase, got, arrived, older[link])
         )
         stores.append((slot >= 0, stage.at[link], outs[link], sems.at[link]))
     run_staged(loads, stores)
 
 
-def keep_kernel(phase, ids_ref, table_ref, *rest):
-    arrived, held_ref, stage, sems = rest[:LINKS], *rest[LINKS + 1 :]
-    _, got = plan(ids_ref, table_ref)
-    ways = range(LINKS)
-    run_staged(
-        [(got(phase, way) >= 0, arrived[way], stage.at[way], sems.at[way]) for way in ways],
-        [(got(phase, way) >= 0, stage.at[way], held_ref.at[jnp.maximum(got(phase, way), 0)], sems.at[way]) for way in ways],
-    )
-
-
-def wherever(slot, phase, got, arrived, held_ref):
+def keep_kernel(phase, brought, lays, ids_ref, table_ref, *rest):
+    arrived, held_in, held_ref, outs = rest[:brought], rest[brought], rest[brought + 1], rest[brought + 2 : -2]
+    stage, sems = rest[-2:]
+    sent, got = plan(ids_ref, table_ref)
+    loads, stores = [], []
+    for way in range(brought):
+        slot = got(phase, way)
+        loads.append((slot >= 0, arrived[way], stage.at[way], sems.at[way]))
+        stores.append((slot >= 0, stage.at[way], held_ref.at[jnp.maximum(slot, 0)], sems.at[way]))
+    for link in range(LINKS * lays):
+        slot = sent(phase + 2, link)
+        at = LINKS + link
+        older = slot >= 0
+        for way in range(LINKS):
+            older = jnp.logical_and(older, got(phase + 1, way) != slot)
+        before = older
+        for way in range(brought):
+            now = got(phase, way) == slot
+            stores.append((jnp.logical_and(older, now), stage.at[way], outs[link], sems.at[at]))
+            before = jnp.logical_and(before, jnp.logical_not(now))
+        loads.append((before, held_in.at[jnp.maximum(slot, 0)], stage.at[at], sems.at[at]))
+        stores.append((before, stage.at[at], outs[link], sems.at[at]))
+    run_staged(loads, stores)
+
+
+def wherever(slot, phase, got, arrived, older_ref):
     older = slot >= 0
     places = []
     for way in range(LINKS):
         places.append((jnp.logical_and(slot >= 0, got(phase, way) == slot), arrived[way]))
         older = jnp.logical_and(older, got(phase, way) != slot)
-    return [*places, (older, held_ref.at[jnp.maximum(slot, 0)])]
+    return [*places, (older, older_ref)]
 
 
 def edge_kernel(held_ref, out_ref, stage, stage_kd, rows, sems):
@@ -254,55 +269,7 @@
     return lax.ppermute(value, "rel", [(i, i ^ 1) for i in range(16)])
 
 
-def broadcast(wind_store, ids, field):
-    table = jnp.asarray(SCHEDULES, jnp.int32).reshape(-1)
-    every = (2 * PIECES,) + PIECE
-    dma = pltpu.SemaphoreType.DMA
-    sent = [PIECE] * LINKS
-
-    def stage(slots):
-        return pltpu.VMEM((slots,) + PIECE, jnp.bfloat16)
-
-    (shared,) = moved(share_kernel, (ids,), [wind_store], [every], [stage(2 * PIECES), dma((4 * PIECES,))])
-    shared = other_core(shared)
-
-    def begin(phase, keeps, wind_store, shared, arrived):
-        return moved(
-            functools.partial(first_kernel, phase, len(arrived), keeps), (ids, table), [wind_store, shared, *arrived],
-            sent + [every] * keeps, [stage(2 * PIECES + LINKS), dma((4 * PIECES + LINKS,))],
-        )
-
-    def one_chip(wind_store, shared):
-        return begin(1, True, wind_store, shared, exchange(begin(0, False, wind_store, shared, [])))
-
-    *sends, held = lax.cond(
-        ids[0] >> 2 == ids[1] >> 2, one_chip, lambda store, shared: begin(1, True, store, shared, []), wind_store, shared
-    )
-    ends = (field[:, :, :4], field[:, :, -4:])
-    for phase in range(1, PHASES + 1):
-        if phase == 2:
-            *ends, sends[0] = lax.optimization_barrier((*ends, sends[0]))
-            west, east = halos(*ends)
-        arrived = exchange(sends)
-        if phase == 3:
-            west, east, arrived[0] = lax.optimization_barrier((west, east, arrived[0]))
-        if phase == PHASES:
-            held, arrived[0] = lax.optimization_barrier((held, arrived[0]))
-            (edges,) = moved(
-                edge_kernel, (), [held], [(4, 16, 1024)],
-                [stage(2), pltpu.VMEM((4, 16, 1024), jnp.bfloat16), pltpu.VMEM((4, 16, 1024), jnp.float32), dma((3,))],
-                vmem_outs=1,
-            )
-        else:
-            sends = moved(
-                functools.partial(forward_kernel, phase), (ids, table), [*arrived, held], sent, [stage(LINKS), dma((LINKS,))]
-            )
-            *sends, held = lax.optimization_barrier((*sends, held))
-        (held,) = moved(
-            functools.partial(keep_kernel, phase), (ids, table), [*arrived, held], [every], [stage(LINKS), dma((LINKS,))],
-            {2 + LINKS: 0},
-        )
-    other = other_core(held)
+def swap_ends(edges):
     ends = []
     for flip in range(2):
         pairs = []
@@ -312,8 +279,66 @@
                 if 0 <= to < 8:
                     pairs.append((slab * 16 + rel, to * 16 + (rel ^ flip)))
         ends.append(lax.ppermute(edges, ("slab", "rel"), pairs))
+    return ends
+
+
+def broadcast(wind_store, ids, field):
+    table = jnp.asarray(SCHEDULES, jnp.int32).reshape(-1)
+    every = (2 * PIECES,) + PIECE
+    dma = pltpu.SemaphoreType.DMA
+    sent = [PIECE] * LINKS
+
+    def stage(slots):
+        return pltpu.VMEM((slots,) + PIECE, jnp.bfloat16)
+
+    (shared,) = moved(share_kernel, (ids,), [wind_store], [every], [stage(2 * PIECES), dma((4 * PIECES,))])
+    shared = other_core(shared)
+
+    def begin(phase, keeps, wind_store, shared, arrived):
+        return moved(
+            functools.partial(first_kernel, phase, len(arrived), keeps), (ids, table), [wind_store, shared, *arrived],
+            sent + [every] * keeps, [stage(2 * PIECES + LINKS), dma((4 * PIECES + LINKS,))],
+        )
+
+    def one_chip(wind_store, shared):
+        return begin(1, True, wind_store, shared, exchange(begin(0, False, wind_store, shared, [])))
+
+    *sends, held = lax.cond(
+        ids[0] >> 2 == ids[1] >> 2, one_chip, lambda store, shared: begin(1, True, store, shared, []), wind_store, shared
+    )
+    ends = (field[:, :, :4], field[:, :, -4:])
+    def keep(phase, arrived, held, lays):
+        held, *older = moved(
+            functools.partial(keep_kernel, phase, len(arrived), lays), (ids, table), [*arrived, held], [every] + sent * lays,
+            [stage(2 * LINKS), dma((2 * LINKS,))], {2 + len(arrived): 0},
+        )
+        return held, older
+
+    came = []
+    for phase in range(1, PHASES + 1):
+        if phase == 2:
+            *ends, held = lax.optimization_barrier((*ends, held))
+            west, east = halos(*ends)
+        *sends, held = lax.optimization_barrier((*sends, held))
+        held, older = keep(phase - 1, came, held, phase < PHASES)
+        arrived = exchange(sends)
+        if phase == 3:
+            west, east, arrived[0] = lax.optimization_barrier((west, east, arrived[0]))
+        if phase < PHASES:
+            sends = moved(
+                functools.partial(forward_kernel, phase), (ids, table), [*arrived, *older], sent, [stage(LINKS), dma((LINKS,))]
+            )
+            came = arrived
+    (edges,) = moved(
+        edge_kernel, (), [held], [(4, 16, 1024)],
+        [stage(2), pltpu.VMEM((4, 16, 1024), jnp.bfloat16), pltpu.VMEM((4, 16, 1024), jnp.float32), dma((3,))],
+        vmem_outs=1,
+    )
+    ends = swap_ends(edges)
+    *ends, arrived[1] = lax.optimization_barrier((*ends, arrived[1]))
+    held, _ = keep(PHASES, arrived, held, False)
     after, west, east, held = lax.optimization_barrier((field, west, east, held))
-    return lay_out(after, west, east), held, other, *ends
+    return lay_out(after, west, east), held, other_core(held), *ends
 
 
 def shifted_y(here, left, right, lane):

time: 93.9 us -> 92.9 us (0.989)
  the two profiles are of different devices: /device:TPU:6 before, /device:TPU:25 now
where the time goes in v3:
time: 92.9 us; the launch traced here: 92.5 us
  starting transfers between devices  37.9 us (41%)
  Pallas kernels  32.8 us (35%)
  waiting for transfers between devices  16 us (17%)
  local copies, waits for them, and re-layouts  4.08 us (4%)
  between operations  1.67 us (2%)
    ppermute x12, starting transfers between devices, exchange(): arrived.append(lax.ppermute(send, 'rel', pairs))  17.2 us
    pallas_call x1, Pallas kernels, steps(): pl.pallas_call(steps_kernel, out_shape=jax.ShapeDtypeStruct(shape, jnp.fl...  17.1 us
    pallas_call x11, Pallas kernels, moved(): pl.pallas_call(kernel, out_shape=tuple((jax.ShapeDtypeStruct(shape, jnp.b...  14.9 us
    ppermute x2, starting transfers between devices, swap_ends(): ends.append(lax.ppermute(edges, ('slab', 'rel'), pairs))  11.6 us
    ppermute x12, waiting for transfers between devices, exchange(): arrived.append(lax.ppermute(send, 'rel', pairs))  9.35 us
    ppermute x2, starting transfers between devices, halos(): return (lax.ppermute(last, 'slab', up), lax.ppermute(first, 'slab', down))  5.27 us
    ppermute x2, starting transfers between devices, other_core(): return lax.ppermute(value, 'rel', [(i, i ^ 1) for i in range(16)])  3.84 us
    ppermute x2, waiting for transfers between devices, swap_ends(): ends.append(lax.ppermute(edges, ('slab', 'rel'), pairs))  3.78 us
  transfers between devices with their start and end apart: 18, of which 8 were waited for; matrix products, arithmetic and copies ran while one was open for 2% of the time, Pallas kernels for 9%

profile of v3, /device:TPU:25, one launch (start us, length us, event | category | flops | bytes accessed | tf_op | source)
XLA Modules:
  0.0 92.5 jit_solution(3971528854708009577)
XLA Ops:
  0.0 3.0 %shard_map.64 = bf16[8,4,2,16,1024]{4,3,2,1,0:T(8,128)(2,1)S(1)} custom-call(s32[2]{0:T(128)} %ids_ref.17, bf16[2,4,4,64,1024]{4,3,2,1,0:T(8,128)(2,1)} %store_ref.1), custom_call_target="tpu_custom_call" | custom-call | bytes 2097152 | tf_op jit(solution)/shard_map/pallas_call | solution.py:243
  5.6 1.9 %collective-permute-done.3 = bf16[8,4,2,16,1024]{4,3,2,1,0:T(8,128)(2,1)S(1)} collective-permute-done((bf16[8,4,2,16,1024]{4,3,2,1,0:T(8,128)(2,1)S(1)}, bf16[8,4,2,16,1024]{4,3,2,1,0:T(8,128)(2,1)S(1)}, u32[]{:S(2)}, u32[]{:S(2)}) %collective-permute-start.3) | collective-permute-done | bytes 2097184 | tf_op jit(solution)/shard_map/ppermute | solution.py:269
  7.5 1.2 %conditional.1 = ((bf16[4,2,16,1024]{3,2,1,0:T(8,128)(2,1)S(1)}, bf16[4,2,16,1024]{3,2,1,0:T(8,128)(2,1)S(1)}, bf16[4,2,16,1024]{3,2,1,0:T(8,128)(2,1)S(1)}, bf16[8,4,2,16,1024]{4,3,2,1,0:T(8,128)(2,1)})) conditional(s32[]{:T(128)} %bitcast.3, (s32[2]{0:T(128)S(1)}, s32[960]{0:T(1024)S(1)}, bf16[2,4,4,64,1024]{4,3,2,1,0:T(8,128)(2,1)S(1)}, ...), branch_computations={%region_0.1_spmd, %region_1.2_spmd} | conditional | bytes 7340160 | solution.py:306
  7.5 1.2 %branch_0_fun.1 = (bf16[4,2,16,1024]{3,2,1,0:T(8,128)(2,1)S(1)}, bf16[4,2,16,1024]{3,2,1,0:T(8,128)(2,1)S(1)}, bf16[4,2,16,1024]{3,2,1,0:T(8,128)(2,1)S(1)}, bf16[8,4,2,16,1024]{4,3,2,1,0:T(8,128)(2,1)}) custom-call(s32[2]{0:T(128)S(1)} %get-tuple-element.21.ids_ref, s32[960]{0:T(1024)S(1)} %get-tuple-element.22.table_ref, ...), custom_call_target="tpu_custom_call" | custom-call | bytes 2097152 | tf_op jit(solution)/shard_map/cond/branch_0_fun/pallas_call | solution.py:243
  8.7 1.7 %collective-permute-start.6 = (bf16[4,2,16,1024]{3,2,1,0:T(8,128)(2,1)S(1)}, bf16[4,2,16,1024]{3,2,1,0:T(8,128)(2,1)S(1)}, u32[]{:S(2)}, u32[]{:S(2)}) collective-permute-start(bf16[4,2,16,1024]{3,2,1,0:T(8,128)(2,1)S(1)} %get-tuple-element.86), channel_id=1, source_target_pairs={{0,4},{1,5},{2,6},{3,7},{4,8},{5,9},{6,10},{7,11},{8,12},{9,13},{1... | collective-permute-start | bytes 786440 | tf_op jit(solution)/shard_map/ppermute | solution.py:264
  10.4 3.0 %collective-permute-start.7 = (bf16[4,2,16,1024]{3,2,1,0:T(8,128)(2,1)S(1)}, bf16[4,2,16,1024]{3,2,1,0:T(8,128)(2,1)S(1)}, u32[]{:S(2)}, u32[]{:S(2)}) collective-permute-start(bf16[4,2,16,1024]{3,2,1,0:T(8,128)(2,1)S(1)} %get-tuple-element.87), channel_id=1, source_target_pairs={{0,12},{1,13},{2,14},{3,15},{4,0},{5,1},{6,2},{7,3},{8,4},{9,5},{1... | collective-permute-start | bytes 786440 | tf_op jit(solution)/shard_map/ppermute | solution.py:264
  13.5 1.9 %collective-permute-start.8 = (bf16[4,2,16,1024]{3,2,1,0:T(8,128)(2,1)S(1)}, bf16[4,2,16,1024]{3,2,1,0:T(8,128)(2,1)S(1)}, u32[]{:S(2)}, u32[]{:S(2)}) collective-permute-start(bf16[4,2,16,1024]{3,2,1,0:T(8,128)(2,1)S(1)} %get-tuple-element.88), channel_id=1, source_target_pairs={{0,2},{1,3},{2,0},{3,1},{4,6},{5,7},{6,4},{7,5},{8,10},{9,11},{10,... | collective-permute-start | bytes 786440 | tf_op jit(solution)/shard_map/ppermute | solution.py:264
  15.4 1.3 %fusion.5 = (f32[4,4,4,1024]{3,2,1,0:T(4,128)S(1)}, f32[4,4,4,1024]{3,2,1,0:T(4,128)S(1)}) fusion(f32[4,4,64,1024]{3,2,1,0:T(8,128)} %field_hbm), kind=kLoop, calls=%fused_computation.18 | loop fusion | bytes 1048576 | tf_op jit(solution)/shard_map/slice | solution.py:309
  17.4 2.4 %collective-permute-done.6.rest_0_ = bf16[4,2,16,1024]{3,2,1,0:T(8,128)(2,1)S(1)} collective-permute-done((bf16[4,2,16,1024]{3,2,1,0:T(8,128)(2,1)S(1)}, bf16[4,2,16,1024]{3,2,1,0:T(8,128)(2,1)S(1)}, u32[]{:S(2)}, u32[]{:S(2)}) %collective-permute-start.6) | collective-permute-done | bytes 262176 | tf_op jit(solution)/shard_map/ppermute | solution.py:264
  19.8 2.4 %collective-permute-done.8.rest_2_ = bf16[4,2,16,1024]{3,2,1,0:T(8,128)(2,1)S(1)} collective-permute-done((bf16[4,2,16,1024]{3,2,1,0:T(8,128)(2,1)S(1)}, bf16[4,2,16,1024]{3,2,1,0:T(8,128)(2,1)S(1)}, u32[]{:S(2)}, u32[]{:S(2)}) %collective-permute-start.8) | collective-permute-done | bytes 262176 | tf_op jit(solution)/shard_map/ppermute | solution.py:264
  23.2 2.5 %collective-permute-start.10 = (bf16[4,2,16,1024]{3,2,1,0:T(8,128)(2,1)S(1)}, bf16[4,2,16,1024]{3,2,1,0:T(8,128)(2,1)S(1)}, u32[]{:S(2)}, u32[]{:S(2)}) collective-permute-start(bf16[4,2,16,1024]{3,2,1,0:T(8,128)(2,1)S(1)} %get-tuple-element.97), channel_id=1, source_target_pairs={{0,12},{1,13},{2,14},{3,15},{4,0},{5,1},{6,2},{7,3},{8,4},{9,5},{1... | collective-permute-start | bytes 786440 | tf_op jit(solution)/shard_map/ppermute | solution.py:264
  25.7 1.8 %collective-permute-start.11 = (bf16[4,2,16,1024]{3,2,1,0:T(8,128)(2,1)S(1)}, bf16[4,2,16,1024]{3,2,1,0:T(8,128)(2,1)S(1)}, u32[]{:S(2)}, u32[]{:S(2)}) collective-permute-start(bf16[4,2,16,1024]{3,2,1,0:T(8,128)(2,1)S(1)} %get-tuple-element.98), channel_id=1, source_target_pairs={{0,2},{1,3},{2,0},{3,1},{4,6},{5,7},{6,4},{7,5},{8,10},{9,11},{10,... | collective-permute-start | bytes 786440 | tf_op jit(solution)/shard_map/ppermute | solution.py:264
  27.6 1.9 %collective-permute-start.4 = (f32[4,4,4,1024]{3,2,1,0:T(4,128)S(1)}, f32[4,4,4,1024]{3,2,1,0:T(4,128)S(1)}, u32[]{:S(2)}, u32[]{:S(2)}) collective-permute-start(f32[4,4,4,1024]{3,2,1,0:T(4,128)S(1)} %get-tuple-element.84), channel_id=1, source_target_pairs={{0,16},{16,32},{32,48},{48,64},{64,80},{80,96},{96,112},{1,17},{17... | collective-permute-start | bytes 786440 | tf_op jit(solution)/shard_map/ppermute | solution.py:597
  29.5 3.4 %collective-permute-start.5 = (f32[4,4,4,1024]{3,2,1,0:T(4,128)S(1)}, f32[4,4,4,1024]{3,2,1,0:T(4,128)S(1)}, u32[]{:S(2)}, u32[]{:S(2)}) collective-permute-start(f32[4,4,4,1024]{3,2,1,0:T(4,128)S(1)} %get-tuple-element.85), channel_id=1, source_target_pairs={{16,0},{32,16},{48,32},{64,48},{80,64},{96,80},{112,96},{17,1},{33... | collective-permute-start | bytes 786440 | tf_op jit(solution)/shard_map/ppermute | solution.py:597
  32.9 1.5 %shard_map.67 = (bf16[8,4,2,16,1024]{4,3,2,1,0:T(8,128)(2,1)}, bf16[4,2,16,1024]{3,2,1,0:T(8,128)(2,1)S(1)}, bf16[4,2,16,1024]{3,2,1,0:T(8,128)(2,1)S(1)}, bf16[4,2,16,1024]{3,2,1,0:T(8,128)(2,1)S(1)}) custom-call(s32[2]{0:T(128)S(1)} %copy-done.4, s32[960]{0:T(1024)S(1)} %copy-done.3, ...), custom_call_target="tpu_custom_call", output_to_operand_aliasing={{0}: (5, {})} | custom-call | bytes 2097152 | tf_op jit(solution)/shard_map/pallas_call | solution.py:243
  34.4 0.8 shard_map.68
  35.3 2.7 %collective-permute-start.13 = (bf16[4,2,16,1024]{3,2,1,0:T(8,128)(2,1)S(1)}, bf16[4,2,16,1024]{3,2,1,0:T(8,128)(2,1)S(1)}, u32[]{:S(2)}, u32[]{:S(2)}) collective-permute-start(bf16[4,2,16,1024]{3,2,1,0:T(8,128)(2,1)S(1)} %get-tuple-element.111), channel_id=1, source_target_pairs={{0,12},{1,13},{2,14},{3,15},{4,0},{5,1},{6,2},{7,3},{8,4},{9,5},{1... | collective-permute-start | bytes 786440 | tf_op jit(solution)/shard_map/ppermute | solution.py:264
  38.5 1.6 %shard_map.69 = (bf16[8,4,2,16,1024]{4,3,2,1,0:T(8,128)(2,1)}, bf16[4,2,16,1024]{3,2,1,0:T(8,128)(2,1)S(1)}, bf16[4,2,16,1024]{3,2,1,0:T(8,128)(2,1)S(1)}, bf16[4,2,16,1024]{3,2,1,0:T(8,128)(2,1)S(1)}) custom-call(s32[2]{0:T(128)S(1)} %copy-done.4, s32[960]{0:T(1024)S(1)} %copy-done.3, ...), custom_call_target="tpu_custom_call", output_to_operand_aliasing={{0}: (5, {})} | custom-call | bytes 2097152 | tf_op jit(solution)/shard_map/pallas_call | solution.py:243
  40.1 1.9 %collective-permute-done.12.rest_0_ = bf16[4,2,16,1024]{3,2,1,0:T(8,128)(2,1)S(1)} collective-permute-done((bf16[4,2,16,1024]{3,2,1,0:T(8,128)(2,1)S(1)}, bf16[4,2,16,1024]{3,2,1,0:T(8,128)(2,1)S(1)}, u32[]{:S(2)}, u32[]{:S(2)}) %collective-permute-start.12) | collective-permute-done | bytes 262176 | tf_op jit(solution)/shard_map/ppermute | solution.py:264
  42.0 2.7 %collective-permute-done.14.rest_2_ = bf16[4,2,16,1024]{3,2,1,0:T(8,128)(2,1)S(1)} collective-permute-done((bf16[4,2,16,1024]{3,2,1,0:T(8,128)(2,1)S(1)}, bf16[4,2,16,1024]{3,2,1,0:T(8,128)(2,1)S(1)}, u32[]{:S(2)}, u32[]{:S(2)}) %collective-permute-start.14) | collective-permute-done | bytes 262176 | tf_op jit(solution)/shard_map/ppermute | solution.py:264
  45.6 1.4 %collective-permute-start.15 = (bf16[4,2,16,1024]{3,2,1,0:T(8,128)(2,1)S(1)}, bf16[4,2,16,1024]{3,2,1,0:T(8,128)(2,1)S(1)}, u32[]{:S(2)}, u32[]{:S(2)}) collective-permute-start(bf16[4,2,16,1024]{3,2,1,0:T(8,128)(2,1)S(1)} %get-tuple-element.121), channel_id=1, source_target_pairs={{0,4},{1,5},{2,6},{3,7},{4,8},{5,9},{6,10},{7,11},{8,12},{9,13},{1... | collective-permute-start | bytes 786440 | tf_op jit(solution)/shard_map/ppermute | solution.py:264
  47.0 1.2 %collective-permute-start.19 = (bf16[4,2,16,1024]{3,2,1,0:T(8,128)(2,1)S(1)}, bf16[4,2,16,1024]{3,2,1,0:T(8,128)(2,1)S(1)}, u32[]{:S(2)}, u32[]{:S(2)}) collective-permute-start(bf16[4,2,16,1024]{3,2,1,0:T(8,128)(2,1)S(1)} %get-tuple-element.125), channel_id=1, source_target_pairs={{0,2},{1,3},{2,0},{3,1},{4,6},{5,7},{6,4},{7,5},{8,10},{9,11},{10,... | collective-permute-start | bytes 786440 | tf_op jit(solution)/shard_map/ppermute | solution.py:264
  48.2 1.8 %shard_map.71.held_ref.rest_3_ = bf16[8,4,2,16,1024]{4,3,2,1,0:T(8,128)(2,1)} custom-call(s32[2]{0:T(128)S(1)} %copy-done.4, s32[960]{0:T(1024)S(1)} %copy-done.3, bf16[4,2,16,1024]{3,2,1,0:T(8,128)(2,1)S(1)} %collective-permute-done.12.rest_0_, bf16[4,2,16,1024]{3,2,1,0:T(8,128)(2,1)S(1)} %collective-permute-done.13.rest_1_, ...), custom_call_target="tpu_custom_call", output_to_operand_aliasing={{}: (5, {})} | custom-call | bytes 2097152 | tf_op jit(solution)/shard_map/pallas_call | solution.py:243
  50.0 1.2 %shard_map.72 = bf16[4,16,1024]{2,1,0:T(8,128)(2,1)S(1)} custom-call(bf16[8,4,2,16,1024]{4,3,2,1,0:T(8,128)(2,1)} %shard_map.71.held_ref.rest_3_), custom_call_target="tpu_custom_call" | custom-call | bytes 2097152 | tf_op jit(solution)/shard_map/pallas_call | solution.py:243
  51.2 9.6 %collective-permute-start.17 = (bf16[4,16,1024]{2,1,0:T(8,128)(2,1)S(1)}, bf16[4,16,1024]{2,1,0:T(8,128)(2,1)S(1)}, u32[]{:S(2)}, u32[]{:S(2)}) collective-permute-start(bf16[4,16,1024]{2,1,0:T(8,128)(2,1)S(1)} %shard_map.72), channel_id=1, source_target_pairs={{1,16},{3,18},{5,20},{7,22},{9,24},{11,26},{13,28},{15,30},{16,1},... | collective-permute-start | bytes 393224 | tf_op jit(solution)/shard_map/ppermute | solution.py:281
  60.9 1.9 %collective-permute-start.16 = (bf16[4,16,1024]{2,1,0:T(8,128)(2,1)S(1)}, bf16[4,16,1024]{2,1,0:T(8,128)(2,1)S(1)}, u32[]{:S(2)}, u32[]{:S(2)}) collective-permute-start(bf16[4,16,1024]{2,1,0:T(8,128)(2,1)S(1)} %shard_map.72), channel_id=1, source_target_pairs={{1,17},{3,19},{5,21},{7,23},{9,25},{11,27},{13,29},{15,31},{16,0},... | collective-permute-start | bytes 393224 | tf_op jit(solution)/shard_map/ppermute | solution.py:281
  63.5 3.1 %collective-permute-done.16.rest_0_ = bf16[4,16,1024]{2,1,0:T(8,128)(2,1)S(1)} collective-permute-done((bf16[4,16,1024]{2,1,0:T(8,128)(2,1)S(1)}, bf16[4,16,1024]{2,1,0:T(8,128)(2,1)S(1)}, u32[]{:S(2)}, u32[]{:S(2)}) %collective-permute-start.16) | collective-permute-done | bytes 131104 | tf_op jit(solution)/shard_map/ppermute | solution.py:281
  66.6 1.5 %shard_map.73.mine_ref = bf16[8,4,2,16,1024]{4,3,2,1,0:T(8,128)(2,1)} custom-call(s32[2]{0:T(128)S(1)} %copy-done.4, s32[960]{0:T(1024)S(1)} %copy-done.3, bf16[4,2,16,1024]{3,2,1,0:T(8,128)(2,1)S(1)} %collective-permute-done.15.rest_0_, bf16[4,2,16,1024]{3,2,1,0:T(8,128)(2,1)S(1)} %collective-permute-done.18.rest_1_, ...), custom_call_target="tpu_custom_call", output_to_operand_aliasing={{}: (5, {})} | custom-call | bytes 2097152 | tf_op jit(solution)/shard_map/pallas_call | solution.py:243
  68.1 3.1 %collective-permute-start.20 = (bf16[8,4,2,16,1024]{4,3,2,1,0:T(8,128)(2,1)}, bf16[8,4,2,16,1024]{4,3,2,1,0:T(8,128)(2,1)S(1)}, u32[]{:S(2)}, u32[]{:S(2)}) collective-permute-start(bf16[8,4,2,16,1024]{4,3,2,1,0:T(8,128)(2,1)} %shard_map.73.mine_ref), channel_id=1, source_target_pairs={{0,1},{1,0},{2,3},{3,2},{4,5},{5,4},{6,7},{7,6},{8,9},{9,8},{10,11... | collective-permute-start | bytes 6291464 | tf_op jit(solution)/shard_map/ppermute | solution.py:269
  71.3 2.2 %copy-done = f32[4,4,64,1024]{3,2,1,0:T(8,128)S(1)} copy-done((f32[4,4,64,1024]{3,2,1,0:T(8,128)S(1)}, f32[4,4,64,1024]{3,2,1,0:T(8,128)}, u32[]{:S(2)}) %copy-start) | copy-done | bytes 4194328
  74.3 1.0 %collective-permute-done.20.other_ref = bf16[8,4,2,16,1024]{4,3,2,1,0:T(8,128)(2,1)S(1)} collective-permute-done((bf16[8,4,2,16,1024]{4,3,2,1,0:T(8,128)(2,1)}, bf16[8,4,2,16,1024]{4,3,2,1,0:T(8,128)(2,1)S(1)}, u32[]{:S(2)}, u32[]{:S(2)}) %collective-permute-start.20) | collective-permute-done | bytes 2097184 | tf_op jit(solution)/shard_map/ppermute | solution.py:269
  75.2 17.1 %shard_map.75 = f32[4,4,64,1024]{3,2,1,0:T(8,128)} custom-call(s32[3,4]{1,0:T(4,128)S(1)} %pad_add_fusion.cells_ref, f32[4]{0:T(128)S(1)} %copy-done.1, f32[4,4,8,96,128]{4,3,2,1,0:T(8,128)S(1)} %shard_map.74.first, bf16[8,4,2,16,1024]{4,3,2,1,0:T(8,128)(2,1)} %shard_map.73.mine_ref, bf16[8,4,2,16,1024]{4,3,2,1,0:T(8,128)(2,1)S(1)} %collective-permute-done.20.other_ref, ...), custom_call_target="tpu_custom_call" | custom-call | flops 125829120 | bytes 12582912 | tf_op jit(solution)/shard_map/pallas_call | solution.py:574
  (34 shorter events, 6.2 us)
Async XLA Ops:
  0.0 7.5 %copy-start.3 = (s32[960]{0:T(1024)S(1)}, s32[960]{0:T(1024)}, u32[]{:S(2)}) copy-start(s32[960]{0:T(1024)} %constant.69.table_ref) | copy-start | bytes 11524
  0.0 3.8 %copy-start.4 = (s32[2]{0:T(128)S(1)}, s32[2]{0:T(128)}, u32[]{:S(2)}) copy-start(s32[2]{0:T(128)} %ids_ref.17) | copy-start | bytes 28
  0.0 7.5 %copy-start.2 = (bf16[2,4,4,64,1024]{4,3,2,1,0:T(8,128)(2,1)S(1)}, bf16[2,4,4,64,1024]{4,3,2,1,0:T(8,128)(2,1)}, u32[]{:S(2)}) copy-start(bf16[2,4,4,64,1024]{4,3,2,1,0:T(8,128)(2,1)} %store_ref.1) | copy-start | bytes 12582916
  3.0 4.5 %collective-permute-start.3 = (bf16[8,4,2,16,1024]{4,3,2,1,0:T(8,128)(2,1)S(1)}, bf16[8,4,2,16,1024]{4,3,2,1,0:T(8,128)(2,1)S(1)}, u32[]{:S(2)}, u32[]{:S(2)}) collective-permute-start(bf16[8,4,2,16,1024]{4,3,2,1,0:T(8,128)(2,1)S(1)} %shard_map.64), channel_id=1, source_target_pairs={{0,1},{1,0},{2,3},{3,2},{4,5},{5,4},{6,7},{7,6},{8,9},{9,8},{10,11... | collective-permute-start | bytes 6291464 | tf_op jit(solution)/shard_map/ppermute | solution.py:269
  8.7 11.0 %collective-permute-start.6 = (bf16[4,2,16,1024]{3,2,1,0:T(8,128)(2,1)S(1)}, bf16[4,2,16,1024]{3,2,1,0:T(8,128)(2,1)S(1)}, u32[]{:S(2)}, u32[]{:S(2)}) collective-permute-start(bf16[4,2,16,1024]{3,2,1,0:T(8,128)(2,1)S(1)} %get-tuple-element.86), channel_id=1, source_target_pairs={{0,4},{1,5},{2,6},{3,7},{4,8},{5,9},{6,10},{7,11},{8,12},{9,13},{1... | collective-permute-start | bytes 786440 | tf_op jit(solution)/shard_map/ppermute | solution.py:264
  10.4 9.3 %collective-permute-start.7 = (bf16[4,2,16,1024]{3,2,1,0:T(8,128)(2,1)S(1)}, bf16[4,2,16,1024]{3,2,1,0:T(8,128)(2,1)S(1)}, u32[]{:S(2)}, u32[]{:S(2)}) collective-permute-start(bf16[4,2,16,1024]{3,2,1,0:T(8,128)(2,1)S(1)} %get-tuple-element.87), channel_id=1, source_target_pairs={{0,12},{1,13},{2,14},{3,15},{4,0},{5,1},{6,2},{7,3},{8,4},{9,5},{1... | collective-permute-start | bytes 786440 | tf_op jit(solution)/shard_map/ppermute | solution.py:264
  13.5 8.7 %collective-permute-start.8 = (bf16[4,2,16,1024]{3,2,1,0:T(8,128)(2,1)S(1)}, bf16[4,2,16,1024]{3,2,1,0:T(8,128)(2,1)S(1)}, u32[]{:S(2)}, u32[]{:S(2)}) collective-permute-start(bf16[4,2,16,1024]{3,2,1,0:T(8,128)(2,1)S(1)} %get-tuple-element.88), channel_id=1, source_target_pairs={{0,2},{1,3},{2,0},{3,1},{4,6},{5,7},{6,4},{7,5},{8,10},{9,11},{10,... | collective-permute-start | bytes 786440 | tf_op jit(solution)/shard_map/ppermute | solution.py:264
  23.0 11.3 %collective-permute-start.9 = (bf16[4,2,16,1024]{3,2,1,0:T(8,128)(2,1)S(1)}, bf16[4,2,16,1024]{3,2,1,0:T(8,128)(2,1)S(1)}, u32[]{:S(2)}, u32[]{:S(2)}) collective-permute-start(bf16[4,2,16,1024]{3,2,1,0:T(8,128)(2,1)S(1)} %get-tuple-element.96), channel_id=1, source_target_pairs={{0,4},{1,5},{2,6},{3,7},{4,8},{5,9},{6,10},{7,11},{8,12},{9,13},{1... | collective-permute-start | bytes 786440 | tf_op jit(solution)/shard_map/ppermute | solution.py:264
  23.2 11.1 %collective-permute-start.10 = (bf16[4,2,16,1024]{3,2,1,0:T(8,128)(2,1)S(1)}, bf16[4,2,16,1024]{3,2,1,0:T(8,128)(2,1)S(1)}, u32[]{:S(2)}, u32[]{:S(2)}) collective-permute-start(bf16[4,2,16,1024]{3,2,1,0:T(8,128)(2,1)S(1)} %get-tuple-element.97), channel_id=1, source_target_pairs={{0,12},{1,13},{2,14},{3,15},{4,0},{5,1},{6,2},{7,3},{8,4},{9,5},{1... | collective-permute-start | bytes 786440 | tf_op jit(solution)/shard_map/ppermute | solution.py:264
  25.7 8.6 %collective-permute-start.11 = (bf16[4,2,16,1024]{3,2,1,0:T(8,128)(2,1)S(1)}, bf16[4,2,16,1024]{3,2,1,0:T(8,128)(2,1)S(1)}, u32[]{:S(2)}, u32[]{:S(2)}) collective-permute-start(bf16[4,2,16,1024]{3,2,1,0:T(8,128)(2,1)S(1)} %get-tuple-element.98), channel_id=1, source_target_pairs={{0,2},{1,3},{2,0},{3,1},{4,6},{5,7},{6,4},{7,5},{8,10},{9,11},{10,... | collective-permute-start | bytes 786440 | tf_op jit(solution)/shard_map/ppermute | solution.py:264
  27.6 12.5 %collective-permute-start.4 = (f32[4,4,4,1024]{3,2,1,0:T(4,128)S(1)}, f32[4,4,4,1024]{3,2,1,0:T(4,128)S(1)}, u32[]{:S(2)}, u32[]{:S(2)}) collective-permute-start(f32[4,4,4,1024]{3,2,1,0:T(4,128)S(1)} %get-tuple-element.84), channel_id=1, source_target_pairs={{0,16},{16,32},{32,48},{48,64},{64,80},{80,96},{96,112},{1,17},{17... | collective-permute-start | bytes 786440 | tf_op jit(solution)/shard_map/ppermute | solution.py:597
  29.5 10.6 %collective-permute-start.5 = (f32[4,4,4,1024]{3,2,1,0:T(4,128)S(1)}, f32[4,4,4,1024]{3,2,1,0:T(4,128)S(1)}, u32[]{:S(2)}, u32[]{:S(2)}) collective-permute-start(f32[4,4,4,1024]{3,2,1,0:T(4,128)S(1)} %get-tuple-element.85), channel_id=1, source_target_pairs={{16,0},{32,16},{48,32},{64,48},{80,64},{96,80},{112,96},{17,1},{33... | collective-permute-start | bytes 786440 | tf_op jit(solution)/shard_map/ppermute | solution.py:597
  35.2 6.8 %collective-permute-start.12 = (bf16[4,2,16,1024]{3,2,1,0:T(8,128)(2,1)S(1)}, bf16[4,2,16,1024]{3,2,1,0:T(8,128)(2,1)S(1)}, u32[]{:S(2)}, u32[]{:S(2)}) collective-permute-start(bf16[4,2,16,1024]{3,2,1,0:T(8,128)(2,1)S(1)} %get-tuple-element.107), channel_id=1, source_target_pairs={{0,4},{1,5},{2,6},{3,7},{4,8},{5,9},{6,10},{7,11},{8,12},{9,13},{1... | collective-permute-start | bytes 786440 | tf_op jit(solution)/shard_map/ppermute | solution.py:264
  35.3 6.7 %collective-permute-start.13 = (bf16[4,2,16,1024]{3,2,1,0:T(8,128)(2,1)S(1)}, bf16[4,2,16,1024]{3,2,1,0:T(8,128)(2,1)S(1)}, u32[]{:S(2)}, u32[]{:S(2)}) collective-permute-start(bf16[4,2,16,1024]{3,2,1,0:T(8,128)(2,1)S(1)} %get-tuple-element.111), channel_id=1, source_target_pairs={{0,12},{1,13},{2,14},{3,15},{4,0},{5,1},{6,2},{7,3},{8,4},{9,5},{1... | collective-permute-start | bytes 786440 | tf_op jit(solution)/shard_map/ppermute | solution.py:264
  37.9 6.7 %collective-permute-start.14 = (bf16[4,2,16,1024]{3,2,1,0:T(8,128)(2,1)S(1)}, bf16[4,2,16,1024]{3,2,1,0:T(8,128)(2,1)S(1)}, u32[]{:S(2)}, u32[]{:S(2)}) collective-permute-start(bf16[4,2,16,1024]{3,2,1,0:T(8,128)(2,1)S(1)} %get-tuple-element.112), channel_id=1, source_target_pairs={{0,2},{1,3},{2,0},{3,1},{4,6},{5,7},{6,4},{7,5},{8,10},{9,11},{10,... | collective-permute-start | bytes 786440 | tf_op jit(solution)/shard_map/ppermute | solution.py:264
  45.5 21.1 %collective-permute-start.18 = (bf16[4,2,16,1024]{3,2,1,0:T(8,128)(2,1)S(1)}, bf16[4,2,16,1024]{3,2,1,0:T(8,128)(2,1)S(1)}, u32[]{:S(2)}, u32[]{:S(2)}) collective-permute-start(bf16[4,2,16,1024]{3,2,1,0:T(8,128)(2,1)S(1)} %get-tuple-element.123), channel_id=1, source_target_pairs={{0,12},{1,13},{2,14},{3,15},{4,0},{5,1},{6,2},{7,3},{8,4},{9,5},{1... | collective-permute-start | bytes 786440 | tf_op jit(solution)/shard_map/ppermute | solution.py:264
  45.6 21.0 %collective-permute-start.15 = (bf16[4,2,16,1024]{3,2,1,0:T(8,128)(2,1)S(1)}, bf16[4,2,16,1024]{3,2,1,0:T(8,128)(2,1)S(1)}, u32[]{:S(2)}, u32[]{:S(2)}) collective-permute-start(bf16[4,2,16,1024]{3,2,1,0:T(8,128)(2,1)S(1)} %get-tuple-element.121), channel_id=1, source_target_pairs={{0,4},{1,5},{2,6},{3,7},{4,8},{5,9},{6,10},{7,11},{8,12},{9,13},{1... | collective-permute-start | bytes 786440 | tf_op jit(solution)/shard_map/ppermute | solution.py:264
  47.0 19.6 %collective-permute-start.19 = (bf16[4,2,16,1024]{3,2,1,0:T(8,128)(2,1)S(1)}, bf16[4,2,16,1024]{3,2,1,0:T(8,128)(2,1)S(1)}, u32[]{:S(2)}, u32[]{:S(2)}) collective-permute-start(bf16[4,2,16,1024]{3,2,1,0:T(8,128)(2,1)S(1)} %get-tuple-element.125), channel_id=1, source_target_pairs={{0,2},{1,3},{2,0},{3,1},{4,6},{5,7},{6,4},{7,5},{8,10},{9,11},{10,... | collective-permute-start | bytes 786440 | tf_op jit(solution)/shard_map/ppermute | solution.py:264
  51.2 20.0 %copy-start.5 = (s32[4]{0:T(128)S(1)}, s32[4]{0:T(128)}, u32[]{:S(2)}) copy-start(s32[4]{0:T(128)} %param.10) | copy-start | bytes 52
  51.2 12.3 %collective-permute-start.17 = (bf16[4,16,1024]{2,1,0:T(8,128)(2,1)S(1)}, bf16[4,16,1024]{2,1,0:T(8,128)(2,1)S(1)}, u32[]{:S(2)}, u32[]{:S(2)}) collective-permute-start(bf16[4,16,1024]{2,1,0:T(8,128)(2,1)S(1)} %shard_map.72), channel_id=1, source_target_pairs={{1,16},{3,18},{5,20},{7,22},{9,24},{11,26},{13,28},{15,30},{16,1},... | collective-permute-start | bytes 393224 | tf_op jit(solution)/shard_map/ppermute | solution.py:281
  60.9 5.7 %collective-permute-start.16 = (bf16[4,16,1024]{2,1,0:T(8,128)(2,1)S(1)}, bf16[4,16,1024]{2,1,0:T(8,128)(2,1)S(1)}, u32[]{:S(2)}, u32[]{:S(2)}) collective-permute-start(bf16[4,16,1024]{2,1,0:T(8,128)(2,1)S(1)} %shard_map.72), channel_id=1, source_target_pairs={{1,17},{3,19},{5,21},{7,23},{9,25},{11,27},{13,29},{15,31},{16,0},... | collective-permute-start | bytes 393224 | tf_op jit(solution)/shard_map/ppermute | solution.py:281
  68.1 7.1 %collective-permute-start.20 = (bf16[8,4,2,16,1024]{4,3,2,1,0:T(8,128)(2,1)}, bf16[8,4,2,16,1024]{4,3,2,1,0:T(8,128)(2,1)S(1)}, u32[]{:S(2)}, u32[]{:S(2)}) collective-permute-start(bf16[8,4,2,16,1024]{4,3,2,1,0:T(8,128)(2,1)} %shard_map.73.mine_ref), channel_id=1, source_target_pairs={{0,1},{1,0},{2,3},{3,2},{4,5},{5,4},{6,7},{7,6},{8,9},{9,8},{10,11... | collective-permute-start | bytes 6291464 | tf_op jit(solution)/shard_map/ppermute | solution.py:269
  71.3 2.2 %copy-start = (f32[4,4,64,1024]{3,2,1,0:T(8,128)S(1)}, f32[4,4,64,1024]{3,2,1,0:T(8,128)}, u32[]{:S(2)}) copy-start(f32[4,4,64,1024]{3,2,1,0:T(8,128)} %field_hbm) | copy-start | bytes 12582916
  73.5 1.8 %copy-start.1 = (f32[4]{0:T(128)S(1)}, f32[4]{0:T(128)}, u32[]{:S(2)}) copy-start(f32[4]{0:T(128)} %amount_ref.1) | copy-start | bytes 52
